TPU v7x, 256 devices: a whole 4x4x8 slice. The times are simulated.
256 devices in a mesh: clip: 64 (over x_hi, y, z), frame: 4 (over x_lo, core).
Axes of the slice: x: 4 (x_hi: 2, x_lo: 2; x = x_hi * 2 + x_lo), y: 4, z: 8, core: 2. Of those that a mesh axis runs over, the one named last changes fastest.
Arguments:
- frames: bfloat16 [2048, 16, 1152], P('clip', 'frame'), may hold values from -6 to 6
- conv_weight: bfloat16 [3, 1152, 1152], replicated, may hold values from -0.109375 to 0.109375
- captions: bfloat16 [2048, 1152], P(('clip', 'frame')), may hold values from -6 to 6
- positive: int32 [2048], P('clip'), may hold values from 0 to 2047, as said below
Outputs:
- loss: float32 [], replicated
- grad_weight: float32 [3, 1152, 1152], P(None, 'clip', 'frame')
- grad_captions: float32 [2048, 1152], P(('clip', 'frame'))
Inputs may be any that keep to these rules, and one draw needn't show every extreme that they name: Each caption id is the positive of exactly one clip.
All inputs are finite; a program needn't handle non-finite values.
Results may differ from a plain program's by a relative error of at most 0.0028.
The roundings to bfloat16 on the way count: a program that leaves them out, or rounds other values in their place, can miss the bound.
Values may be sent and summed in bfloat16 or wider, within the bound.
No kernel may reach another device: no remote copies, remote signals or barrier semaphores. Data moves between devices by JAX's collectives and lax.ppermute only.
A program may use at most 128 MiB of HBM per device.

v0:
```python
import jax
import jax.numpy as jnp
from jax import lax
from jax.sharding import PartitionSpec as P

FRAMES = 16


def with_halo(block, sides, width):
    for axis, dim in sides:
        count = lax.axis_size(axis)
        forward = [(i, i + 1) for i in range(count - 1)]
        backward = [(target, source) for source, target in forward]
        low = lax.ppermute(
            lax.slice_in_dim(block, block.shape[dim] - width, None, axis=dim), axis, forward
        )
        high = lax.ppermute(lax.slice_in_dim(block, 0, width, axis=dim), axis, backward)
        block = jnp.concatenate([low, block, high], axis=dim)
    return block


def on_device(frames, conv_weight, captions, positive):
    clip_dev, fr_dev, width = frames.shape
    rows = clip_dev * fr_dev
    padded = with_halo(frames, (("frame", 1),), 1)
    shifted = [padded[:, k : k + fr_dev].reshape(rows, width) for k in range(3)]
    conv = jnp.dot(shifted[0], conv_weight[0], preferred_element_type=jnp.float32)
    conv = conv + jnp.dot(shifted[1], conv_weight[1], preferred_element_type=jnp.float32)
    conv = conv + jnp.dot(shifted[2], conv_weight[2], preferred_element_type=jnp.float32)
    hidden = frames.reshape(rows, width).astype(jnp.float32) + jax.nn.gelu(conv)
    partial_pool = jnp.sum(hidden.reshape(clip_dev, fr_dev, width), axis=1)
    pooled = lax.psum(partial_pool, "frame") / FRAMES
    pnorm = jnp.sqrt(jnp.sum(pooled * pooled, axis=1, keepdims=True) + 1e-06)
    unit = pooled / pnorm
    u_low = unit.astype(jnp.bfloat16)
    capf = captions.astype(jnp.float32)
    cnorm = jnp.sqrt(jnp.sum(capf * capf, axis=1, keepdims=True) + 1e-06)
    vunit = capf / cnorm
    v_low = vunit.astype(jnp.bfloat16)
    cap_dev = captions.shape[0]
    frame_pos = lax.axis_index("frame")
    piece = lax.all_gather(v_low, "clip", axis=0, tiled=True)
    count = piece.shape[0]
    place = jnp.arange(count, dtype=jnp.int32)
    ids = place // cap_dev * clip_dev + frame_pos * cap_dev + place % cap_dev
    logits = (
        10.0
        * lax.dot_general(
            u_low, piece, (((1,), (1,)), ((), ())), preferred_element_type=jnp.float32
        )
        - 10.0
    )
    match = (positive[:, None] == ids[None, :]).astype(jnp.float32)
    sign = 2.0 * match - 1.0
    total = jnp.sum(jax.nn.softplus(-sign * logits))
    coef = (10.0 * (jax.nn.sigmoid(logits) - match)).astype(jnp.bfloat16)
    du_acc = jnp.dot(coef, piece, preferred_element_type=jnp.float32)
    dv_piece = lax.dot_general(
        coef, u_low, (((0,), (0,)), ((), ())), preferred_element_type=jnp.float32
    )
    total, du_part, dv_all = (total, du_acc, dv_piece)
    dv_mine = lax.psum_scatter(dv_all, "clip", scatter_dimension=0, tiled=True)
    grad_captions = (dv_mine - vunit * jnp.sum(vunit * dv_mine, axis=1, keepdims=True)) / cnorm
    loss = lax.psum(total, ("clip", "frame")) / (clip_dev * lax.axis_size("clip"))
    du_full = lax.psum(du_part, "frame")
    dpooled = (du_full - unit * jnp.sum(unit * du_full, axis=1, keepdims=True)) / pnorm
    dhidden = jnp.broadcast_to((dpooled / FRAMES)[:, None, :], (clip_dev, fr_dev, width)).reshape(
        rows, width
    )
    _, pull = jax.vjp(jax.nn.gelu, conv)
    dconv = pull(dhidden)[0].astype(jnp.bfloat16).reshape(clip_dev, fr_dev, width)
    dconv_cols = lax.all_to_all(dconv, "frame", split_axis=2, concat_axis=1, tiled=True)
    block = fr_dev + 2
    col_width = dconv_cols.shape[2]
    every_block = lax.all_gather(padded, "frame", axis=1, tiled=True)
    groups = every_block.shape[1] // block
    blocks = every_block.reshape(clip_dev, groups, block, width)
    grads = dconv_cols.reshape(clip_dev, groups, fr_dev, col_width)
    parts = [
        jnp.einsum(
            "cgtd,cgte->de", blocks[:, :, k : k + fr_dev], grads, preferred_element_type=jnp.float32
        )
        for k in range(3)
    ]
    terms = jnp.stack(parts)
    grad_weight = lax.psum_scatter(terms, "clip", scatter_dimension=1, tiled=True)
    return (loss, grad_weight, grad_captions)


def solution(mesh):
    placed = (P("clip", "frame", None), P(), P(("clip", "frame"), None), P("clip"))
    return jax.shard_map(
        on_device,
        mesh=mesh,
        in_specs=placed,
        out_specs=(P(), P(None, "clip", "frame"), P(("clip", "frame"), None)),
        check_vma=False,
    )
```

profile of v0, /device:TPU:8, one launch (start us, length us, event | category | flops | bytes accessed | tf_op | source)
XLA Modules:
  0.0 966.6 jit_solution(17515562955962899216)
XLA Ops:
  8.0 0.0 all-reduce.7.cloned.1.call-start
  8.0 1.0 copy.13
  9.1 1.7 collective-permute-start
  10.8 1.3 collective-permute-start.1
  12.1 1.0 reshape.69
  13.2 0.8 fusion.33
  14.0 2.4 fusion.2
  16.4 0.0 collective-permute-done
  16.4 0.1 copy.14
  16.5 0.0 collective-permute-done.1
  16.6 0.1 copy.16
  16.7 0.7 pad_maximum_fusion.3
  17.3 0.1 reshape.71
  17.4 3.1 fusion
  20.6 0.1 reshape.70
  20.7 2.6 multiply_add_fusion
  23.2 0.0 copy-start.3
  23.2 0.0 copy-start.4
  23.3 0.2 reshape.72
  23.4 1.0 reduce_sum.54
  24.4 0.0 all-reduce.7.cloned.1.call-update
  24.5 0.0 all-gather.3.cloned.1.call-start
  24.5 0.7 fusion.47
  25.2 0.0 all-gather.3.cloned.1.call-update
  25.2 0.0 all-reduce.9.cloned.1.call-start
  25.3 45.5 %all-reduce.7.cloned.1.call-done = f32[32,1152]{1,0:T(8,128)} async-done(((f32[32,1152]{1,0:T(8,128)}), f32[32,1152]{1,0:T(8,128)}) %all-reduce.7.cloned.1.call-update) | async-done | bytes 147472 | tf_op jit(solution)/shard_map/psum | solution.py:32
  70.8 1.0 multiply_reduce_fusion.1
  71.8 77.9 %all-gather.3.cloned.1.call-done = bf16[512,1152]{1,0:T(8,128)(2,1)} async-done(((bf16[8,1152]{1,0:T(8,128)(2,1)}), bf16[512,1152]{1,0:T(8,128)(2,1)}) %all-gather.3.cloned.1.call-update) | async-done | bytes 1179664 | tf_op jit(solution)/shard_map/all_gather | solution.py:42
  149.7 2.5 fusion.32
  152.2 2.3 fusion.49
  154.5 0.0 all-reduce.9.cloned.1.call-update
  154.5 0.0 all-gather.5.cloned.1.call-start
  154.6 0.8 pad_maximum_fusion.1
  155.4 0.0 all-gather.5.cloned.1.call-update
  155.4 36.2 %all-reduce.9.cloned.1.call-done = f32[32,1152]{1,0:T(8,128)} async-done(((f32[32,1152]{1,0:T(8,128)}), f32[32,1152]{1,0:T(8,128)}) %all-reduce.9.cloned.1.call-update) | async-done | bytes 147472 | tf_op jit(solution)/shard_map/psum | solution.py:65
  191.7 1.1 multiply_reduce_fusion
  192.8 1.0 divide_multiply_fusion
  193.8 0.1 broadcast_in_dim.2
  193.9 0.2 reshape.74
  194.1 0.4 fusion.22
  194.5 0.1 reshape.75
  194.6 0.9 copy.18
  195.5 1.8 reshape.81
  197.3 3.5 all-to-all-start
  200.7 0.0 all-reduce.11.cloned.1.call-start
  200.8 2.0 fusion.34
  202.7 4.3 all-to-all-done
  207.1 0.6 reshape.82
  207.6 0.7 copy.20
  208.4 15.0 %all-gather.5.cloned.1.call-done = bf16[32,24,1152]{2,0,1:T(8,128)(2,1)} async-done(((bf16[32,6,1152]{2,0,1:T(8,128)(2,1)}), bf16[32,24,1152]{2,0,1:T(8,128)(2,1)}) %all-gather.5.cloned.1.call-update) | async-done | bytes 1769488 | tf_op jit(solution)/shard_map/all_gather | solution.py:75
  223.4 2.0 convolution_bitcast_fusion
  225.4 0.6 convolution_bitcast_fusion.1
  226.0 0.6 convolution_bitcast_fusion.2
  226.6 2.3 pad_maximum_fusion
  228.9 8.6 copy.21
  237.4 0.0 all-reduce.11.cloned.1.call-update
  237.5 0.6 copy-done.5
  238.1 0.6 dynamic-slice
  240.0 77.2 %psum.22 = f32[]{:T(128)} all-reduce(f32[]{:T(128)} %get-tuple-element.20), channel_id=1, replica_groups=mesh['clip'=64,'frame'=4] {'clip','frame'}, use_global_device_ids=true, to_apply=%region_5.6 | all-reduce | flops 1 | bytes 8 | tf_op jit(solution)/shard_map/psum | solution.py:64
  317.8 636.5 %all-reduce.11.cloned.1.call-done = (f32[3,1152,288]{2,0,1:T(4,128)}, f32[512,1152]{1,0:T(8,128)}) async-done(((f32[3,1152,288]{2,0,1:T(4,128)}, f32[512,1152]{1,0:T(8,128)}), (f32[3,1152,288]{2,0,1:T(4,128)}, f32[512,1152]{1,0:T(8,128)})) %all-reduce.11.cloned.1.call-update) | async-done | bytes 6340624
  954.3 0.9 constant_dynamic-slice_fusion
  955.2 0.7 copy.22
  955.9 1.0 multiply_reduce_fusion.2
  956.8 1.5 subtract_divide_fusion
  (13 shorter events, 0.1 us)
Async XLA Ops:
  8.0 62.8 %all-reduce.7.cloned.1.call-start = ((), (), s32[]{:S(2)}) async-start(), calls=%async_computation.1 | async-start | bytes 294912 | tf_op jit(solution)/shard_map/psum | solution.py:32
  9.1 7.4 collective-permute-start
  10.8 5.7 collective-permute-start.1
  14.0 2.7 copy-start.1
  23.2 1.3 copy-start.3
  23.2 126.5 %copy-start.4 = (s32[32]{0:T(128)S(1)}, s32[32]{0:T(128)}, u32[]{:S(2)}) copy-start(s32[32]{0:T(128)} %param.7) | copy-start | bytes 388
  24.5 125.2 %all-gather.3.cloned.1.call-start = ((), (), s32[]{:S(2)}) async-start(), calls=%async_computation.2 | async-start | bytes 1198080 | tf_op jit(solution)/shard_map/all_gather | solution.py:42
  25.2 166.4 %all-reduce.9.cloned.1.call-start = ((), (), s32[]{:S(2)}) async-start(), calls=%async_computation.4 | async-start | bytes 294912 | tf_op jit(solution)/shard_map/psum | solution.py:65
  152.2 39.5 %copy-start.2 = (f32[32,1152]{1,0:T(8,128)S(1)}, f32[32,1152]{1,0:T(8,128)}, u32[]{:S(2)}) copy-start(f32[32,1152]{1,0:T(8,128)} %all-reduce.7.cloned.1.call-done) | copy-start | bytes 442372
  154.5 68.9 %all-gather.5.cloned.1.call-start = ((), (), s32[]{:S(2)}) async-start(), calls=%async_computation.3 | async-start | bytes 2211840 | tf_op jit(solution)/shard_map/all_gather | solution.py:75
  197.3 9.8 %all-to-all-start = ((bf16[4,2,18432]{2,1,0:T(2,128)(2,1)}), bf16[4,2,18432]{2,1,0:T(2,128)(2,1)S(1)}, u32[]{:S(2)}, u32[]{:S(2)}) async-start(bf16[4,2,18432]{2,1,0:T(2,128)(2,1)} %reshape.81), calls=%async_computation | async-start | bytes 589824 | tf_op jit(solution)/shard_map/all_to_all | solution.py:72
  200.7 753.6 %all-reduce.11.cloned.1.call-start = ((), (), s32[]{:S(2)}) async-start(), calls=%async_computation.5 | async-start | bytes 18874368
  223.4 2.0 copy-start
  237.4 0.7 copy-start.5
Sparse Core Ops, SparseCore 0:
  24.6 46.1 all-reduce.6
  154.7 36.9 all-reduce.8
  193.5 29.8 all-gather.4
Sparse Core Ops, SparseCore 1:
  29.1 120.5 all-gather.2
  237.5 716.7 all-reduce.10
where the time goes:
time: 981 us; the launch traced here: 967 us
  waiting for transfers between devices  816 us (83%)
  blocking collectives  77.2 us (8%)
  between operations  18.5 us (2%)
  local copies, waits for them, and re-layouts  18.3 us (2%)
  matrix products  18.1 us (2%)
  other arithmetic  12.3 us (1%)
    unnamed x6, waiting for transfers between devices  637 us
    all_gather x1, waiting for transfers between devices, on_device(): piece = lax.all_gather(v_low, 'clip', axis=0, tiled=True)  77.9 us
    psum x1, blocking collectives, on_device(): lax.psum(total, ('clip', 'frame')) / (clip_dev * lax.axis_size('clip'))  77.2 us
    psum x1, waiting for transfers between devices, on_device(): pooled = lax.psum(partial_pool, 'frame') / FRAMES  45.5 us
    psum x1, waiting for transfers between devices, on_device(): du_full = lax.psum(du_part, 'frame')  36.2 us
  transfers between devices with their start and end apart: 8, of which 6 were waited for; matrix products, arithmetic and copies ran while one was open for 2% of the time, Pallas kernels for 0%

commit v1 on v0

v1 whole, which is shorter than its diff:
```python
import jax
import jax.numpy as jnp
import numpy as np
from jax import lax
from jax.sharding import PartitionSpec as P

FRAMES = 16
XH, Y, Z, XL, CORE = 2, 4, 8, 2, 2
BOTH = ("clip", "frame")


def place(index):
    clip, frame = divmod(index, XL * CORE)
    xh, rest = divmod(clip, Y * Z)
    y, z = divmod(rest, Z)
    xl, core = divmod(frame, CORE)
    return xh, y, z, xl, core


def index_of(xh, y, z, xl, core):
    return (((xh * Y + y) * Z + z) * XL + xl) * CORE + core


def swap(value, flip_xh, flip_xl, flip_core):
    pairs = []
    for source in range(XH * Y * Z * XL * CORE):
        xh, y, z, xl, core = place(source)
        pairs.append((source, index_of(xh ^ flip_xh, y, z, xl ^ flip_xl, core ^ flip_core)))
    return lax.ppermute(value, BOTH, pairs)


Z_GROUPS = [[(xh * Y + y) * Z + z for z in range(Z)] for xh in range(XH) for y in range(Y)]
Y_GROUPS = [[(xh * Y + y) * Z + z for y in range(Y)] for xh in range(XH) for z in range(Z)]


def exchange(value, groups):
    return lax.all_to_all(value, "clip", 0, 0, axis_index_groups=groups, tiled=True)


def in_order(parts, pos):
    low, high = pos % 2 == 1, pos // 2 == 1
    parts = [jnp.where(low, parts[j ^ 1], parts[j]) for j in range(4)]
    return [jnp.where(high, parts[j ^ 2], parts[j]) for j in range(4)]


def on_device(frames, conv_weight, captions, positive):
    clip_dev, fr_dev, width = frames.shape
    cap_dev = captions.shape[0]
    clip_pos = lax.axis_index("clip")
    pos = lax.axis_index("frame")
    half, core = clip_pos // (Y * Z), pos % CORE
    cols = width // (XL * CORE)
    group = clip_dev * XH

    capf = captions.astype(jnp.float32)
    cnorm = jnp.sqrt(jnp.sum(capf * capf, axis=1, keepdims=True) + 1e-06)
    vunit = capf / cnorm
    v_low = vunit.astype(jnp.bfloat16)
    piece = exchange(jnp.broadcast_to(v_low, (Z, cap_dev, width)), Z_GROUPS)
    piece = piece.reshape(1, Z * cap_dev, width)
    piece = exchange(jnp.broadcast_to(piece, (Y, Z * cap_dev, width)), Y_GROUPS)
    piece = piece.reshape(Y * Z * cap_dev, width)
    count = piece.shape[0]
    row = jnp.arange(count, dtype=jnp.int32)
    ids = ((half * Y * Z + row // cap_dev) * (XL * CORE) + pos) * cap_dev + row % cap_dev

    mine = jnp.transpose(frames, (1, 0, 2))
    far = [mine, swap(mine, 0, 1, 0), swap(mine, 1, 0, 0), swap(mine, 1, 1, 0)]
    near = [swap(part, 0, 0, 1) for part in far]
    own = in_order([far[0], near[0], far[1], near[1]], pos)
    other = in_order([far[2], near[2], far[3], near[3]], pos)
    zero = jnp.zeros((1, group, width), frames.dtype)
    both = jnp.concatenate(
        [jnp.concatenate(own, axis=0), jnp.concatenate(other, axis=0)], axis=1
    )
    padded = jnp.concatenate([zero, both, zero], axis=0).reshape((FRAMES + 2) * group, width)
    wanted = jnp.concatenate([positive, swap(positive, 1, 0, 0)])

    rows = FRAMES * group
    shifted = [padded[k * group : k * group + rows] for k in range(3)]
    conv = jnp.dot(shifted[0], conv_weight[0], preferred_element_type=jnp.float32)
    conv = conv + jnp.dot(shifted[1], conv_weight[1], preferred_element_type=jnp.float32)
    conv = conv + jnp.dot(shifted[2], conv_weight[2], preferred_element_type=jnp.float32)
    hidden = shifted[1].astype(jnp.float32) + jax.nn.gelu(conv)
    pooled = jnp.sum(hidden.reshape(FRAMES, group, width), axis=0) / FRAMES
    pnorm = jnp.sqrt(jnp.sum(pooled * pooled, axis=1, keepdims=True) + 1e-06)
    unit = pooled / pnorm
    u_low = unit.astype(jnp.bfloat16)

    dots = lax.dot_general(u_low, piece, (((1,), (1,)), ((), ())), preferred_element_type=jnp.float32)
    logits = 10.0 * dots - 10.0
    match = (wanted[:, None] == ids[None, :]).astype(jnp.float32)
    sign = 2.0 * match - 1.0
    total = jnp.sum(jax.nn.softplus(-sign * logits))
    coef = (10.0 * (jax.nn.sigmoid(logits) - match)).astype(jnp.bfloat16)
    du_part = jnp.dot(coef, piece, preferred_element_type=jnp.float32)
    dv_part = lax.dot_general(
        coef, u_low, (((0,), (0,)), ((), ())), preferred_element_type=jnp.float32
    )

    dv = jnp.sum(exchange(dv_part.reshape(Y, Z * cap_dev, width), Y_GROUPS), axis=0)
    dv = jnp.sum(exchange(dv.reshape(Z, cap_dev, width), Z_GROUPS), axis=0)
    grad_captions = (dv - vunit * jnp.sum(vunit * dv, axis=1, keepdims=True)) / cnorm

    along = jnp.sum(unit * du_part, axis=1, keepdims=True)
    tail = jnp.concatenate([along, jnp.broadcast_to(total, (group, 1))], axis=1)
    chunks = [du_part[:, i * cols : (i + 1) * cols] for i in range(4)]
    keep = jnp.concatenate(
        [jnp.where(core == 0, chunks[0], chunks[1]), jnp.where(core == 0, chunks[2], chunks[3]), tail], axis=1
    )
    send = jnp.concatenate(
        [jnp.where(core == 0, chunks[1], chunks[0]), jnp.where(core == 0, chunks[3], chunks[2]), tail], axis=1
    )
    chip = keep + swap(send, 0, 0, 1)
    tail = chip[:, 2 * cols :]
    low, high = chip[:, :cols], chip[:, cols : 2 * cols]
    same = jnp.concatenate([jnp.where(pos // CORE == 0, low, high), tail], axis=1)
    cross = jnp.concatenate([jnp.where(pos // CORE == 0, high, low), tail], axis=1)
    full = same + swap(jnp.roll(same, clip_dev, axis=0), 1, 0, 0)
    full = full + swap(cross, 0, 1, 0) + swap(jnp.roll(cross, clip_dev, axis=0), 1, 1, 0)
    du, along, total = full[:, :cols], full[:, cols : cols + 1], full[0, cols + 1]

    unit_own = lax.dynamic_slice_in_dim(unit, pos * cols, cols, axis=1)
    conv_own = lax.dynamic_slice_in_dim(conv, pos * cols, cols, axis=1)
    dpooled = (du - unit_own * along) / pnorm
    dhidden = jnp.broadcast_to((dpooled / FRAMES)[None], (FRAMES, group, cols)).reshape(rows, cols)
    _, pull = jax.vjp(jax.nn.gelu, conv_own)
    dconv = pull(dhidden)[0].astype(jnp.bfloat16)
    part_rows = width // XH
    left = lax.dynamic_slice_in_dim(padded, half * part_rows, part_rows, axis=1)
    terms = [
        lax.dot_general(
            left[k * group : k * group + rows], dconv, (((0,), (0,)), ((), ())), preferred_element_type=jnp.float32
        )
        for k in range(3)
    ]
    first = lax.reduce_precision(total, 8, 7)
    second = lax.reduce_precision(total - first, 8, 7)
    third = lax.reduce_precision(total - first - second, 8, 7)
    spare = -(-3 * cols // 128) * 128 - 3 * cols
    if spare < 3:
        spare += 128
    extra = jnp.concatenate([jnp.stack([first, second, third]), jnp.zeros((spare - 3,), jnp.float32)])
    terms = jnp.concatenate(terms + [jnp.broadcast_to(extra, (part_rows, spare))], axis=1)
    out = exchange(terms.astype(jnp.bfloat16).reshape(Y, part_rows // Y, 3 * cols + spare), Y_GROUPS)
    out = jnp.sum(out.astype(jnp.float32), axis=0)
    out = exchange(out.reshape(Z, part_rows // (Y * Z), 3 * cols + spare), Z_GROUPS)
    out = jnp.sum(out, axis=0)
    loss = jnp.sum(out[0, 3 * cols : 3 * cols + 3]) / (clip_dev * lax.axis_size("clip"))
    grad_weight = jnp.stack([out[:, k * cols : (k + 1) * cols] for k in range(3)])
    return (loss, grad_weight, grad_captions)


def solution(mesh):
    placed = (P("clip", "frame", None), P(), P(("clip", "frame"), None), P("clip"))
    return jax.shard_map(
        on_device,
        mesh=mesh,
        in_specs=placed,
        out_specs=(P(), P(None, "clip", "frame"), P(("clip", "frame"), None)),
        check_vma=False,
    )
```

time: 981 us -> 156 us (0.16); the launches traced: 967 us -> 155 us
  waiting for transfers between devices: 816 us -> 51.8 us
  blocking collectives: 77.2 us -> 0 us
  starting transfers between devices: 6.69 us -> 42.6 us
  between operations: 18.5 us -> 6.85 us
  local copies, waits for them, and re-layouts: 18.3 us -> 7.2 us
  other arithmetic: 12.3 us -> 23.2 us
    unnamed x6 -> x0, waiting for transfers between devices: 637 us -> none
    all_gather x2 -> x0, waiting for transfers between devices: 92.9 us -> none  [the longest x1 77.9 us: on_device(): piece = lax.all_gather(v_low, 'clip', axis=0, tiled=True)]
    psum x2 -> x0, waiting for transfers between devices: 81.7 us -> none  [the longest x1 45.5 us: on_device(): pooled = lax.psum(partial_pool, 'frame') / FRAMES]
    psum x1 -> x0, blocking collectives: 77.2 us -> none  [on_device(): lax.psum(total, ('clip', 'frame')) / (clip_dev * lax.axis_size('clip'))]
    all_to_all x1 -> x6, waiting for transfers between devices: 4.33 us -> 43.6 us  [exchange(): lax.all_to_all(value, 'clip', 0, 0, axis_index_groups=groups, tiled=True)]
    all_to_all x1 -> x6, starting transfers between devices: 3.45 us -> 29.9 us  [exchange(): lax.all_to_all(value, 'clip', 0, 0, axis_index_groups=groups, tiled=True)]
  transfers between devices with their start and end apart: 8 -> 18, of which waited for: 6 -> 8; matrix products, arithmetic and copies ran while one was open for 2% -> 31% of each run, Pallas kernels for 0% -> 0%
where the time goes in v1:
time: 156 us; the launch traced here: 155 us
  waiting for transfers between devices  51.8 us (33%)
  starting transfers between devices  42.6 us (27%)
  matrix products  23.5 us (15%)
  other arithmetic  23.2 us (15%)
  local copies, waits for them, and re-layouts  7.2 us (5%)
  between operations  6.85 us (4%)
    all_to_all x6, waiting for transfers between devices, exchange(): lax.all_to_all(value, 'clip', 0, 0, axis_index_groups=groups, tiled=True)  43.6 us
    all_to_all x6, starting transfers between devices, exchange(): lax.all_to_all(value, 'clip', 0, 0, axis_index_groups=groups, tiled=True)  29.9 us
    ppermute x12, starting transfers between devices, swap(): return lax.ppermute(value, BOTH, pairs)  12.6 us
    ppermute x12, waiting for transfers between devices, swap(): return lax.ppermute(value, BOTH, pairs)  8.26 us
    dot_general x3, matrix products, on_device(): lax.dot_general(left[k * group:k * group + rows], dconv, (((0,), (0,)), (...  7.23 us
    dot_general x1, matrix products, on_device(): jnp.dot(shifted[2], conv_weight[2], preferred_element_type=jnp.float32)  6.43 us
    concatenate x1, other arithmetic, on_device(): jnp.concatenate([jnp.concatenate(own, axis=0), jnp.concatenate(other, axi...  4.14 us
    dot_general x1, matrix products, on_device(): jnp.dot(shifted[0], conv_weight[0], preferred_element_type=jnp.float32)  3.51 us
  transfers between devices with their start and end apart: 18, of which 8 were waited for; matrix products, arithmetic and copies ran while one was open for 31% of the time, Pallas kernels for 0%

profile of v1, /device:TPU:8, one launch (start us, length us, event | category | flops | bytes accessed | tf_op | source)
XLA Modules:
  0.0 155.1 jit_solution(11212383634396658935)
XLA Ops:
  0.6 1.1 copy.31
  1.7 1.6 %collective-permute-start = (bf16[4,32,1152]{2,1,0:T(8,128)(2,1)S(1)}, bf16[4,32,1152]{2,1,0:T(8,128)(2,1)S(1)}, u32[]{:S(2)}, u32[]{:S(2)}) collective-permute-start(bf16[4,32,1152]{2,1,0:T(8,128)(2,1)S(1)} %bitcast.81), channel_id=1, source_target_pairs={{0,2},{1,3},{2,0},{3,1},{4,6},{5,7},{6,4},{7,5},{8,10},{9,11},{10,... | collective-permute-start | bytes 884744 | tf_op jit(solution)/shard_map/ppermute | solution.py:29
  3.3 2.1 %collective-permute-start.3 = (bf16[4,32,1152]{2,1,0:T(8,128)(2,1)S(1)}, bf16[4,32,1152]{2,1,0:T(8,128)(2,1)S(1)}, u32[]{:S(2)}, u32[]{:S(2)}) collective-permute-start(bf16[4,32,1152]{2,1,0:T(8,128)(2,1)S(1)} %bitcast.83), channel_id=1, source_target_pairs={{0,130},{1,131},{2,128},{3,129},{4,134},{5,135},{6,132},{7,133},{8... | collective-permute-start | bytes 884744 | tf_op jit(solution)/shard_map/ppermute | solution.py:29
  5.4 0.6 collective-permute-start.5
  6.0 0.8 fusion.64
  6.9 4.8 %collective-permute-done = bf16[4,32,1152]{2,1,0:T(8,128)(2,1)S(1)} collective-permute-done((bf16[4,32,1152]{2,1,0:T(8,128)(2,1)S(1)}, bf16[4,32,1152]{2,1,0:T(8,128)(2,1)S(1)}, u32[]{:S(2)}, u32[]{:S(2)}) %collective-permute-start) | collective-permute-done | bytes 294944 | tf_op jit(solution)/shard_map/ppermute | solution.py:29
  11.7 0.8 fusion.73
  12.5 0.7 broadcast_in_dim.34
  13.1 8.5 %all-to-all-start = ((bf16[8,8,1152]{2,1,0:T(8,128)(2,1)}), bf16[8,8,1152]{2,1,0:T(8,128)(2,1)S(1)}, u32[]{:S(2)}, u32[]{:S(2)}) async-start(bf16[8,8,1152]{2,1,0:T(8,128)(2,1)} %broadcast_in_dim.34), calls=%async_computation | async-start | bytes 294912 | tf_op jit(solution)/shard_map/all_to_all | solution.py:37
  21.6 3.0 %collective-permute-start.7 = (s32[32]{0:T(128)}, s32[32]{0:T(128)S(1)}, u32[]{:S(2)}, u32[]{:S(2)}) collective-permute-start(s32[32]{0:T(128)} %param.7), channel_id=1, source_target_pairs={{0,128},{1,129},{2,130},{3,131},{4,132},{5,133},{6,134},{7,135},{8... | collective-permute-start | bytes 392 | tf_op jit(solution)/shard_map/ppermute | solution.py:29
  24.6 2.1 %collective-permute-done.7 = s32[32]{0:T(128)S(1)} collective-permute-done((s32[32]{0:T(128)}, s32[32]{0:T(128)S(1)}, u32[]{:S(2)}, u32[]{:S(2)}) %collective-permute-start.7) | collective-permute-done | bytes 160 | tf_op jit(solution)/shard_map/ppermute | solution.py:29
  26.8 0.7 pad_add_fusion
  27.5 4.2 %all-to-all-done = bf16[8,8,1152]{2,1,0:T(8,128)(2,1)S(1)} async-done(((bf16[8,8,1152]{2,1,0:T(8,128)(2,1)}), bf16[8,8,1152]{2,1,0:T(8,128)(2,1)S(1)}, u32[]{:S(2)}, u32[]{:S(2)}) %all-to-all-start) | async-done | bytes 147488 | tf_op jit(solution)/shard_map/all_to_all | solution.py:37
  31.7 0.9 broadcast_in_dim.36
  32.6 4.9 %all-to-all-start.1 = ((bf16[4,64,1152]{2,1,0:T(8,128)(2,1)}), bf16[4,64,1152]{2,1,0:T(8,128)(2,1)S(1)}, u32[]{:S(2)}, u32[]{:S(2)}) async-start(bf16[4,64,1152]{2,1,0:T(8,128)(2,1)} %broadcast_in_dim.36), calls=%async_computation.1 | async-start | bytes 1179648 | tf_op jit(solution)/shard_map/all_to_all | solution.py:37
  37.5 0.5 collective-permute-start.6
  38.0 0.2 broadcast_select_fusion.15
  38.2 0.9 collective-permute-done.4
  39.1 0.4 collective-permute-done.6
  39.5 1.1 broadcast_select_fusion.11
  40.6 4.1 %maximum_maximum_fusion = bf16[16,64,1152]{2,1,0:T(8,128)(2,1)S(1)} fusion(bf16[4,32,1152]{2,1,0:T(8,128)(2,1)S(1)} %get-tuple-element.12, bf16[4,32,1152]{2,1,0:T(8,128)(2,1)S(1)} %get-tuple-element.11, bf16[4,32,1152]{2,1,0:T(8,128)(2,1)S(1)} %get-tuple-element.10, bf16[4,32,1152]{2,1,0:T(8,128)(2,1)S(1)} %get-tuple-element.9, ...), kind=kLoop, calls=%fused_computation.23 | loop fusion | flops 18874368 | bytes 4718592 | tf_op jit(solution)/shard_map/concatenate | solution.py:73
  44.8 0.3 pad_slice_fusion
  45.2 3.5 %fusion.11 = f32[1024,1152]{1,0:T(8,128)S(1)} fusion(bf16[1024,1152]{1,0:T(8,128)(2,1)S(1)} %bitcast.76, bf16[3,1152,1152]{2,1,0:T(8,128)(2,1)S(1)} %bitcast.87), kind=kOutput, calls=%fused_computation.14 | convolution fusion | flops 2717908992 | bytes 9732096 | tf_op jit(solution)/shard_map/dot_general | solution.py:81
  48.7 3.5 %fusion.9 = f32[1024,1152]{1,0:T(8,128)S(1)} fusion(bf16[1024,1152]{1,0:T(8,128)(2,1)S(1)} %bitcast.68, bf16[3,1152,1152]{2,1,0:T(8,128)(2,1)S(1)} %bitcast.87), kind=kOutput, calls=%fused_computation.12 | convolution fusion | flops 2717908992 | bytes 9732096 | tf_op jit(solution)/shard_map/dot_general | solution.py:82
  52.2 6.4 %fusion.7 = (f32[1024,1152]{1,0:T(8,128)}, f32[1024,1152]{1,0:T(8,128)}) fusion(bf16[16,64,1152]{2,1,0:T(8,128)(2,1)S(1)} %maximum_maximum_fusion, bf16[1024,1152]{1,0:T(8,128)(2,1)S(1)} %bitcast.75, bf16[3,1152,1152]{2,1,0:T(8,128)(2,1)S(1)} %bitcast.87, f32[1024,1152]{1,0:T(8,128)S(1)} %fusion.11, f32[1024,1152]{1,0:T(8,128)S(1)} %fusion.9), kind=kOutput, calls=%fused_computation.8 | convolution fusion | flops 2732064768 | bytes 26247168 | tf_op jit(solution)/shard_map/dot_general | solution.py:83
  58.6 2.6 %reduce_sum.99 = f32[64,1152]{1,0:T(8,128)S(1)} reduce(f32[16,64,1152]{2,1,0:T(8,128)} %bitcast.71, f32[]{:T(128)} %constant.124.clone.1), dimensions={0}, to_apply=%region_0.1 | reduce | flops 1105920 | bytes 5013508 | tf_op jit(solution)/shard_map/reduce_sum | solution.py:85
  61.2 0.1 multiply_reduce_fusion.1
  61.3 0.5 copy-done.5
  62.0 1.0 fusion.59
  62.9 0.4 multiply_reduce_fusion
  63.3 0.3 copy-done.1
  63.6 0.1 slice_select_fusion.5
  63.8 0.7 pad.28.clone
  64.6 0.2 collective-permute-start.8
  64.9 2.2 %pad_maximum_fusion = bf16[18,64,1152]{2,1,0:T(8,128)(2,1)} fusion(bf16[1,64,1152]{2,1,0:T(8,128)(2,1)S(1)} %broadcast_in_dim.16, bf16[4,32,1152]{2,1,0:T(8,128)(2,1)S(1)} %get-tuple-element.12, bf16[4,32,1152]{2,1,0:T(8,128)(2,1)S(1)} %get-tuple-element.11, bf16[4,32,1152]{2,1,0:T(8,128)(2,1)S(1)} %get-tuple-element.10, ...), kind=kLoop, calls=%fused_computation.10 | loop fusion | flops 26542080 | bytes 5160960 | tf_op jit(solution)/shard_map/concatenate | solution.py:76
  67.6 3.3 %collective-permute-start.9 = (f32[64,290]{1,0:T(8,128)S(1)}, f32[64,290]{1,0:T(8,128)S(1)}, u32[]{:S(2)}, u32[]{:S(2)}) collective-permute-start(f32[64,290]{1,0:T(8,128)S(1)} %pad_maximum_fusion.6), channel_id=1, source_target_pairs={{0,128},{1,129},{2,130},{3,131},{4,132},{5,133},{6,134},{7,135},{8... | collective-permute-start | bytes 222728 | tf_op jit(solution)/shard_map/ppermute | solution.py:29
  70.9 0.6 collective-permute-start.10
  71.5 0.6 collective-permute-start.11
  72.2 1.5 fusion.50
  73.7 4.8 %all-to-all-start.4 = ((f32[4,64,1152]{2,1,0:T(8,128)}), f32[4,64,1152]{2,1,0:T(8,128)S(1)}, u32[]{:S(2)}, u32[]{:S(2)}) async-start(f32[4,64,1152]{2,1,0:T(8,128)} %bitcast.23), calls=%async_computation.4 | async-start | bytes 2359296 | tf_op jit(solution)/shard_map/all_to_all | solution.py:37
  78.6 0.2 slice_reduce_fusion
  78.9 2.8 %fusion.22 = bf16[1024,288]{1,0:T(8,128)(2,1)S(1)} fusion(f32[1024,1152]{1,0:T(8,128)} %get-tuple-element.29, s32[]{:T(128)S(6)} %select_n.184, f32[64,288]{1,0:T(8,128)S(1)} %fusion.49), kind=kLoop, calls=%fused_computation.33 | loop fusion | flops 5898240 | bytes 1843204 | tf_op jit(solution)/shard_map/convert_element_type | solution.py:128
  81.6 2.3 %fusion.32 = bf16[576,288]{0,1:T(8,128)(2,1)S(1)} fusion(bf16[1024,288]{1,0:T(8,128)(2,1)S(1)} %fusion.22, bf16[1152,1152]{1,0:T(8,128)(2,1)} %bitcast.72, s32[]{:T(128)S(6)} %select_n.172), kind=kOutput, calls=%fused_computation.43 | convolution fusion | flops 339904512 | bytes 2232324 | tf_op jit(solution)/shard_map/dot_general | solution.py:132
  84.0 0.6 slice.138
  88.7 0.2 copy.19
  88.9 2.4 %fusion.35 = bf16[576,288]{0,1:T(8,128)(2,1)S(1)} fusion(bf16[1024,288]{1,0:T(8,128)(2,1)S(1)} %fusion.22, bf16[1152,1152]{1,0:T(8,128)(2,1)} %bitcast.73, s32[]{:T(128)S(6)} %add.154, s32[]{:T(128)S(6)} %select_n.172), kind=kOutput, calls=%fused_computation.44 | convolution fusion | flops 339904512 | bytes 2232328 | tf_op jit(solution)/shard_map/dot_general | solution.py:132
  91.4 0.2 copy.20
  91.6 2.4 %fusion.38 = bf16[576,288]{0,1:T(8,128)(2,1)S(1)} fusion(bf16[1024,288]{1,0:T(8,128)(2,1)S(1)} %fusion.22, bf16[1152,1152]{1,0:T(8,128)(2,1)} %bitcast.74, s32[]{:T(128)S(6)} %add.155, s32[]{:T(128)S(6)} %select_n.172), kind=kOutput, calls=%fused_computation.45 | convolution fusion | flops 339904512 | bytes 2232328 | tf_op jit(solution)/shard_map/dot_general | solution.py:132
  94.1 0.2 copy.21
  94.3 2.0 %maximum_convert_fusion = bf16[32]{0:T(256)(128)(2,1)S(1)} fusion(bf16[29]{0:T(256)(128)(2,1)S(1)} %broadcast.141, bf16[1]{0:T(256)(128)(2,1)} %bitcast.19, f32[1]{0:T(128)} %bitcast.18, f32[1]{0:T(128)} %bitcast.17), kind=kLoop, calls=%fused_computation.138 | loop fusion | flops 256 | bytes 132 | tf_op jit(solution)/shard_map/convert.7
  96.4 1.5 maximum_maximum_fusion.1
  97.9 4.8 %all-to-all-start.2 = ((bf16[4,144,896]{2,1,0:T(8,128)(2,1)}), bf16[4,144,896]{2,1,0:T(8,128)(2,1)S(1)}, u32[]{:S(2)}, u32[]{:S(2)}) async-start(bf16[4,144,896]{2,1,0:T(8,128)(2,1)} %maximum_maximum_fusion.1), calls=%async_computation.2 | async-start | bytes 2064384 | tf_op jit(solution)/shard_map/all_to_all | solution.py:37
  102.7 0.8 reduce_sum.107
  103.5 12.1 %all-to-all-done.2 = bf16[4,144,896]{2,1,0:T(8,128)(2,1)S(1)} async-done(((bf16[4,144,896]{2,1,0:T(8,128)(2,1)}), bf16[4,144,896]{2,1,0:T(8,128)(2,1)S(1)}, u32[]{:S(2)}, u32[]{:S(2)}) %all-to-all-start.2) | async-done | bytes 1032224 | tf_op jit(solution)/shard_map/all_to_all | solution.py:37
  115.6 3.4 %all-to-all-start.5 = ((f32[8,8,1152]{2,1,0:T(8,128)}), f32[8,8,1152]{2,1,0:T(8,128)S(1)}, u32[]{:S(2)}, u32[]{:S(2)}) async-start(f32[8,8,1152]{2,1,0:T(8,128)} %bitcast.24), calls=%async_computation.5 | async-start | bytes 589824 | tf_op jit(solution)/shard_map/all_to_all | solution.py:37
  119.0 0.1 convert_reduce_fusion
  119.2 0.9 reshape.86
  120.1 9.9 %all-to-all-done.5 = f32[8,8,1152]{2,1,0:T(8,128)S(1)} async-done(((f32[8,8,1152]{2,1,0:T(8,128)}), f32[8,8,1152]{2,1,0:T(8,128)S(1)}, u32[]{:S(2)}, u32[]{:S(2)}) %all-to-all-start.5) | async-done | bytes 294944 | tf_op jit(solution)/shard_map/all_to_all | solution.py:37
  130.0 3.5 %all-to-all-start.3 = ((f32[8,18,896]{2,1,0:T(8,128)}), f32[8,18,896]{2,1,0:T(8,128)S(1)}, u32[]{:S(2)}, u32[]{:S(2)}) async-start(f32[8,18,896]{2,1,0:T(8,128)} %reshape.86), calls=%async_computation.3 | async-start | bytes 1376256 | tf_op jit(solution)/shard_map/all_to_all | solution.py:37
  133.6 0.2 multiply_reduce_fusion.2
  133.8 0.7 subtract_divide_fusion
  134.5 17.4 %all-to-all-done.3 = f32[8,18,896]{2,1,0:T(8,128)S(1)} async-done(((f32[8,18,896]{2,1,0:T(8,128)}), f32[8,18,896]{2,1,0:T(8,128)S(1)}, u32[]{:S(2)}, u32[]{:S(2)}) %all-to-all-start.3) | async-done | bytes 516128 | tf_op jit(solution)/shard_map/all_to_all | solution.py:37
  152.0 0.7 slice_reduce_fusion.1
  153.3 0.7 pad_maximum_fusion.5
  (51 shorter events, 1.3 us)
Async XLA Ops:
  0.6 37.4 %copy-start = (bf16[32,4,1152]{2,1,0:T(4,128)(2,1)S(1)}, bf16[32,4,1152]{2,1,0:T(4,128)(2,1)}, u32[]{:S(2)}) copy-start(bf16[32,4,1152]{2,1,0:T(4,128)(2,1)} %param.4) | copy-start | bytes 884740
  1.7 10.0 %collective-permute-start = (bf16[4,32,1152]{2,1,0:T(8,128)(2,1)S(1)}, bf16[4,32,1152]{2,1,0:T(8,128)(2,1)S(1)}, u32[]{:S(2)}, u32[]{:S(2)}) collective-permute-start(bf16[4,32,1152]{2,1,0:T(8,128)(2,1)S(1)} %bitcast.81), channel_id=1, source_target_pairs={{0,2},{1,3},{2,0},{3,1},{4,6},{5,7},{6,4},{7,5},{8,10},{9,11},{10,... | collective-permute-start | bytes 884744 | tf_op jit(solution)/shard_map/ppermute | solution.py:29
  3.3 34.7 %collective-permute-start.2 = (bf16[4,32,1152]{2,1,0:T(8,128)(2,1)S(1)}, bf16[4,32,1152]{2,1,0:T(8,128)(2,1)S(1)}, u32[]{:S(2)}, u32[]{:S(2)}) collective-permute-start(bf16[4,32,1152]{2,1,0:T(8,128)(2,1)S(1)} %bitcast.82), channel_id=1, source_target_pairs={{0,1},{1,0},{2,3},{3,2},{4,5},{5,4},{6,7},{7,6},{8,9},{9,8},{10,11... | collective-permute-start | bytes 884744 | tf_op jit(solution)/shard_map/ppermute | solution.py:29
  3.3 34.2 %collective-permute-start.3 = (bf16[4,32,1152]{2,1,0:T(8,128)(2,1)S(1)}, bf16[4,32,1152]{2,1,0:T(8,128)(2,1)S(1)}, u32[]{:S(2)}, u32[]{:S(2)}) collective-permute-start(bf16[4,32,1152]{2,1,0:T(8,128)(2,1)S(1)} %bitcast.83), channel_id=1, source_target_pairs={{0,130},{1,131},{2,128},{3,129},{4,134},{5,135},{6,132},{7,133},{8... | collective-permute-start | bytes 884744 | tf_op jit(solution)/shard_map/ppermute | solution.py:29
  5.4 32.1 %collective-permute-start.5 = (bf16[4,32,1152]{2,1,0:T(8,128)(2,1)S(1)}, bf16[4,32,1152]{2,1,0:T(8,128)(2,1)S(1)}, u32[]{:S(2)}, u32[]{:S(2)}) collective-permute-start(bf16[4,32,1152]{2,1,0:T(8,128)(2,1)S(1)} %bitcast.84), channel_id=1, source_target_pairs={{0,128},{1,129},{2,130},{3,131},{4,132},{5,133},{6,134},{7,135},{8... | collective-permute-start | bytes 884744 | tf_op jit(solution)/shard_map/ppermute | solution.py:29
  11.7 26.3 %collective-permute-start.1 = (bf16[4,32,1152]{2,1,0:T(8,128)(2,1)S(1)}, bf16[4,32,1152]{2,1,0:T(8,128)(2,1)S(1)}, u32[]{:S(2)}, u32[]{:S(2)}) collective-permute-start(bf16[4,32,1152]{2,1,0:T(8,128)(2,1)S(1)} %collective-permute-done), channel_id=1, source_target_pairs={{0,1},{1,0},{2,3},{3,2},{4,5},{5,4},{6,7},{7,6},{8,9},{9,8},{10,11... | collective-permute-start | bytes 884744 | tf_op jit(solution)/shard_map/ppermute | solution.py:29
  13.1 18.6 %all-to-all-start = ((bf16[8,8,1152]{2,1,0:T(8,128)(2,1)}), bf16[8,8,1152]{2,1,0:T(8,128)(2,1)S(1)}, u32[]{:S(2)}, u32[]{:S(2)}) async-start(bf16[8,8,1152]{2,1,0:T(8,128)(2,1)} %broadcast_in_dim.34), calls=%async_computation | async-start | bytes 294912 | tf_op jit(solution)/shard_map/all_to_all | solution.py:37
  21.6 5.2 %collective-permute-start.7 = (s32[32]{0:T(128)}, s32[32]{0:T(128)S(1)}, u32[]{:S(2)}, u32[]{:S(2)}) collective-permute-start(s32[32]{0:T(128)} %param.7), channel_id=1, source_target_pairs={{0,128},{1,129},{2,130},{3,131},{4,132},{5,133},{6,134},{7,135},{8... | collective-permute-start | bytes 392 | tf_op jit(solution)/shard_map/ppermute | solution.py:29
  32.6 29.4 %all-to-all-start.1 = ((bf16[4,64,1152]{2,1,0:T(8,128)(2,1)}), bf16[4,64,1152]{2,1,0:T(8,128)(2,1)S(1)}, u32[]{:S(2)}, u32[]{:S(2)}) async-start(bf16[4,64,1152]{2,1,0:T(8,128)(2,1)} %broadcast_in_dim.36), calls=%async_computation.1 | async-start | bytes 1179648 | tf_op jit(solution)/shard_map/all_to_all | solution.py:37
  37.5 1.6 %collective-permute-start.4 = (bf16[4,32,1152]{2,1,0:T(8,128)(2,1)S(1)}, bf16[4,32,1152]{2,1,0:T(8,128)(2,1)S(1)}, u32[]{:S(2)}, u32[]{:S(2)}) collective-permute-start(bf16[4,32,1152]{2,1,0:T(8,128)(2,1)S(1)} %collective-permute-done.3), channel_id=1, source_target_pairs={{0,1},{1,0},{2,3},{3,2},{4,5},{5,4},{6,7},{7,6},{8,9},{9,8},{10,11... | collective-permute-start | bytes 884744 | tf_op jit(solution)/shard_map/ppermute | solution.py:29
  37.5 1.6 %copy-start.4 = (bf16[4,32,1152]{2,1,0:T(8,128)(2,1)}, bf16[4,32,1152]{2,1,0:T(8,128)(2,1)S(1)}, u32[]{:S(2)}) copy-start(bf16[4,32,1152]{2,1,0:T(8,128)(2,1)S(1)} %collective-permute-done.5) | copy-start | bytes 884740
  37.5 2.0 %collective-permute-start.6 = (bf16[4,32,1152]{2,1,0:T(8,128)(2,1)S(1)}, bf16[4,32,1152]{2,1,0:T(8,128)(2,1)S(1)}, u32[]{:S(2)}, u32[]{:S(2)}) collective-permute-start(bf16[4,32,1152]{2,1,0:T(8,128)(2,1)S(1)} %collective-permute-done.5), channel_id=1, source_target_pairs={{0,1},{1,0},{2,3},{3,2},{4,5},{5,4},{6,7},{7,6},{8,9},{9,8},{10,11... | collective-permute-start | bytes 884744 | tf_op jit(solution)/shard_map/ppermute | solution.py:29
  38.0 7.1 %slice-start = ((s8[7962624]{0:T(1024)(128)(4,1)}), s8[4194304]{0:T(1024)(128)(4,1)S(1)}, s32[]{:S(2)}) async-start(s8[7962624]{0:T(1024)(128)(4,1)} %bitcast.86), calls=%async_computation.6 | async-start | bytes 8388608
  40.6 4.5 %slice-start.1 = ((s8[7962624]{0:T(1024)(128)(4,1)}), s8[3768320]{0:T(1024)(128)(4,1)S(1)}, s32[]{:S(2)}) async-start(s8[7962624]{0:T(1024)(128)(4,1)} %bitcast.86), calls=%async_computation.7 | async-start | bytes 7536640
  61.3 0.5 copy-start.5
  62.9 0.6 copy-start.1
  64.6 2.5 %collective-permute-start.8 = (f32[64,578]{1,0:T(8,128)S(1)}, f32[64,578]{1,0:T(8,128)S(1)}, u32[]{:S(2)}, u32[]{:S(2)}) collective-permute-start(f32[64,578]{1,0:T(8,128)S(1)} %fusion.44), channel_id=1, source_target_pairs={{0,1},{1,0},{2,3},{3,2},{4,5},{5,4},{6,7},{7,6},{8,9},{9,8},{10,11... | collective-permute-start | bytes 443912 | tf_op jit(solution)/shard_map/ppermute | solution.py:29
  64.9 7.3 %copy-start.2 = (f32[64,256]{1,0:T(8,128)S(1)}, f32[64,256]{1,0:T(8,128)}, u32[]{:S(2)}) copy-start(f32[64,256]{1,0:T(8,128)} %copy-done.1) | copy-start | bytes 196612
  67.5 11.3 %copy-start.6 = (f32[64]{0:T(128)S(1)}, f32[64]{0:T(128)}, u32[]{:S(2)}) copy-start(f32[64]{0:T(128)} %copy-done.5) | copy-start | bytes 772
  67.6 10.9 %collective-permute-start.9 = (f32[64,290]{1,0:T(8,128)S(1)}, f32[64,290]{1,0:T(8,128)S(1)}, u32[]{:S(2)}, u32[]{:S(2)}) collective-permute-start(f32[64,290]{1,0:T(8,128)S(1)} %pad_maximum_fusion.6), channel_id=1, source_target_pairs={{0,128},{1,129},{2,130},{3,131},{4,132},{5,133},{6,134},{7,135},{8... | collective-permute-start | bytes 222728 | tf_op jit(solution)/shard_map/ppermute | solution.py:29
  70.9 7.6 %collective-permute-start.10 = (f32[64,290]{1,0:T(8,128)S(1)}, f32[64,290]{1,0:T(8,128)S(1)}, u32[]{:S(2)}, u32[]{:S(2)}) collective-permute-start(f32[64,290]{1,0:T(8,128)S(1)} %pad_maximum_fusion.3), channel_id=1, source_target_pairs={{0,2},{1,3},{2,0},{3,1},{4,6},{5,7},{6,4},{7,5},{8,10},{9,11},{10,... | collective-permute-start | bytes 222728 | tf_op jit(solution)/shard_map/ppermute | solution.py:29
  71.5 6.9 %collective-permute-start.11 = (f32[64,290]{1,0:T(8,128)S(1)}, f32[64,290]{1,0:T(8,128)S(1)}, u32[]{:S(2)}, u32[]{:S(2)}) collective-permute-start(f32[64,290]{1,0:T(8,128)S(1)} %pad_maximum_fusion.7), channel_id=1, source_target_pairs={{0,130},{1,131},{2,128},{3,129},{4,134},{5,135},{6,132},{7,133},{8... | collective-permute-start | bytes 222728 | tf_op jit(solution)/shard_map/ppermute | solution.py:29
  73.7 24.3 %all-to-all-start.4 = ((f32[4,64,1152]{2,1,0:T(8,128)}), f32[4,64,1152]{2,1,0:T(8,128)S(1)}, u32[]{:S(2)}, u32[]{:S(2)}) async-start(f32[4,64,1152]{2,1,0:T(8,128)} %bitcast.23), calls=%async_computation.4 | async-start | bytes 2359296 | tf_op jit(solution)/shard_map/all_to_all | solution.py:37
  97.9 17.7 %all-to-all-start.2 = ((bf16[4,144,896]{2,1,0:T(8,128)(2,1)}), bf16[4,144,896]{2,1,0:T(8,128)(2,1)S(1)}, u32[]{:S(2)}, u32[]{:S(2)}) async-start(bf16[4,144,896]{2,1,0:T(8,128)(2,1)} %maximum_maximum_fusion.1), calls=%async_computation.2 | async-start | bytes 2064384 | tf_op jit(solution)/shard_map/all_to_all | solution.py:37
  103.5 30.1 %copy-start.3 = (bf16[8,1152]{1,0:T(8,128)(2,1)S(1)}, bf16[8,1152]{1,0:T(8,128)(2,1)}, u32[]{:S(2)}) copy-start(bf16[8,1152]{1,0:T(8,128)(2,1)} %param.6) | copy-start | bytes 55300
  115.6 14.4 %all-to-all-start.5 = ((f32[8,8,1152]{2,1,0:T(8,128)}), f32[8,8,1152]{2,1,0:T(8,128)S(1)}, u32[]{:S(2)}, u32[]{:S(2)}) async-start(f32[8,8,1152]{2,1,0:T(8,128)} %bitcast.24), calls=%async_computation.5 | async-start | bytes 589824 | tf_op jit(solution)/shard_map/all_to_all | solution.py:37
  130.0 21.9 %all-to-all-start.3 = ((f32[8,18,896]{2,1,0:T(8,128)}), f32[8,18,896]{2,1,0:T(8,128)S(1)}, u32[]{:S(2)}, u32[]{:S(2)}) async-start(f32[8,18,896]{2,1,0:T(8,128)} %reshape.86), calls=%async_computation.3 | async-start | bytes 1376256 | tf_op jit(solution)/shard_map/all_to_all | solution.py:37

commit v2 on v0

v2 whole, which is shorter than its diff:
```python
import functools
import math

import jax
import jax.numpy as jnp
from jax import lax
from jax.experimental import pallas as pl
from jax.experimental.pallas import tpu as pltpu
from jax.sharding import PartitionSpec as P

FRAMES = 16
XH, Y, Z, XL, CORE = 2, 4, 8, 2, 2
BOTH = ("clip", "frame")
F32, BF16 = jnp.float32, jnp.bfloat16
ROOT = math.sqrt(2.0 / math.pi)
CUBE = 0.044715


def place(index):
    clip, frame = divmod(index, XL * CORE)
    xh, rest = divmod(clip, Y * Z)
    y, z = divmod(rest, Z)
    xl, core = divmod(frame, CORE)
    return xh, y, z, xl, core


def index_of(xh, y, z, xl, core):
    return (((xh * Y + y) * Z + z) * XL + xl) * CORE + core


def swap(value, flip_xh, flip_xl, flip_core):
    pairs = []
    for source in range(XH * Y * Z * XL * CORE):
        xh, y, z, xl, core = place(source)
        pairs.append((source, index_of(xh ^ flip_xh, y, z, xl ^ flip_xl, core ^ flip_core)))
    return lax.ppermute(value, BOTH, pairs)


def move(value, by_y, by_z):
    pairs = []
    for source in range(XH * Y * Z * XL * CORE):
        xh, y, z, xl, core = place(source)
        pairs.append((source, index_of(xh, (y + by_y) % Y, (z + by_z) % Z, xl, core)))
    return lax.ppermute(value, BOTH, pairs)


Z_GROUPS = [[(xh * Y + y) * Z + z for z in range(Z)] for xh in range(XH) for y in range(Y)]
YZ_GROUPS = [[xh * Y * Z + yz for yz in range(Y * Z)] for xh in range(XH)]


def exchange(value, groups):
    return lax.all_to_all(value, "clip", 0, 0, axis_index_groups=groups, tiled=True)


def roundup(value, unit):
    return -(-value // unit) * unit


def whereabouts():
    clip = lax.axis_index("clip")
    return lax.axis_index("frame"), clip // (Y * Z), clip // Z % Y, clip % Z


def call(body, mib, out_shapes, scratch, flops, moved, *operands, loose={}, far={}):
    specs = []
    operands = list(operands)
    for i, o in enumerate(operands):
        space = loose.get(i, pltpu.VMEM)
        if space is pltpu.HBM:
            operands[i] = pltpu.with_memory_space_constraint(o, space)
        specs.append(pl.BlockSpec(memory_space=space))
    return pl.pallas_call(
        body,
        out_shape=[
            far[i](s, d) if i in far else jax.ShapeDtypeStruct(s, d) for i, (s, d) in enumerate(out_shapes)
        ],
        in_specs=specs,
        out_specs=[pl.BlockSpec(memory_space=far.get(i, pltpu.VMEM)) for i in range(len(out_shapes))],
        scratch_shapes=scratch,
        cost_estimate=pl.CostEstimate(flops=flops, bytes_accessed=moved, transcendentals=0),
        compiler_params=pltpu.CompilerParams(vmem_limit_bytes=mib * 2**20),
    )(*operands)


def conv_kernel(cols, *refs):
    pieces, weights, (x_ref, out_ref, pooled_ref, slope_ref, w_ref, sum_ref, part_ref, x_sem, w_sem, o_sem) = (
        refs[:8],
        refs[8],
        refs[9:],
    )
    frame, half, _, _ = whereabouts()
    steps, block, width = pieces[0].shape
    group = pooled_ref.shape[0]
    wide = slope_ref.shape[2]
    copies = []
    for i, piece in enumerate(pieces):
        j, side = i % 4, i // 4
        first = (frame ^ j) * steps + 1
        start = pl.multiple_of((half ^ side) * block, block)
        copies.append(
            pltpu.make_async_copy(
                piece, x_ref.at[pl.ds(first, steps), pl.ds(start, block), :], x_sem.at[i]
            )
        )
    for k in range(3):
        for i in range(XL):
            start = pl.multiple_of((frame ^ (i * CORE)) * (wide - 128), 128)
            copies.append(
                pltpu.make_async_copy(
                    weights.at[k, :, pl.ds(start, wide)], w_ref.at[k, :, pl.ds(i * wide, wide)], w_sem.at[k, i]
                )
            )
    for copy in copies:
        copy.start()
    filled = copies[len(pieces) :]
    x_ref[0] = jnp.zeros((group, width), BF16)
    x_ref[FRAMES + 1] = jnp.zeros((group, width), BF16)
    sum_ref[...] = jnp.zeros_like(sum_ref)
    part_ref[...] = jnp.zeros_like(part_ref)
    for copy in copies[: len(pieces)]:
        copy.wait()

    def step(m, first):
        base = m * steps
        conv = jnp.zeros((steps * group, XL * wide), F32)
        for k in range(3):
            if first:
                for copy in filled[k * XL : (k + 1) * XL]:
                    copy.wait()
            rows = x_ref[pl.ds(base + k, steps)].reshape(steps * group, width)
            conv = conv + jnp.dot(rows, w_ref[k], preferred_element_type=F32)
        tanh = jnp.tanh(ROOT * conv * (1.0 + CUBE * (conv * conv)))
        gelu = 0.5 * conv * (1.0 + tanh)
        part_ref[...] += jnp.sum(gelu.reshape(steps, group, XL * wide), axis=0)
        conv, tanh = conv[:, :wide], tanh[:, :wide]
        slope = 0.5 * (1.0 + tanh) + 0.5 * conv * (1.0 - tanh * tanh) * (
            ROOT * (1.0 + 3.0 * CUBE * (conv * conv))
        )
        slope_ref[pl.ds(base, steps)] = slope.reshape(steps, group, wide)
        sum_ref[...] += jnp.sum(x_ref[pl.ds(base + 1, steps)].astype(F32), axis=0)

    stores = []
    for m in range(FRAMES // steps):
        step(m, m == 0)
        rows = pl.ds(m * steps, steps)
        stores.append(pltpu.make_async_copy(slope_ref.at[rows], out_ref.at[rows], o_sem.at[m]))
        stores[-1].start()
    shift = cols + 128 - wide
    for f in range(XL * CORE):

        @pl.when(frame == f)
        def _():
            for i in range(XL):
                g = f ^ (i * CORE)
                gelu = part_ref[:, i * wide + g * shift : i * wide + g * shift + cols]
                pooled_ref[:, i * cols : (i + 1) * cols] = (
                    sum_ref[:, g * cols : (g + 1) * cols] + gelu
                ) / FRAMES

    for store in stores:
        store.wait()


def pair_kernel(cap_dev, mine, peer, v_ref, positive, across, *refs):
    (keep_ref, send_ref, unit_ref, norm_ref), dv_refs, (pooled_ref, lay_ref) = refs[:4], refs[4 : 4 + Y], refs[4 + Y :]
    frame, half, y_pos, _ = whereabouts()
    part = mine.shape[1]
    cols = part // 2
    group = mine.shape[0]
    pooled_ref[:, 0:part] = mine[...]
    pooled_ref[:, part : 2 * part] = peer[...]
    pooled = pooled_ref[...]
    pnorm = jnp.sqrt(jnp.sum(pooled * pooled, axis=1, keepdims=True) + 1e-06)
    unit = pooled / pnorm
    u_low = unit.astype(BF16)
    v_low = v_ref[...]
    dots = lax.dot_general(u_low, v_low, (((1,), (1,)), ((), ())), preferred_element_type=F32)
    logits = 10.0 * dots - 10.0
    first = jnp.where(half == 0, positive[...], across[...])
    second = jnp.where(half == 0, across[...], positive[...])
    wanted = jnp.concatenate([first, second], axis=0)
    row = lax.broadcasted_iota(jnp.int32, (1, v_low.shape[0]), 1)
    ids = ((half * (Y * Z) + row // cap_dev) * (XL * CORE) + frame) * cap_dev + row % cap_dev
    match = jnp.where(wanted == ids, 1.0, 0.0).astype(F32)
    sign = 2.0 * match - 1.0
    turned = -sign * logits
    terms = jnp.maximum(turned, 0.0) + jnp.log1p(jnp.exp(-jnp.abs(turned)))
    total = jnp.sum(jnp.sum(terms, axis=1, keepdims=True), axis=0, keepdims=True)
    coef = (10.0 * (1.0 / (1.0 + jnp.exp(-logits)) - match)).astype(BF16)
    du = jnp.dot(coef, v_low, preferred_element_type=F32)
    dv = lax.dot_general(coef, u_low, (((0,), (0,)), ((), ())), preferred_element_type=F32)
    lay_ref[...] = dv.reshape(lay_ref.shape)
    for i, dv_ref in enumerate(dv_refs):
        dv_ref[...] = lay_ref[(y_pos + i) % Y]
    along = jnp.sum(unit * du, axis=1, keepdims=True)
    pooled_ref[...] = du
    spare = keep_ref.shape[1] - part
    lane = lax.broadcasted_iota(jnp.int32, (group, spare), 1)
    tail = jnp.where(lane == 0, along, jnp.where(lane == 1, total, 0.0))
    keep_ref[:, 0:part] = pooled_ref[:, 0:part]
    send_ref[:, 0:part] = pooled_ref[:, part : 2 * part]
    keep_ref[:, part:] = tail
    send_ref[:, part:] = tail
    unit_ref[...] = unit[:, 0:cols]
    norm_ref[...] = pnorm


def weight_kernel(s0, s1, s2, s3, unit, norm, slope_in, x_ref, *refs):
    outs, (d_ref, g_ref, p_ref, c_ref, slope, sem) = refs[:Y], refs[Y:]
    load = pltpu.make_async_copy(slope_in, slope, sem)
    load.start()
    frame, half, y_pos, _ = whereabouts()
    group, cols = unit.shape
    width = x_ref.shape[2]
    wide = slope.shape[2]
    shift = cols + 128 - wide
    share = outs[0].shape[0]
    full = s0[...] + s1[...] + s2[...] + s3[...]
    along, total = full[:, cols : cols + 1], full[0:1, cols + 1 : cols + 2]
    dpooled = (full[:, 0:cols] - unit[...] * along) / norm[...] / FRAMES
    p_ref[...] = jnp.zeros_like(p_ref)
    for f in range(XL * CORE):

        @pl.when(frame == f)
        def _():
            p_ref[:, f * shift : f * shift + cols] = dpooled

    dpooled = p_ref[...]
    zero = jnp.zeros((group, wide), BF16)
    for k in range(3):
        for t in range(FRAMES + 2):
            if t < k or t >= FRAMES + k:
                d_ref[t * group : (t + 1) * group, k * wide : (k + 1) * wide] = zero
    load.wait()
    for t in range(FRAMES):
        dconv = (slope[t] * dpooled).astype(BF16)
        for k in range(3):
            d_ref[(t + k) * group : (t + k + 1) * group, k * wide : (k + 1) * wide] = dconv
    tile = 128
    tiles = roundup(Y * share, tile) // tile
    offset = width - tiles * tile

    def step(m, carry):
        start = pl.multiple_of(half * offset + m * tile, tile)
        rows = x_ref[:, :, pl.ds(start, tile)].reshape((FRAMES + 2) * group, tile)
        g_ref[pl.ds(pl.multiple_of(m * tile, tile), tile), :] = lax.dot_general(
            rows, d_ref[...], (((0,), (0,)), ((), ())), preferred_element_type=F32
        )
        return carry

    lax.fori_loop(0, tiles, step, 0)
    skip = tiles * tile - Y * share
    lane = lax.broadcasted_iota(jnp.int32, (share, c_ref.shape[1] - 3 * cols), 1)
    c_ref[:, 3 * cols :] = loss_lanes(total, lane)
    for i, out_ref in enumerate(outs):
        start = pl.multiple_of(half * skip + ((y_pos + i) % Y) * share, 16)
        for f in range(XL * CORE):

            @pl.when(frame == f)
            def _():
                for k in range(3):
                    c_ref[:, k * cols : (k + 1) * cols] = g_ref[
                        pl.ds(start, share), k * wide + f * shift : k * wide + f * shift + cols
                    ]

        out_ref[...] = c_ref[...].astype(BF16)


def loss_lanes(total, lane):
    first = total.astype(BF16).astype(F32)
    second = (total - first).astype(BF16).astype(F32)
    third = total - first - second
    return jnp.where(lane == 0, first, jnp.where(lane == 1, second, jnp.where(lane == 2, third, 0.0)))


def along_y_kernel(first_lane, *refs):
    ins, caps, (out_ref, sum_ref, lay_ref) = refs[:Y], refs[Y : 2 * Y], refs[2 * Y :]
    rows, lanes = ins[0].shape[0] // Z, ins[0].shape[1]
    kept, packed = lay_ref.shape[1:]
    total = ins[0][...].astype(F32)
    for part in ins[1:]:
        total = total + part[...].astype(F32)
    sum_ref[...] = total
    loss = jnp.sum(sum_ref[0:1, first_lane : first_lane + 3], axis=1, keepdims=True)
    lane = lax.broadcasted_iota(jnp.int32, (1, lanes - first_lane), 1)
    tail = loss_lanes(loss, lane)
    lay_ref[...] = jnp.zeros_like(lay_ref)
    for z in range(Z):
        sum_ref[z * rows : z * rows + 1, first_lane:] = tail
        lay_ref[z, :, 0:lanes] = sum_ref[z * rows : z * rows + kept, :]
        for j in range(rows - kept):
            for i in range(lanes // 128):
                at = j * (lanes // 128) + i
                lay_ref[z, at : at + 1, lanes:] = sum_ref[
                    z * rows + kept + j : z * rows + kept + j + 1, i * 128 : (i + 1) * 128
                ]
    out_ref[:, :, 0:packed] = lay_ref[...].astype(BF16)
    total = caps[0][...]
    for part in caps[1:]:
        total = total + part[...]
    high = total.astype(BF16).astype(F32)
    low = total - high
    own = total.shape[0] // Z
    for z in range(Z):
        both = jnp.concatenate([high[z * own : (z + 1) * own], low[z * own : (z + 1) * own]], axis=0)
        out_ref[z, :, packed:] = both.astype(BF16)


def along_z_kernel(lanes, packed, in_ref, captions, grad_ref, loss_ref, cap_ref, sum_ref, turn_ref):
    rows, cols = grad_ref.shape[1:]
    kept = in_ref.shape[1]
    own, width = captions.shape
    total = in_ref[0].astype(F32)
    for z in range(1, Z):
        total = total + in_ref[z].astype(F32)
    sum_ref[0:kept, :] = total
    for j in range(rows - kept):
        for i in range(lanes // 128):
            at = j * (lanes // 128) + i
            sum_ref[kept + j : kept + j + 1, i * 128 : (i + 1) * 128] = sum_ref[at : at + 1, lanes:packed]
    for k in range(3):
        grad_ref[k] = sum_ref[0:rows, k * cols : (k + 1) * cols]
    loss_ref[...] = jnp.sum(sum_ref[0:1, 3 * cols : 3 * cols + 3], axis=1, keepdims=True)
    frame = whereabouts()[0]
    for f in range(len(ORDER)):

        @pl.when(frame == f)
        def _():
            for i, j in enumerate(ORDER):
                g = f ^ j
                at = packed + i * cols
                turn_ref[:, g * cols : (g + 1) * cols] = (
                    sum_ref[0:own, at : at + cols] + sum_ref[own : 2 * own, at : at + cols]
                )

    dv = turn_ref[...]
    cnorm, unit = norm_of(captions[...])
    cap_ref[...] = (dv - unit * jnp.sum(unit * dv, axis=1, keepdims=True)) / cnorm


ORDER = (0, CORE, 1, CORE ^ 1)


def norm_of(captions):
    capf = captions.astype(F32)
    cnorm = jnp.sqrt(jnp.sum(capf * capf, axis=1, keepdims=True) + 1e-06)
    return cnorm, capf / cnorm


def caption_kernel(captions, out_ref, unit_ref, turn_ref):
    frame = whereabouts()[0]
    cols = captions.shape[1] // len(ORDER)
    unit_ref[...] = norm_of(captions[...])[1]
    for f in range(len(ORDER)):

        @pl.when(frame == f)
        def _():
            for i, j in enumerate(ORDER):
                g = f ^ j
                turn_ref[:, i * cols : (i + 1) * cols] = unit_ref[:, g * cols : (g + 1) * cols]

    low = turn_ref[...].astype(BF16)
    out_ref[...] = jnp.broadcast_to(low[None], out_ref.shape)


def on_device(frames, conv_weight, captions, positive):
    clip_dev, fr_dev, width = frames.shape
    cap_dev = captions.shape[0]
    cols = width // (XL * CORE)
    group = clip_dev * XH
    rows = FRAMES * group

    mine = jnp.transpose(frames, (1, 0, 2))
    first = swap(mine, 0, 0, 1)
    far = [swap(mine, 0, 1, 0), swap(mine, 1, 0, 0), swap(mine, 1, 1, 0)]
    positive = positive[:, None]
    across = swap(positive, 1, 0, 0)
    far[1], across = lax.optimization_barrier((far[1], across))
    near = [first] + [swap(part, 0, 0, 1) for part in far]
    far = [mine] + far
    given = captions
    pieces = [far[0], near[0], far[1], near[1], far[2], near[2], far[3], near[3]]

    (spread,) = call(
        caption_kernel,
        4,
        [((Y * Z, cap_dev, width), BF16)],
        [pltpu.VMEM((cap_dev, width), F32), pltpu.VMEM((cap_dev, width), F32)],
        0,
        Y * Z * cap_dev * width * 2,
        given,
    )
    piece = exchange(spread, YZ_GROUPS).reshape(Y * Z * cap_dev, width)
    count = piece.shape[0]
    wide = cols + (XL * CORE - 1) * (cols % 128)
    x, slope, pooled = call(
        functools.partial(conv_kernel, cols),
        24,
        [((FRAMES + 2, group, width), BF16), ((FRAMES, group, wide), F32), ((group, XL * cols), F32)],
        [
            pltpu.VMEM((FRAMES, group, wide), F32),
            pltpu.VMEM((3, width, XL * wide), BF16),
            pltpu.VMEM((group, width), F32),
            pltpu.VMEM((group, XL * wide), F32),
            pltpu.SemaphoreType.DMA((8,)),
            pltpu.SemaphoreType.DMA((3, XL)),
            pltpu.SemaphoreType.DMA((FRAMES // fr_dev,)),
        ],
        int(3 * rows * 3 * width * 2 * cols),
        3 * width * 2 * wide * 2,
        *pieces,
        conv_weight,
        loose={i: pl.ANY for i in range(8)} | {8: pltpu.HBM},
        far={1: pltpu.HBM},
    )
    pooled, piece = lax.optimization_barrier((pooled, piece))
    peer = swap(pooled, 0, 0, 1)
    lanes = roundup(2 * cols + 2, 128)
    keep, send, unit, pnorm, *dv = call(
        functools.partial(pair_kernel, cap_dev),
        8,
        [((group, lanes), F32), ((group, lanes), F32), ((group, cols), F32), ((group, 1), F32)]
        + [((count // Y, width), F32)] * Y,
        [pltpu.VMEM((group, width), F32), pltpu.VMEM((Y, count // Y, width), F32)],
        6 * group * count * width,
        count * width * 6,
        pooled,
        peer,
        piece,
        positive,
        across,
    )

    chip = keep + swap(send, 0, 0, 1)
    chip, *dv = lax.optimization_barrier((chip, *dv))
    tail = chip[:, 2 * cols : 2 * cols + 2]
    spare = jnp.zeros((group, roundup(cols + 2, 128) - cols - 2), F32)
    same = jnp.concatenate([chip[:, :cols], tail, spare], axis=1)
    cross = jnp.concatenate([chip[:, cols : 2 * cols], tail, spare], axis=1)
    parts = [same, swap(same, 1, 0, 0), swap(cross, 0, 1, 0), swap(cross, 1, 1, 0)]

    share = width // XH // Y
    packed = roundup(3 * cols + 3, 128)
    terms = call(
        weight_kernel,
        16,
        [((share, packed), BF16)] * Y,
        [
            pltpu.VMEM((rows + 2 * group, 3 * wide), BF16),
            pltpu.VMEM((roundup(Y * share, 128), 3 * wide), F32),
            pltpu.VMEM((group, wide), F32),
            pltpu.VMEM((share, packed), F32),
            pltpu.VMEM((FRAMES, group, wide), F32),
            pltpu.SemaphoreType.DMA(()),
        ],
        6 * rows * Y * share * cols,
        rows * width * 2,
        *parts,
        unit,
        pnorm,
        slope,
        x,
        loose={6: pltpu.HBM},
    )
    dv = [dv[0]] + [move(dv[i], i, 0) for i in range(1, Y)]
    terms = [terms[0]] + [move(terms[i], i, 0) for i in range(1, Y)]
    own_rows = share // Z
    kept = own_rows // 16 * 16
    (terms,) = call(
        functools.partial(along_y_kernel, 3 * cols),
        8,
        [((Z, kept, packed + 128 + width), BF16)],
        [pltpu.VMEM((share, packed), F32), pltpu.VMEM((Z, kept, packed + 128), F32)],
        0,
        share * packed * 16,
        *terms,
        *dv,
    )
    terms = exchange(terms, Z_GROUPS)
    grad_weight, loss, grad_captions = call(
        functools.partial(along_z_kernel, packed, packed + 128),
        4,
        [((3, own_rows, cols), F32), ((1, 1), F32), ((cap_dev, width), F32)],
        [pltpu.VMEM((roundup(own_rows, 8), packed + 128 + width), F32), pltpu.VMEM((cap_dev, width), F32)],
        0,
        share * packed * 2,
        terms,
        captions,
    )
    loss = loss[0, 0] / (clip_dev * lax.axis_size("clip"))
    return (loss, grad_weight, grad_captions)


def solution(mesh):
    placed = (P("clip", "frame", None), P(), P(("clip", "frame"), None), P("clip"))
    return jax.shard_map(
        on_device,
        mesh=mesh,
        in_specs=placed,
        out_specs=(P(), P(None, "clip", "frame"), P(("clip", "frame"), None)),
        check_vma=False,
    )
```

time: 981 us -> 112 us (0.11); the launches traced: 967 us -> 111 us
  waiting for transfers between devices: 816 us -> 21.1 us
  blocking collectives: 77.2 us -> 24.4 us
  starting transfers between devices: 6.69 us -> 31.3 us
  Pallas kernels: 0 us -> 21.2 us
  matrix products: 18.1 us -> 0 us
  between operations: 18.5 us -> 2.53 us
  other arithmetic: 12.3 us -> 0.1 us
    unnamed x6 -> x0, waiting for transfers between devices: 637 us -> none
    all_gather x2 -> x0, waiting for transfers between devices: 92.9 us -> none  [the longest x1 77.9 us: on_device(): piece = lax.all_gather(v_low, 'clip', axis=0, tiled=True)]
    psum x2 -> x0, waiting for transfers between devices: 81.7 us -> none  [the longest x1 45.5 us: on_device(): pooled = lax.psum(partial_pool, 'frame') / FRAMES]
    psum x1 -> x0, blocking collectives: 77.2 us -> none  [on_device(): lax.psum(total, ('clip', 'frame')) / (clip_dev * lax.axis_size('clip'))]
    all_to_all x0 -> x1, blocking collectives: none -> 24.4 us  [exchange(): lax.all_to_all(value, 'clip', 0, 0, axis_index_groups=groups, tiled=True)]
    pallas_call x0 -> x6, Pallas kernels: none -> 21.2 us  [call(): pl.pallas_call(body, out_shape=[far[i](s, d) if i in far else jax.ShapeDt...]
    ppermute x2 -> x19, waiting for transfers between devices: 0.01 us -> 21.1 us  [the longest x6 12.3 us: move(): return lax.ppermute(value, BOTH, pairs)]
    dot_general x9 -> x0, matrix products: 18.1 us -> none  [the longest x3 3.19 us: on_device(): jnp.einsum('cgtd,cgte->de', blocks[:, :, k:k + fr_dev], grads, preferred_...]
  transfers between devices with their start and end apart: 8 -> 20, of which waited for: 6 -> 10; matrix products, arithmetic and copies ran while one was open for 2% -> 1% of each run, Pallas kernels for 0% -> 17%
where the time goes in v2:
time: 112 us; the launch traced here: 111 us
  starting transfers between devices  31.3 us (28%)
  blocking collectives  24.4 us (22%)
  Pallas kernels  21.2 us (19%)
  waiting for transfers between devices  21.1 us (19%)
  local copies, waits for them, and re-layouts  10.6 us (9%)
  between operations  2.53 us (2%)
    all_to_all x1, blocking collectives, exchange(): lax.all_to_all(value, 'clip', 0, 0, axis_index_groups=groups, tiled=True)  24.4 us
    pallas_call x6, Pallas kernels, call(): pl.pallas_call(body, out_shape=[far[i](s, d) if i in far else jax.ShapeDt...  21.2 us
    ppermute x13, starting transfers between devices, swap(): return lax.ppermute(value, BOTH, pairs)  12.4 us
    ppermute x6, waiting for transfers between devices, move(): return lax.ppermute(value, BOTH, pairs)  12.3 us
    all_to_all x1, starting transfers between devices, exchange(): lax.all_to_all(value, 'clip', 0, 0, axis_index_groups=groups, tiled=True)  11.7 us
    unnamed x25, local copies, waits for them, and re-layouts  9.65 us
    ppermute x13, waiting for transfers between devices, swap(): return lax.ppermute(value, BOTH, pairs)  8.81 us
    ppermute x6, starting transfers between devices, move(): return lax.ppermute(value, BOTH, pairs)  7.15 us
  transfers between devices with their start and end apart: 20, of which 10 were waited for; matrix products, arithmetic and copies ran while one was open for 1% of the time, Pallas kernels for 17%

profile of v2, /device:TPU:8, one launch (start us, length us, event | category | flops | bytes accessed | tf_op | source)
XLA Modules:
  0.0 111.3 jit_solution(2401522653273137004)
XLA Ops:
  0.6 1.0 copy.11
  1.6 3.1 %collective-permute-start.3 = (bf16[4,32,1152]{2,1,0:T(8,128)(2,1)S(1)}, bf16[4,32,1152]{2,1,0:T(8,128)(2,1)S(1)}, u32[]{:S(2)}, u32[]{:S(2)}) collective-permute-start(bf16[4,32,1152]{2,1,0:T(8,128)(2,1)S(1)} %bitcast.7), channel_id=1, source_target_pairs={{0,128},{1,129},{2,130},{3,131},{4,132},{5,133},{6,134},{7,135},{8... | collective-permute-start | bytes 884744 | tf_op jit(solution)/shard_map/ppermute | solution.py:36
  4.7 0.6 collective-permute-start.1
  5.3 0.6 collective-permute-start.6
  5.9 0.7 copy-done.2
  6.6 1.1 shard_map.68
  7.7 11.7 %all-to-all-start = ((bf16[32,8,1152]{2,1,0:T(8,128)(2,1)}), bf16[32,8,1152]{2,1,0:T(8,128)(2,1)S(1)}, u32[]{:S(2)}, u32[]{:S(2)}) async-start(bf16[32,8,1152]{2,1,0:T(8,128)(2,1)} %shard_map.68), calls=%async_computation | async-start | bytes 1179648 | tf_op jit(solution)/shard_map/all_to_all | solution.py:52
  19.4 0.7 copy.8.positive
  20.1 3.0 %collective-permute-start.4 = (s32[32,1]{1,0:T(8,128)S(1)}, s32[32,1]{1,0:T(8,128)S(1)}, u32[]{:S(2)}, u32[]{:S(2)}) collective-permute-start(s32[32,1]{1,0:T(8,128)S(1)} %copy.8.positive), channel_id=1, source_target_pairs={{0,128},{1,129},{2,130},{3,131},{4,132},{5,133},{6,134},{7,135},{8... | collective-permute-start | bytes 392 | tf_op jit(solution)/shard_map/ppermute | solution.py:36
  23.1 0.0 collective-permute-start
  23.1 2.3 %collective-permute-done.4.across = s32[32,1]{1,0:T(8,128)S(1)} collective-permute-done((s32[32,1]{1,0:T(8,128)S(1)}, s32[32,1]{1,0:T(8,128)S(1)}, u32[]{:S(2)}, u32[]{:S(2)}) %collective-permute-start.4) | collective-permute-done | bytes 160 | tf_op jit(solution)/shard_map/ppermute | solution.py:36
  25.4 0.6 copy-done.4
  26.0 0.0 collective-permute-done.3.refs_4_
  26.0 0.0 collective-permute-start.5
  26.0 0.7 copy-done.6
  26.7 0.0 collective-permute-done.1.refs_2_
  26.7 0.5 collective-permute-start.2
  27.2 0.7 copy-done.8
  27.9 0.0 collective-permute-done.6.refs_6_
  27.9 0.0 collective-permute-start.7
  27.9 0.7 copy-done.10
  28.6 0.0 collective-permute-done.refs_1_
  28.6 0.0 collective-permute-done.5.refs_5_
  28.7 0.8 collective-permute-done.7.refs_7_
  29.5 1.0 copy-done.7
  30.5 1.0 copy-done.9
  31.4 1.0 copy-done.11
  32.4 11.7 %shard_map.67 = (bf16[18,64,1152]{2,1,0:T(8,128)(2,1)S(1)}, f32[16,64,384]{2,1,0:T(8,128)}, f32[64,576]{1,0:T(8,128)S(1)}) custom-call(bf16[4,32,1152]{2,1,0:T(8,128)(2,1)S(1)} %bitcast.11, bf16[4,32,1152]{2,1,0:T(8,128)(2,1)S(1)} %collective-permute-done.refs_1_, bf16[4,32,1152]{2,1,0:T(8,128)(2,1)S(1)} %copy-done.9, ...), custom_call_target="tpu_custom_call" | custom-call | flops 6115295232 | bytes 5308416 | tf_op jit(solution)/shard_map/pallas_call | solution.py:72
  44.1 0.7 copy-done
  44.7 0.0 all-to-all-done
  44.7 0.1 collective-permute-start.8
  44.9 1.5 %collective-permute-done.8.peer = f32[64,576]{1,0:T(8,128)S(1)} collective-permute-done((f32[64,576]{1,0:T(8,128)}, f32[64,576]{1,0:T(8,128)S(1)}, u32[]{:S(2)}, u32[]{:S(2)}) %collective-permute-start.8) | collective-permute-done | bytes 147488 | tf_op jit(solution)/shard_map/ppermute | solution.py:36
  46.4 0.9 copy-done.1
  47.3 0.7 copy-done.5
  48.0 1.2 %shard_map.69 = (f32[64,640]{1,0:T(8,128)S(1)}, f32[64,640]{1,0:T(8,128)S(1)}, f32[64,288]{1,0:T(8,128)S(1)}, f32[64,1]{1,0:T(8,128)S(1)}, f32[64,1152]{1,0:T(8,...) custom-call(f32[64,576]{1,0:T(8,128)S(1)} %copy-done.1, ...), custom_call_target="tpu_custom_call" | custom-call | flops 113246208 | bytes 1769472 | tf_op jit(solution)/shard_map/pallas_call | solution.py:72
  49.2 0.2 collective-permute-start.9
  49.4 0.1 pad.3.clone
  49.5 1.2 %collective-permute-done.9 = f32[64,640]{1,0:T(8,128)S(1)} collective-permute-done((f32[64,640]{1,0:T(8,128)S(1)}, f32[64,640]{1,0:T(8,128)S(1)}, u32[]{:S(2)}, u32[]{:S(2)}) %collective-permute-start.9) | collective-permute-done | bytes 163872 | tf_op jit(solution)/shard_map/ppermute | solution.py:36
  50.7 0.1 slice.11
  50.8 1.5 %collective-permute-start.16 = (f32[64,1152]{1,0:T(8,128)S(1)}, f32[64,1152]{1,0:T(8,128)S(1)}, u32[]{:S(2)}, u32[]{:S(2)}) collective-permute-start(f32[64,1152]{1,0:T(8,128)S(1)} %get-tuple-element.51), channel_id=1, source_target_pairs={{0,32},{1,33},{2,34},{3,35},{4,36},{5,37},{6,38},{7,39},{8,40},{9,... | collective-permute-start | bytes 884744 | tf_op jit(solution)/shard_map/ppermute | solution.py:44
  52.2 0.1 maximum_maximum_fusion.s0
  52.3 3.0 %collective-permute-start.10 = (f32[64,384]{1,0:T(8,128)S(1)}, f32[64,384]{1,0:T(8,128)S(1)}, u32[]{:S(2)}, u32[]{:S(2)}) collective-permute-start(f32[64,384]{1,0:T(8,128)S(1)} %maximum_maximum_fusion.s0), channel_id=1, source_target_pairs={{0,128},{1,129},{2,130},{3,131},{4,132},{5,133},{6,134},{7,135},{8... | collective-permute-start | bytes 294920 | tf_op jit(solution)/shard_map/ppermute | solution.py:36
  55.3 0.1 slice.12
  55.4 0.7 collective-permute-start.11
  56.1 0.7 collective-permute-start.12
  56.7 0.8 collective-permute-start.17
  57.6 1.1 %collective-permute-done.10.s1 = f32[64,384]{1,0:T(8,128)S(1)} collective-permute-done((f32[64,384]{1,0:T(8,128)S(1)}, f32[64,384]{1,0:T(8,128)S(1)}, u32[]{:S(2)}, u32[]{:S(2)}) %collective-permute-start.10) | collective-permute-done | bytes 98336 | tf_op jit(solution)/shard_map/ppermute | solution.py:36
  58.7 1.3 %collective-permute-start.18 = (f32[64,1152]{1,0:T(8,128)S(1)}, f32[64,1152]{1,0:T(8,128)S(1)}, u32[]{:S(2)}, u32[]{:S(2)}) collective-permute-start(f32[64,1152]{1,0:T(8,128)S(1)} %get-tuple-element.53), channel_id=1, source_target_pairs={{0,96},{1,97},{2,98},{3,99},{4,100},{5,101},{6,102},{7,103},{8,104... | collective-permute-start | bytes 884744 | tf_op jit(solution)/shard_map/ppermute | solution.py:44
  60.0 0.6 collective-permute-done.11.s2
  60.6 1.3 %collective-permute-done.12.s3 = f32[64,384]{1,0:T(8,128)S(1)} collective-permute-done((f32[64,384]{1,0:T(8,128)S(1)}, f32[64,384]{1,0:T(8,128)S(1)}, u32[]{:S(2)}, u32[]{:S(2)}) %collective-permute-start.12) | collective-permute-done | bytes 98336 | tf_op jit(solution)/shard_map/ppermute | solution.py:36
  61.9 5.8 %shard_map.70 = (bf16[144,896]{1,0:T(8,128)(2,1)S(1)}, bf16[144,896]{1,0:T(8,128)(2,1)S(1)}, bf16[144,896]{1,0:T(8,128)(2,1)S(1)}, bf16[144,896]{1,0:T(8,128)(2,1)S(1)}) custom-call(f32[64,384]{1,0:T(8,128)S(1)} %maximum_maximum_fusion.s0, f32[64,384]{1,0:T(8,128)S(1)} %collective-permute-done.10.s1, f32[64,384]{1,0:T(8,128)S(1)} %collective-permute-done.11.s2, ...), custom_call_target="tpu_custom_call" | custom-call | flops 1019215872 | bytes 2359296 | tf_op jit(solution)/shard_map/pallas_call | solution.py:72
  67.7 0.0 copy-start.3
  67.7 1.3 %collective-permute-start.13 = (bf16[144,896]{1,0:T(8,128)(2,1)S(1)}, bf16[144,896]{1,0:T(8,128)(2,1)S(1)}, u32[]{:S(2)}, u32[]{:S(2)}) collective-permute-start(bf16[144,896]{1,0:T(8,128)(2,1)S(1)} %get-tuple-element.47), channel_id=1, source_target_pairs={{0,32},{1,33},{2,34},{3,35},{4,36},{5,37},{6,38},{7,39},{8,40},{9,... | collective-permute-start | bytes 774152 | tf_op jit(solution)/shard_map/ppermute | solution.py:44
  69.0 1.4 %collective-permute-start.14 = (bf16[144,896]{1,0:T(8,128)(2,1)S(1)}, bf16[144,896]{1,0:T(8,128)(2,1)S(1)}, u32[]{:S(2)}, u32[]{:S(2)}) collective-permute-start(bf16[144,896]{1,0:T(8,128)(2,1)S(1)} %get-tuple-element.48), channel_id=1, source_target_pairs={{0,64},{1,65},{2,66},{3,67},{4,68},{5,69},{6,70},{7,71},{8,72},{9,... | collective-permute-start | bytes 774152 | tf_op jit(solution)/shard_map/ppermute | solution.py:44
  70.4 0.0 collective-permute-done.16.refs_5_
  70.4 0.8 collective-permute-start.15
  71.2 0.0 collective-permute-done.17.refs_6_
  71.2 5.6 %collective-permute-done.18.refs_7_ = f32[64,1152]{1,0:T(8,128)S(1)} collective-permute-done((f32[64,1152]{1,0:T(8,128)S(1)}, f32[64,1152]{1,0:T(8,128)S(1)}, u32[]{:S(2)}, u32[]{:S(2)}) %collective-permute-start.18) | collective-permute-done | bytes 294944 | tf_op jit(solution)/shard_map/ppermute | solution.py:44
  76.9 0.0 collective-permute-done.13.refs_1_
  76.9 3.2 %collective-permute-done.14.refs_2_ = bf16[144,896]{1,0:T(8,128)(2,1)S(1)} collective-permute-done((bf16[144,896]{1,0:T(8,128)(2,1)S(1)}, bf16[144,896]{1,0:T(8,128)(2,1)S(1)}, u32[]{:S(2)}, u32[]{:S(2)}) %collective-permute-start.14) | collective-permute-done | bytes 258080 | tf_op jit(solution)/shard_map/ppermute | solution.py:44
  80.1 3.4 %collective-permute-done.15.refs_3_ = bf16[144,896]{1,0:T(8,128)(2,1)S(1)} collective-permute-done((bf16[144,896]{1,0:T(8,128)(2,1)S(1)}, bf16[144,896]{1,0:T(8,128)(2,1)S(1)}, u32[]{:S(2)}, u32[]{:S(2)}) %collective-permute-start.15) | collective-permute-done | bytes 258080 | tf_op jit(solution)/shard_map/ppermute | solution.py:44
  83.5 0.5 shard_map.71
  84.0 24.4 %all_to_all.10.in_ref = bf16[8,16,2176]{2,1,0:T(8,128)(2,1)S(1)} all-to-all(bf16[8,16,2176]{2,1,0:T(8,128)(2,1)S(1)} %shard_map.71), channel_id=1, replica_groups={{0,4,8,12,16,20,24,28},{32,36,40,44,48,52,56,60},{64,68,72,76,80,84,88,..., dimensions={0} | all-to-all | bytes 1114112 | tf_op jit(solution)/shard_map/all_to_all | solution.py:52
  108.4 1.0 shard_map.72
  (17 shorter events, 0.1 us)
Async XLA Ops:
  1.6 24.3 %collective-permute-start.3 = (bf16[4,32,1152]{2,1,0:T(8,128)(2,1)S(1)}, bf16[4,32,1152]{2,1,0:T(8,128)(2,1)S(1)}, u32[]{:S(2)}, u32[]{:S(2)}) collective-permute-start(bf16[4,32,1152]{2,1,0:T(8,128)(2,1)S(1)} %bitcast.7), channel_id=1, source_target_pairs={{0,128},{1,129},{2,130},{3,131},{4,132},{5,133},{6,134},{7,135},{8... | collective-permute-start | bytes 884744 | tf_op jit(solution)/shard_map/ppermute | solution.py:36
  4.7 21.9 %collective-permute-start.1 = (bf16[4,32,1152]{2,1,0:T(8,128)(2,1)S(1)}, bf16[4,32,1152]{2,1,0:T(8,128)(2,1)S(1)}, u32[]{:S(2)}, u32[]{:S(2)}) collective-permute-start(bf16[4,32,1152]{2,1,0:T(8,128)(2,1)S(1)} %bitcast.8), channel_id=1, source_target_pairs={{0,2},{1,3},{2,0},{3,1},{4,6},{5,7},{6,4},{7,5},{8,10},{9,11},{10,... | collective-permute-start | bytes 884744 | tf_op jit(solution)/shard_map/ppermute | solution.py:36
  5.3 22.6 %collective-permute-start.6 = (bf16[4,32,1152]{2,1,0:T(8,128)(2,1)S(1)}, bf16[4,32,1152]{2,1,0:T(8,128)(2,1)S(1)}, u32[]{:S(2)}, u32[]{:S(2)}) collective-permute-start(bf16[4,32,1152]{2,1,0:T(8,128)(2,1)S(1)} %bitcast.9), channel_id=1, source_target_pairs={{0,130},{1,131},{2,128},{3,129},{4,134},{5,135},{6,132},{7,133},{8... | collective-permute-start | bytes 884744 | tf_op jit(solution)/shard_map/ppermute | solution.py:36
  5.9 0.7 copy-start.2
  7.7 37.1 %all-to-all-start = ((bf16[32,8,1152]{2,1,0:T(8,128)(2,1)}), bf16[32,8,1152]{2,1,0:T(8,128)(2,1)S(1)}, u32[]{:S(2)}, u32[]{:S(2)}) async-start(bf16[32,8,1152]{2,1,0:T(8,128)(2,1)} %shard_map.68), calls=%async_computation | async-start | bytes 1179648 | tf_op jit(solution)/shard_map/all_to_all | solution.py:52
  20.1 5.2 %collective-permute-start.4 = (s32[32,1]{1,0:T(8,128)S(1)}, s32[32,1]{1,0:T(8,128)S(1)}, u32[]{:S(2)}, u32[]{:S(2)}) collective-permute-start(s32[32,1]{1,0:T(8,128)S(1)} %copy.8.positive), channel_id=1, source_target_pairs={{0,128},{1,129},{2,130},{3,131},{4,132},{5,133},{6,134},{7,135},{8... | collective-permute-start | bytes 392 | tf_op jit(solution)/shard_map/ppermute | solution.py:36
  23.1 5.6 %collective-permute-start = (bf16[4,32,1152]{2,1,0:T(8,128)(2,1)S(1)}, bf16[4,32,1152]{2,1,0:T(8,128)(2,1)S(1)}, u32[]{:S(2)}, u32[]{:S(2)}) collective-permute-start(bf16[4,32,1152]{2,1,0:T(8,128)(2,1)S(1)} %bitcast.10), channel_id=1, source_target_pairs={{0,1},{1,0},{2,3},{3,2},{4,5},{5,4},{6,7},{7,6},{8,9},{9,8},{10,11... | collective-permute-start | bytes 884744 | tf_op jit(solution)/shard_map/ppermute | solution.py:36
  25.4 0.6 copy-start.4
  26.0 2.7 %collective-permute-start.5 = (bf16[4,32,1152]{2,1,0:T(8,128)(2,1)S(1)}, bf16[4,32,1152]{2,1,0:T(8,128)(2,1)S(1)}, u32[]{:S(2)}, u32[]{:S(2)}) collective-permute-start(bf16[4,32,1152]{2,1,0:T(8,128)(2,1)S(1)} %collective-permute-done.3.refs_4_), channel_id=1, source_target_pairs={{0,1},{1,0},{2,3},{3,2},{4,5},{5,4},{6,7},{7,6},{8,9},{9,8},{10,11... | collective-permute-start | bytes 884744 | tf_op jit(solution)/shard_map/ppermute | solution.py:36
  26.0 0.7 copy-start.6
  26.7 2.0 %collective-permute-start.2 = (bf16[4,32,1152]{2,1,0:T(8,128)(2,1)S(1)}, bf16[4,32,1152]{2,1,0:T(8,128)(2,1)S(1)}, u32[]{:S(2)}, u32[]{:S(2)}) collective-permute-start(bf16[4,32,1152]{2,1,0:T(8,128)(2,1)S(1)} %collective-permute-done.1.refs_2_), channel_id=1, source_target_pairs={{0,1},{1,0},{2,3},{3,2},{4,5},{5,4},{6,7},{7,6},{8,9},{9,8},{10,11... | collective-permute-start | bytes 884744 | tf_op jit(solution)/shard_map/ppermute | solution.py:36
  27.2 0.7 copy-start.8
  27.9 1.6 %collective-permute-start.7 = (bf16[4,32,1152]{2,1,0:T(8,128)(2,1)S(1)}, bf16[4,32,1152]{2,1,0:T(8,128)(2,1)S(1)}, u32[]{:S(2)}, u32[]{:S(2)}) collective-permute-start(bf16[4,32,1152]{2,1,0:T(8,128)(2,1)S(1)} %collective-permute-done.6.refs_6_), channel_id=1, source_target_pairs={{0,1},{1,0},{2,3},{3,2},{4,5},{5,4},{6,7},{7,6},{8,9},{9,8},{10,11... | collective-permute-start | bytes 884744 | tf_op jit(solution)/shard_map/ppermute | solution.py:36
  27.9 0.7 copy-start.10
  29.5 1.0 copy-start.7
  30.5 1.0 copy-start.9
  31.4 1.0 copy-start.11
  44.1 0.7 copy-start
  44.7 1.6 %collective-permute-start.8 = (f32[64,576]{1,0:T(8,128)}, f32[64,576]{1,0:T(8,128)S(1)}, u32[]{:S(2)}, u32[]{:S(2)}) collective-permute-start(f32[64,576]{1,0:T(8,128)} %copy-done), channel_id=1, source_target_pairs={{0,1},{1,0},{2,3},{3,2},{4,5},{5,4},{6,7},{7,6},{8,9},{9,8},{10,11... | collective-permute-start | bytes 442376 | tf_op jit(solution)/shard_map/ppermute | solution.py:36
  46.3 0.9 copy-start.1
  47.3 0.7 copy-start.5
  49.2 1.5 %collective-permute-start.9 = (f32[64,640]{1,0:T(8,128)S(1)}, f32[64,640]{1,0:T(8,128)S(1)}, u32[]{:S(2)}, u32[]{:S(2)}) collective-permute-start(f32[64,640]{1,0:T(8,128)S(1)} %get-tuple-element.36), channel_id=1, source_target_pairs={{0,1},{1,0},{2,3},{3,2},{4,5},{5,4},{6,7},{7,6},{8,9},{9,8},{10,11... | collective-permute-start | bytes 491528 | tf_op jit(solution)/shard_map/ppermute | solution.py:36
  50.8 19.7 %collective-permute-start.16 = (f32[64,1152]{1,0:T(8,128)S(1)}, f32[64,1152]{1,0:T(8,128)S(1)}, u32[]{:S(2)}, u32[]{:S(2)}) collective-permute-start(f32[64,1152]{1,0:T(8,128)S(1)} %get-tuple-element.51), channel_id=1, source_target_pairs={{0,32},{1,33},{2,34},{3,35},{4,36},{5,37},{6,38},{7,39},{8,40},{9,... | collective-permute-start | bytes 884744 | tf_op jit(solution)/shard_map/ppermute | solution.py:44
  52.3 6.4 %collective-permute-start.10 = (f32[64,384]{1,0:T(8,128)S(1)}, f32[64,384]{1,0:T(8,128)S(1)}, u32[]{:S(2)}, u32[]{:S(2)}) collective-permute-start(f32[64,384]{1,0:T(8,128)S(1)} %maximum_maximum_fusion.s0), channel_id=1, source_target_pairs={{0,128},{1,129},{2,130},{3,131},{4,132},{5,133},{6,134},{7,135},{8... | collective-permute-start | bytes 294920 | tf_op jit(solution)/shard_map/ppermute | solution.py:36
  55.4 5.2 %collective-permute-start.11 = (f32[64,384]{1,0:T(8,128)S(1)}, f32[64,384]{1,0:T(8,128)S(1)}, u32[]{:S(2)}, u32[]{:S(2)}) collective-permute-start(f32[64,384]{1,0:T(8,128)S(1)} %concatenate.8), channel_id=1, source_target_pairs={{0,2},{1,3},{2,0},{3,1},{4,6},{5,7},{6,4},{7,5},{8,10},{9,11},{10,... | collective-permute-start | bytes 294920 | tf_op jit(solution)/shard_map/ppermute | solution.py:36
  56.1 5.8 %collective-permute-start.12 = (f32[64,384]{1,0:T(8,128)S(1)}, f32[64,384]{1,0:T(8,128)S(1)}, u32[]{:S(2)}, u32[]{:S(2)}) collective-permute-start(f32[64,384]{1,0:T(8,128)S(1)} %concatenate.8), channel_id=1, source_target_pairs={{0,130},{1,131},{2,128},{3,129},{4,134},{5,135},{6,132},{7,133},{8... | collective-permute-start | bytes 294920 | tf_op jit(solution)/shard_map/ppermute | solution.py:36
  56.7 14.5 %collective-permute-start.17 = (f32[64,1152]{1,0:T(8,128)S(1)}, f32[64,1152]{1,0:T(8,128)S(1)}, u32[]{:S(2)}, u32[]{:S(2)}) collective-permute-start(f32[64,1152]{1,0:T(8,128)S(1)} %get-tuple-element.52), channel_id=1, source_target_pairs={{0,64},{1,65},{2,66},{3,67},{4,68},{5,69},{6,70},{7,71},{8,72},{9,... | collective-permute-start | bytes 884744 | tf_op jit(solution)/shard_map/ppermute | solution.py:44
  58.7 18.2 %collective-permute-start.18 = (f32[64,1152]{1,0:T(8,128)S(1)}, f32[64,1152]{1,0:T(8,128)S(1)}, u32[]{:S(2)}, u32[]{:S(2)}) collective-permute-start(f32[64,1152]{1,0:T(8,128)S(1)} %get-tuple-element.53), channel_id=1, source_target_pairs={{0,96},{1,97},{2,98},{3,99},{4,100},{5,101},{6,102},{7,103},{8,104... | collective-permute-start | bytes 884744 | tf_op jit(solution)/shard_map/ppermute | solution.py:44
  67.7 40.7 %copy-start.3 = (bf16[8,1152]{1,0:T(8,128)(2,1)S(1)}, bf16[8,1152]{1,0:T(8,128)(2,1)}, u32[]{:S(2)}) copy-start(bf16[8,1152]{1,0:T(8,128)(2,1)} %captions.3) | copy-start | bytes 55300
  67.7 9.2 %collective-permute-start.13 = (bf16[144,896]{1,0:T(8,128)(2,1)S(1)}, bf16[144,896]{1,0:T(8,128)(2,1)S(1)}, u32[]{:S(2)}, u32[]{:S(2)}) collective-permute-start(bf16[144,896]{1,0:T(8,128)(2,1)S(1)} %get-tuple-element.47), channel_id=1, source_target_pairs={{0,32},{1,33},{2,34},{3,35},{4,36},{5,37},{6,38},{7,39},{8,40},{9,... | collective-permute-start | bytes 774152 | tf_op jit(solution)/shard_map/ppermute | solution.py:44
  69.0 11.1 %collective-permute-start.14 = (bf16[144,896]{1,0:T(8,128)(2,1)S(1)}, bf16[144,896]{1,0:T(8,128)(2,1)S(1)}, u32[]{:S(2)}, u32[]{:S(2)}) collective-permute-start(bf16[144,896]{1,0:T(8,128)(2,1)S(1)} %get-tuple-element.48), channel_id=1, source_target_pairs={{0,64},{1,65},{2,66},{3,67},{4,68},{5,69},{6,70},{7,71},{8,72},{9,... | collective-permute-start | bytes 774152 | tf_op jit(solution)/shard_map/ppermute | solution.py:44
  70.4 13.1 %collective-permute-start.15 = (bf16[144,896]{1,0:T(8,128)(2,1)S(1)}, bf16[144,896]{1,0:T(8,128)(2,1)S(1)}, u32[]{:S(2)}, u32[]{:S(2)}) collective-permute-start(bf16[144,896]{1,0:T(8,128)(2,1)S(1)} %get-tuple-element.49), channel_id=1, source_target_pairs={{0,96},{1,97},{2,98},{3,99},{4,100},{5,101},{6,102},{7,103},{8,104... | collective-permute-start | bytes 774152 | tf_op jit(solution)/shard_map/ppermute | solution.py:44

commit v3 on v2

--- a/solution.py
+++ b/solution.py
@@ -83,13 +83,15 @@
 
 
 def conv_kernel(cols, *refs):
-    pieces, weights, (x_ref, out_ref, pooled_ref, slope_ref, w_ref, sum_ref, part_ref, x_sem, w_sem, o_sem) = (
-        refs[:8],
-        refs[8],
-        refs[9:],
-    )
+    (mine, *near, held), w_ref, (x_ref, out_ref, mean_ref, slope_ref, sum_ref, part_ref, pooled_ref, x_sem, o_sem) = (
+        refs[:6],
+        refs[6],
+        refs[7:],
+    )
+    far = [mine] + [held.at[i] for i in range(held.shape[0])]
+    pieces = [far[0], near[0], far[1], near[1], far[2], near[2], far[3], near[3]]
     frame, half, _, _ = whereabouts()
-    steps, block, width = pieces[0].shape
+    steps, block, width = mine.shape
     group = pooled_ref.shape[0]
     wide = slope_ref.shape[2]
     copies = []
@@ -102,46 +104,36 @@
                 piece, x_ref.at[pl.ds(first, steps), pl.ds(start, block), :], x_sem.at[i]
             )
         )
-    for k in range(3):
-        for i in range(XL):
-            start = pl.multiple_of((frame ^ (i * CORE)) * (wide - 128), 128)
-            copies.append(
-                pltpu.make_async_copy(
-                    weights.at[k, :, pl.ds(start, wide)], w_ref.at[k, :, pl.ds(i * wide, wide)], w_sem.at[k, i]
-                )
-            )
     for copy in copies:
         copy.start()
-    filled = copies[len(pieces) :]
     x_ref[0] = jnp.zeros((group, width), BF16)
     x_ref[FRAMES + 1] = jnp.zeros((group, width), BF16)
     sum_ref[...] = jnp.zeros_like(sum_ref)
     part_ref[...] = jnp.zeros_like(part_ref)
-    for copy in copies[: len(pieces)]:
+    for copy in copies:
         copy.wait()
 
-    def step(m, first):
+    def step(m):
         base = m * steps
-        conv = jnp.zeros((steps * group, XL * wide), F32)
+        conv = None
         for k in range(3):
-            if first:
-                for copy in filled[k * XL : (k + 1) * XL]:
-                    copy.wait()
             rows = x_ref[pl.ds(base + k, steps)].reshape(steps * group, width)
-            conv = conv + jnp.dot(rows, w_ref[k], preferred_element_type=F32)
-        tanh = jnp.tanh(ROOT * conv * (1.0 + CUBE * (conv * conv)))
-        gelu = 0.5 * conv * (1.0 + tanh)
+            term = jnp.dot(rows, w_ref[k], preferred_element_type=F32)
+            conv = term if conv is None else conv + term
+        tanh = jnp.tanh(conv * (ROOT + (ROOT * CUBE) * (conv * conv)))
+        part = 0.5 * conv
+        gelu = part + part * tanh
         part_ref[...] += jnp.sum(gelu.reshape(steps, group, XL * wide), axis=0)
-        conv, tanh = conv[:, :wide], tanh[:, :wide]
-        slope = 0.5 * (1.0 + tanh) + 0.5 * conv * (1.0 - tanh * tanh) * (
-            ROOT * (1.0 + 3.0 * CUBE * (conv * conv))
+        conv, tanh, part = conv[:, :wide], tanh[:, :wide], part[:, :wide]
+        slope = 0.5 * (1.0 + tanh) + part * (1.0 - tanh * tanh) * (
+            ROOT + (3.0 * ROOT * CUBE) * (conv * conv)
         )
         slope_ref[pl.ds(base, steps)] = slope.reshape(steps, group, wide)
         sum_ref[...] += jnp.sum(x_ref[pl.ds(base + 1, steps)].astype(F32), axis=0)
 
     stores = []
     for m in range(FRAMES // steps):
-        step(m, m == 0)
+        step(m)
         rows = pl.ds(m * steps, steps)
         stores.append(pltpu.make_async_copy(slope_ref.at[rows], out_ref.at[rows], o_sem.at[m]))
         stores[-1].start()
@@ -157,12 +149,19 @@
                     sum_ref[:, g * cols : (g + 1) * cols] + gelu
                 ) / FRAMES
 
+    stores.append(pltpu.make_async_copy(pooled_ref, mean_ref, o_sem.at[FRAMES // steps]))
+    stores[-1].start()
     for store in stores:
         store.wait()
 
 
-def pair_kernel(cap_dev, mine, peer, v_ref, positive, across, *refs):
-    (keep_ref, send_ref, unit_ref, norm_ref), dv_refs, (pooled_ref, lay_ref) = refs[:4], refs[4 : 4 + Y], refs[4 + Y :]
+def pair_kernel(cap_dev, pooled_in, peer, v_ref, wanted, *refs):
+    (keep_ref, send_ref, unit_ref, norm_ref), dv_refs, (pooled_ref, lay_ref, mine, near_ref, sem) = refs[:4], refs[4 : 4 + Y], refs[4 + Y :]
+    first = pltpu.make_async_copy(pooled_in, mine, sem.at[0])
+    first.start()
+    load = pltpu.make_async_copy(wanted, near_ref, sem.at[1])
+    load.start()
+    first.wait()
     frame, half, y_pos, _ = whereabouts()
     part = mine.shape[1]
     cols = part // 2
@@ -176,22 +175,25 @@
     v_low = v_ref[...]
     dots = lax.dot_general(u_low, v_low, (((1,), (1,)), ((), ())), preferred_element_type=F32)
     logits = 10.0 * dots - 10.0
-    first = jnp.where(half == 0, positive[...], across[...])
-    second = jnp.where(half == 0, across[...], positive[...])
-    wanted = jnp.concatenate([first, second], axis=0)
     row = lax.broadcasted_iota(jnp.int32, (1, v_low.shape[0]), 1)
     ids = ((half * (Y * Z) + row // cap_dev) * (XL * CORE) + frame) * cap_dev + row % cap_dev
-    match = jnp.where(wanted == ids, 1.0, 0.0).astype(F32)
+    load.wait()
+    match = jnp.where(near_ref[...] == ids, 1.0, 0.0).astype(F32)
     sign = 2.0 * match - 1.0
     turned = -sign * logits
     terms = jnp.maximum(turned, 0.0) + jnp.log1p(jnp.exp(-jnp.abs(turned)))
     total = jnp.sum(jnp.sum(terms, axis=1, keepdims=True), axis=0, keepdims=True)
-    coef = (10.0 * (1.0 / (1.0 + jnp.exp(-logits)) - match)).astype(BF16)
+    grad = 10.0 * (1.0 / (1.0 + jnp.exp(-logits)) - match)
+    coef = grad.astype(BF16)
     du = jnp.dot(coef, v_low, preferred_element_type=F32)
-    dv = lax.dot_general(coef, u_low, (((0,), (0,)), ((), ())), preferred_element_type=F32)
-    lay_ref[...] = dv.reshape(lay_ref.shape)
+    share = coef.shape[1] // Y
+    for y in range(Y):
+        block = grad[:, y * share : (y + 1) * share]
+        pad = jnp.zeros((group, lay_ref.shape[2] - share), F32)
+        lay_ref[y] = jnp.concatenate([block, pad], axis=1).astype(BF16)
     for i, dv_ref in enumerate(dv_refs):
-        dv_ref[...] = lay_ref[(y_pos + i) % Y]
+        dv_ref[:, 0 : 2 * part] = u_low
+        dv_ref[:, 2 * part :] = lay_ref[(y_pos + i) % Y]
     along = jnp.sum(unit * du, axis=1, keepdims=True)
     pooled_ref[...] = du
     spare = keep_ref.shape[1] - part
@@ -205,13 +207,23 @@
     norm_ref[...] = pnorm
 
 
+def turn_kernel(x_ref, out_ref):
+    half = whereabouts()[1]
+    tile = 128
+    tiles = out_ref.shape[0] // tile
+    offset = x_ref.shape[2] - tiles * tile
+    for m in range(tiles):
+        start = pl.multiple_of(half * offset + m * tile, tile)
+        rows = x_ref[:, :, pl.ds(start, tile)].reshape(x_ref.shape[0] * x_ref.shape[1], tile)
+        out_ref[m * tile : (m + 1) * tile, :] = rows.T
+
+
 def weight_kernel(s0, s1, s2, s3, unit, norm, slope_in, x_ref, *refs):
     outs, (d_ref, g_ref, p_ref, c_ref, slope, sem) = refs[:Y], refs[Y:]
     load = pltpu.make_async_copy(slope_in, slope, sem)
     load.start()
     frame, half, y_pos, _ = whereabouts()
     group, cols = unit.shape
-    width = x_ref.shape[2]
     wide = slope.shape[2]
     shift = cols + 128 - wide
     share = outs[0].shape[0]
@@ -236,20 +248,8 @@
         dconv = (slope[t] * dpooled).astype(BF16)
         for k in range(3):
             d_ref[(t + k) * group : (t + k + 1) * group, k * wide : (k + 1) * wide] = dconv
-    tile = 128
-    tiles = roundup(Y * share, tile) // tile
-    offset = width - tiles * tile
-
-    def step(m, carry):
-        start = pl.multiple_of(half * offset + m * tile, tile)
-        rows = x_ref[:, :, pl.ds(start, tile)].reshape((FRAMES + 2) * group, tile)
-        g_ref[pl.ds(pl.multiple_of(m * tile, tile), tile), :] = lax.dot_general(
-            rows, d_ref[...], (((0,), (0,)), ((), ())), preferred_element_type=F32
-        )
-        return carry
-
-    lax.fori_loop(0, tiles, step, 0)
-    skip = tiles * tile - Y * share
+    g_ref[...] = jnp.dot(x_ref[...], d_ref[...], preferred_element_type=F32)
+    skip = x_ref.shape[0] - Y * share
     lane = lax.broadcasted_iota(jnp.int32, (share, c_ref.shape[1] - 3 * cols), 1)
     c_ref[:, 3 * cols :] = loss_lanes(total, lane)
     for i, out_ref in enumerate(outs):
@@ -274,7 +274,7 @@
 
 
 def along_y_kernel(first_lane, *refs):
-    ins, caps, (out_ref, sum_ref, lay_ref) = refs[:Y], refs[Y : 2 * Y], refs[2 * Y :]
+    ins, caps, (out_ref, sum_ref, lay_ref) = refs[:Y], refs[Y], refs[Y + 1 :]
     rows, lanes = ins[0].shape[0] // Z, ins[0].shape[1]
     kept, packed = lay_ref.shape[1:]
     total = ins[0][...].astype(F32)
@@ -295,15 +295,23 @@
                     z * rows + kept + j : z * rows + kept + j + 1, i * 128 : (i + 1) * 128
                 ]
     out_ref[:, :, 0:packed] = lay_ref[...].astype(BF16)
-    total = caps[0][...]
-    for part in caps[1:]:
-        total = total + part[...]
+    out_ref[:, :, packed:] = caps[...]
+
+
+def caption_y_kernel(own, *refs):
+    ins, out_ref = refs[:Y], refs[Y]
+    width = out_ref.shape[2]
+    total = None
+    for part in ins:
+        term = lax.dot_general(
+            part[:, width:], part[:, 0:width], (((0,), (0,)), ((), ())), preferred_element_type=F32
+        )
+        total = term if total is None else total + term
     high = total.astype(BF16).astype(F32)
     low = total - high
-    own = total.shape[0] // Z
     for z in range(Z):
-        both = jnp.concatenate([high[z * own : (z + 1) * own], low[z * own : (z + 1) * own]], axis=0)
-        out_ref[z, :, packed:] = both.astype(BF16)
+        rows = slice(z * own, (z + 1) * own)
+        out_ref[z] = jnp.concatenate([high[rows], low[rows]], axis=0).astype(BF16)
 
 
 def along_z_kernel(lanes, packed, in_ref, captions, grad_ref, loss_ref, cap_ref, sum_ref, turn_ref):
@@ -347,6 +355,14 @@
     return cnorm, capf / cnorm
 
 
+def column(values):
+    count = values.shape[1]
+    row = lax.broadcasted_iota(jnp.int32, (count, count), 0)
+    lane = lax.broadcasted_iota(jnp.int32, (count, count), 1)
+    spread = jnp.where(row == lane, values.astype(F32), 0.0)
+    return jnp.sum(spread, axis=1, keepdims=True).astype(jnp.int32)
+
+
 def caption_kernel(captions, out_ref, unit_ref, turn_ref):
     frame = whereabouts()[0]
     cols = captions.shape[1] // len(ORDER)
@@ -361,6 +377,33 @@
 
     low = turn_ref[...].astype(BF16)
     out_ref[...] = jnp.broadcast_to(low[None], out_ref.shape)
+
+
+def stage_kernel(wide, positive, across, weights, *refs):
+    ins, (out_ref, far_ref, w_ref, near_ref, pos_ref, sem, w_sem) = refs[:-7], refs[-7:]
+    frame, half, _, _ = whereabouts()
+    copies = []
+    for k in range(3):
+        for i in range(XL):
+            start = pl.multiple_of((frame ^ (i * CORE)) * (wide - 128), 128)
+            copies.append(
+                pltpu.make_async_copy(
+                    weights.at[k, :, pl.ds(start, wide)], w_ref.at[k, :, pl.ds(i * wide, wide)], w_sem.at[k, i]
+                )
+            )
+    load = pltpu.make_async_copy(positive, pos_ref, sem.at[len(ins) + 1])
+    copies = [pltpu.make_async_copy(piece, out_ref.at[i], sem.at[i]) for i, piece in enumerate(ins)] + copies
+    load.start()
+    for copy in copies:
+        copy.start()
+    load.wait()
+    first = jnp.where(half == 0, pos_ref[...], across[...])
+    second = jnp.where(half == 0, across[...], pos_ref[...])
+    near_ref[...] = jnp.concatenate([column(first), column(second)], axis=0)
+    copies.append(pltpu.make_async_copy(near_ref, far_ref, sem.at[len(ins)]))
+    copies[-1].start()
+    for copy in copies:
+        copy.wait()
 
 
 def on_device(frames, conv_weight, captions, positive):
@@ -370,17 +413,9 @@
     group = clip_dev * XH
     rows = FRAMES * group
 
+    positive = positive[None, :]
+    across = swap(positive, 1, 0, 0)
     mine = jnp.transpose(frames, (1, 0, 2))
-    first = swap(mine, 0, 0, 1)
-    far = [swap(mine, 0, 1, 0), swap(mine, 1, 0, 0), swap(mine, 1, 1, 0)]
-    positive = positive[:, None]
-    across = swap(positive, 1, 0, 0)
-    far[1], across = lax.optimization_barrier((far[1], across))
-    near = [first] + [swap(part, 0, 0, 1) for part in far]
-    far = [mine] + far
-    given = captions
-    pieces = [far[0], near[0], far[1], near[1], far[2], near[2], far[3], near[3]]
-
     (spread,) = call(
         caption_kernel,
         4,
@@ -388,30 +423,54 @@
         [pltpu.VMEM((cap_dev, width), F32), pltpu.VMEM((cap_dev, width), F32)],
         0,
         Y * Z * cap_dev * width * 2,
-        given,
-    )
+        captions,
+    )
+    mine, across, spread = lax.optimization_barrier((mine, across, spread))
+    first = swap(mine, 0, 0, 1)
+    far = [swap(mine, 0, 1, 0), swap(mine, 1, 0, 0), swap(mine, 1, 1, 0)]
+    near = [first] + [swap(part, 0, 0, 1) for part in far]
+    wide = cols + (XL * CORE - 1) * (cols % 128)
+    held, wanted, weights = call(
+        functools.partial(stage_kernel, wide),
+        2,
+        [((3,) + mine.shape, BF16), ((group, 1), jnp.int32), ((3, width, XL * wide), BF16)],
+        [
+            pltpu.VMEM((group, 1), jnp.int32),
+            pltpu.VMEM(positive.shape, jnp.int32),
+            pltpu.SemaphoreType.DMA((5,)),
+            pltpu.SemaphoreType.DMA((3, XL)),
+        ],
+        0,
+        mine.size * 12,
+        positive,
+        across,
+        conv_weight,
+        *far,
+        loose={0: pltpu.HBM, 2: pltpu.HBM} | {i: pl.ANY for i in range(3, 6)},
+        far={0: pltpu.HBM, 1: pltpu.HBM},
+    )
+    pieces = [mine, *near, held]
+
     piece = exchange(spread, YZ_GROUPS).reshape(Y * Z * cap_dev, width)
     count = piece.shape[0]
-    wide = cols + (XL * CORE - 1) * (cols % 128)
     x, slope, pooled = call(
         functools.partial(conv_kernel, cols),
         24,
         [((FRAMES + 2, group, width), BF16), ((FRAMES, group, wide), F32), ((group, XL * cols), F32)],
         [
             pltpu.VMEM((FRAMES, group, wide), F32),
-            pltpu.VMEM((3, width, XL * wide), BF16),
             pltpu.VMEM((group, width), F32),
             pltpu.VMEM((group, XL * wide), F32),
+            pltpu.VMEM((group, XL * cols), F32),
             pltpu.SemaphoreType.DMA((8,)),
-            pltpu.SemaphoreType.DMA((3, XL)),
-            pltpu.SemaphoreType.DMA((FRAMES // fr_dev,)),
+            pltpu.SemaphoreType.DMA((FRAMES // fr_dev + 1,)),
         ],
-        int(3 * rows * 3 * width * 2 * cols),
+        int(3.5 * rows * 3 * width * 2 * cols),
         3 * width * 2 * wide * 2,
         *pieces,
-        conv_weight,
-        loose={i: pl.ANY for i in range(8)} | {8: pltpu.HBM},
-        far={1: pltpu.HBM},
+        weights,
+        loose={i: pl.ANY for i in range(5)} | {5: pltpu.HBM},
+        far={1: pltpu.HBM, 2: pltpu.HBM},
     )
     pooled, piece = lax.optimization_barrier((pooled, piece))
     peer = swap(pooled, 0, 0, 1)
@@ -420,26 +479,42 @@
         functools.partial(pair_kernel, cap_dev),
         8,
         [((group, lanes), F32), ((group, lanes), F32), ((group, cols), F32), ((group, 1), F32)]
-        + [((count // Y, width), F32)] * Y,
-        [pltpu.VMEM((group, width), F32), pltpu.VMEM((Y, count // Y, width), F32)],
+        + [((group, width + roundup(count // Y, 128)), BF16)] * Y,
+        [
+            pltpu.VMEM((group, width), F32),
+            pltpu.VMEM((Y, group, roundup(count // Y, 128)), BF16),
+            pltpu.VMEM((group, 2 * cols), F32),
+            pltpu.VMEM((group, 1), jnp.int32),
+            pltpu.SemaphoreType.DMA((2,)),
+        ],
         6 * group * count * width,
         count * width * 6,
         pooled,
         peer,
         piece,
-        positive,
-        across,
+        wanted,
+        loose={0: pltpu.HBM, 3: pltpu.HBM},
     )
 
     chip = keep + swap(send, 0, 0, 1)
-    chip, *dv = lax.optimization_barrier((chip, *dv))
     tail = chip[:, 2 * cols : 2 * cols + 2]
     spare = jnp.zeros((group, roundup(cols + 2, 128) - cols - 2), F32)
     same = jnp.concatenate([chip[:, :cols], tail, spare], axis=1)
     cross = jnp.concatenate([chip[:, cols : 2 * cols], tail, spare], axis=1)
+    same, cross, x = lax.optimization_barrier((same, cross, x))
     parts = [same, swap(same, 1, 0, 0), swap(cross, 0, 1, 0), swap(cross, 1, 1, 0)]
 
     share = width // XH // Y
+    (x,) = call(
+        turn_kernel,
+        6,
+        [((roundup(Y * share, 128), rows + 2 * group), BF16)],
+        [],
+        0,
+        rows * width * 2,
+        x,
+    )
+    x, *dv = lax.optimization_barrier((x, *dv))
     packed = roundup(3 * cols + 3, 128)
     terms = call(
         weight_kernel,
@@ -463,6 +538,17 @@
         loose={6: pltpu.HBM},
     )
     dv = [dv[0]] + [move(dv[i], i, 0) for i in range(1, Y)]
+    *dv, first = lax.optimization_barrier((*dv, terms[1]))
+    terms = [terms[0], first, *terms[2:]]
+    (dv,) = call(
+        functools.partial(caption_y_kernel, cap_dev),
+        6,
+        [((Z, 2 * cap_dev, width), BF16)],
+        [],
+        2 * count * group * width,
+        count * width * 4,
+        *dv,
+    )
     terms = [terms[0]] + [move(terms[i], i, 0) for i in range(1, Y)]
     own_rows = share // Z
     kept = own_rows // 16 * 16
@@ -474,7 +560,7 @@
         0,
         share * packed * 16,
         *terms,
-        *dv,
+        dv,
     )
     terms = exchange(terms, Z_GROUPS)
     grad_weight, loss, grad_captions = call(

time: 112 us -> 101 us (0.902)
  local copies, waits for them, and re-layouts: 10.6 us -> 1.98 us
  waiting for transfers between devices: 21.1 us -> 15 us
  starting transfers between devices: 31.3 us -> 33.4 us
    unnamed x25 -> x5, local copies, waits for them, and re-layouts: 9.65 us -> 1.72 us
    ppermute x13, waiting for transfers between devices: 8.81 us -> 3.76 us  [swap(): return lax.ppermute(value, BOTH, pairs)]
    ppermute x6, waiting for transfers between devices: 12.3 us -> 9.54 us  [move(): return lax.ppermute(value, BOTH, pairs)]
    all_to_all x1, waiting for transfers between devices: 0.01 us -> 1.74 us  [exchange(): lax.all_to_all(value, 'clip', 0, 0, axis_index_groups=groups, tiled=True)]
    ppermute x6, starting transfers between devices: 7.15 us -> 8.78 us  [move(): return lax.ppermute(value, BOTH, pairs)]
    pallas_call x6 -> x9, Pallas kernels: 21.2 us -> 22.1 us  [call(): pl.pallas_call(body, out_shape=[far[i](s, d) if i in far else jax.ShapeDt...]
  transfers between devices with their start and end apart: 20 -> 20, of which waited for: 10 -> 7; matrix products, arithmetic and copies ran while one was open for 1% -> 1% of each run, Pallas kernels for 17% -> 18%
where the time goes in v3:
time: 101 us
  starting transfers between devices  33.4 us (33%)
  blocking collectives  25.5 us (25%)
  Pallas kernels  22.1 us (22%)
  waiting for transfers between devices  15 us (15%)
  between operations  2.59 us (3%)
  local copies, waits for them, and re-layouts  1.98 us (2%)
    all_to_all x1, blocking collectives, exchange(): lax.all_to_all(value, 'clip', 0, 0, axis_index_groups=groups, tiled=True)  25.5 us
    pallas_call x9, Pallas kernels, call(): pl.pallas_call(body, out_shape=[far[i](s, d) if i in far else jax.ShapeDt...  22.1 us
    ppermute x13, starting transfers between devices, swap(): return lax.ppermute(value, BOTH, pairs)  12.9 us
    all_to_all x1, starting transfers between devices, exchange(): lax.all_to_all(value, 'clip', 0, 0, axis_index_groups=groups, tiled=True)  11.7 us
    ppermute x6, waiting for transfers between devices, move(): return lax.ppermute(value, BOTH, pairs)  9.54 us
    ppermute x6, starting transfers between devices, move(): return lax.ppermute(value, BOTH, pairs)  8.78 us
    ppermute x13, waiting for transfers between devices, swap(): return lax.ppermute(value, BOTH, pairs)  3.76 us
  transfers between devices with their start and end apart: 20, of which 7 were waited for; matrix products, arithmetic and copies ran while one was open for 1% of the time, Pallas kernels for 18%

profile of v3, /device:TPU:8, one launch (start us, length us, event | category | flops | bytes accessed | tf_op | source)
XLA Modules:
  0.0 100.7 jit_solution(8586781487980646207)
XLA Ops:
  0.6 3.1 %collective-permute-start = (s32[1,32]{1,0:T(1,128)}, s32[1,32]{1,0:T(1,128)S(1)}, u32[]{:S(2)}, u32[]{:S(2)}) collective-permute-start(s32[1,32]{1,0:T(1,128)} %bitcast.12), channel_id=1, source_target_pairs={{0,128},{1,129},{2,130},{3,131},{4,132},{5,133},{6,134},{7,135},{8... | collective-permute-start | bytes 392 | tf_op jit(solution)/shard_map/ppermute | solution.py:36
  3.7 0.0 copy-start
  3.7 0.7 copy-done
  4.5 1.0 %shard_map.67 = bf16[32,8,1152]{2,1,0:T(8,128)(2,1)} custom-call(bf16[8,1152]{1,0:T(8,128)(2,1)S(1)} %copy-done), custom_call_target="tpu_custom_call" | custom-call | bytes 589824 | tf_op jit(solution)/shard_map/pallas_call | solution.py:72
  5.5 1.0 copy.9
  6.5 0.0 collective-permute-done.across
  6.5 0.9 collective-permute-start.2
  7.4 2.7 %collective-permute-start.4 = (bf16[4,32,1152]{2,1,0:T(8,128)(2,1)S(1)}, bf16[4,32,1152]{2,1,0:T(8,128)(2,1)S(1)}, u32[]{:S(2)}, u32[]{:S(2)}) collective-permute-start(bf16[4,32,1152]{2,1,0:T(8,128)(2,1)S(1)} %bitcast.8), channel_id=1, source_target_pairs={{0,128},{1,129},{2,130},{3,131},{4,132},{5,133},{6,134},{7,135},{8... | collective-permute-start | bytes 884744 | tf_op jit(solution)/shard_map/ppermute | solution.py:36
  10.1 1.2 %collective-permute-start.6 = (bf16[4,32,1152]{2,1,0:T(8,128)(2,1)S(1)}, bf16[4,32,1152]{2,1,0:T(8,128)(2,1)S(1)}, u32[]{:S(2)}, u32[]{:S(2)}) collective-permute-start(bf16[4,32,1152]{2,1,0:T(8,128)(2,1)S(1)} %bitcast.9), channel_id=1, source_target_pairs={{0,130},{1,131},{2,128},{3,129},{4,134},{5,135},{6,132},{7,133},{8... | collective-permute-start | bytes 884744 | tf_op jit(solution)/shard_map/ppermute | solution.py:36
  11.3 11.7 %all-to-all-start = ((bf16[32,8,1152]{2,1,0:T(8,128)(2,1)}), bf16[32,8,1152]{2,1,0:T(8,128)(2,1)S(1)}, u32[]{:S(2)}, u32[]{:S(2)}) async-start(bf16[32,8,1152]{2,1,0:T(8,128)(2,1)} %shard_map.67), calls=%async_computation | async-start | bytes 1179648 | tf_op jit(solution)/shard_map/all_to_all | solution.py:52
  23.0 0.1 collective-permute-start.1
  23.1 0.0 collective-permute-done.2.refs_0_
  23.1 0.5 collective-permute-start.3
  23.6 0.0 collective-permute-done.4.refs_1_
  23.6 0.1 collective-permute-start.5
  23.7 1.0 collective-permute-done.6.refs_2_
  24.7 0.0 collective-permute-start.7
  24.7 3.0 %shard_map.68 = (bf16[3,4,32,1152]{3,2,1,0:T(8,128)(2,1)}, s32[64,1]{1,0:T(8,128)}, bf16[3,1152,768]{2,1,0:T(8,128)(2,1)S(1)}) custom-call(s32[1,32]{1,0:T(1,128)} %bitcast.13, s32[1,32]{1,0:T(1,128)S(1)} %collective-permute-done.across, bf16[3,1152,1152]{2,1,0:T(8,128)(2,1)} %weights.1, bf16[4,32,1152]{2,1,0:T(8,128)(2,1)S(1)} %collective-permute-done.2.refs_0_, ...), custom_call_target="tpu_custom_call" | custom-call | bytes 1769472 | tf_op jit(solution)/shard_map/pallas_call | solution.py:72
  27.7 0.0 collective-permute-done.1.refs_1_
  27.7 0.0 collective-permute-done.3.refs_2_
  27.7 0.0 collective-permute-done.5.refs_3_
  27.7 0.0 collective-permute-done.7.refs_4_
  27.7 9.0 %shard_map.69 = (bf16[18,64,1152]{2,1,0:T(8,128)(2,1)S(1)}, f32[16,64,384]{2,1,0:T(8,128)}, f32[64,576]{1,0:T(8,128)}) custom-call(bf16[4,32,1152]{2,1,0:T(8,128)(2,1)S(1)} %bitcast.11, bf16[4,32,1152]{2,1,0:T(8,128)(2,1)S(1)} %collective-permute-done.1.refs_1_, bf16[4,32,1152]{2,1,0:T(8,128)(2,1)S(1)} %collective-permute-done.3.refs_2_, ...), custom_call_target="tpu_custom_call" | custom-call | flops 7134511104 | bytes 5308416 | tf_op jit(solution)/shard_map/pallas_call | solution.py:72
  36.7 1.7 %all-to-all-done = bf16[32,8,1152]{2,1,0:T(8,128)(2,1)S(1)} async-done(((bf16[32,8,1152]{2,1,0:T(8,128)(2,1)}), bf16[32,8,1152]{2,1,0:T(8,128)(2,1)S(1)}, u32[]{:S(2)}, u32[]{:S(2)}) %all-to-all-start) | async-done | bytes 589856 | tf_op jit(solution)/shard_map/all_to_all | solution.py:52
  38.5 0.0 collective-permute-start.8
  38.5 1.6 %collective-permute-done.8.peer = f32[64,576]{1,0:T(8,128)S(1)} collective-permute-done((f32[64,576]{1,0:T(8,128)}, f32[64,576]{1,0:T(8,128)S(1)}, u32[]{:S(2)}, u32[]{:S(2)}) %collective-permute-start.8) | collective-permute-done | bytes 147488 | tf_op jit(solution)/shard_map/ppermute | solution.py:36
  40.1 2.0 %shard_map.70 = (f32[64,640]{1,0:T(8,128)S(1)}, f32[64,640]{1,0:T(8,128)S(1)}, f32[64,288]{1,0:T(8,128)S(1)}, f32[64,1]{1,0:T(8,128)S(1)}, bf16[64,1280]{1,0:T(8...) custom-call(f32[64,576]{1,0:T(8,128)} %get-tuple-element.48.pooled_in, ...), custom_call_target="tpu_custom_call" | custom-call | flops 113246208 | bytes 1769472 | tf_op jit(solution)/shard_map/pallas_call | solution.py:72
  42.1 0.2 collective-permute-start.9
  42.3 0.1 pad.3.clone
  42.4 1.2 %collective-permute-done.9 = f32[64,640]{1,0:T(8,128)S(1)} collective-permute-done((f32[64,640]{1,0:T(8,128)S(1)}, f32[64,640]{1,0:T(8,128)S(1)}, u32[]{:S(2)}, u32[]{:S(2)}) %collective-permute-start.9) | collective-permute-done | bytes 163872 | tf_op jit(solution)/shard_map/ppermute | solution.py:36
  43.6 0.1 slice.14
  43.7 0.1 slice.15
  43.8 0.1 maximum_maximum_fusion.s0
  43.9 0.3 collective-permute-start.10
  44.2 1.8 %collective-permute-start.11 = (f32[64,384]{1,0:T(8,128)S(1)}, f32[64,384]{1,0:T(8,128)S(1)}, u32[]{:S(2)}, u32[]{:S(2)}) collective-permute-start(f32[64,384]{1,0:T(8,128)S(1)} %concatenate.8), channel_id=1, source_target_pairs={{0,2},{1,3},{2,0},{3,1},{4,6},{5,7},{6,4},{7,5},{8,10},{9,11},{10,... | collective-permute-start | bytes 294920 | tf_op jit(solution)/shard_map/ppermute | solution.py:36
  46.0 2.0 %collective-permute-start.12 = (f32[64,384]{1,0:T(8,128)S(1)}, f32[64,384]{1,0:T(8,128)S(1)}, u32[]{:S(2)}, u32[]{:S(2)}) collective-permute-start(f32[64,384]{1,0:T(8,128)S(1)} %concatenate.8), channel_id=1, source_target_pairs={{0,130},{1,131},{2,128},{3,129},{4,134},{5,135},{6,132},{7,133},{8... | collective-permute-start | bytes 294920 | tf_op jit(solution)/shard_map/ppermute | solution.py:36
  48.0 0.4 shard_map.71.x_ref
  48.5 1.5 %collective-permute-start.13 = (bf16[64,1280]{1,0:T(8,128)(2,1)S(1)}, bf16[64,1280]{1,0:T(8,128)(2,1)S(1)}, u32[]{:S(2)}, u32[]{:S(2)}) collective-permute-start(bf16[64,1280]{1,0:T(8,128)(2,1)S(1)} %get-tuple-element.67), channel_id=1, source_target_pairs={{0,32},{1,33},{2,34},{3,35},{4,36},{5,37},{6,38},{7,39},{8,40},{9,... | collective-permute-start | bytes 491528 | tf_op jit(solution)/shard_map/ppermute | solution.py:44
  50.0 3.0 %collective-permute-start.14 = (bf16[64,1280]{1,0:T(8,128)(2,1)S(1)}, bf16[64,1280]{1,0:T(8,128)(2,1)S(1)}, u32[]{:S(2)}, u32[]{:S(2)}) collective-permute-start(bf16[64,1280]{1,0:T(8,128)(2,1)S(1)} %get-tuple-element.68), channel_id=1, source_target_pairs={{0,64},{1,65},{2,66},{3,67},{4,68},{5,69},{6,70},{7,71},{8,72},{9,... | collective-permute-start | bytes 491528 | tf_op jit(solution)/shard_map/ppermute | solution.py:44
  53.0 0.0 collective-permute-done.10.s1
  53.0 0.5 collective-permute-start.15
  53.4 0.0 collective-permute-done.11.s2
  53.4 0.0 collective-permute-done.12.s3
  53.5 4.6 %shard_map.72 = (bf16[144,896]{1,0:T(8,128)(2,1)S(1)}, bf16[144,896]{1,0:T(8,128)(2,1)S(1)}, bf16[144,896]{1,0:T(8,128)(2,1)S(1)}, bf16[144,896]{1,0:T(8,128)(2,1)S(1)}) custom-call(f32[64,384]{1,0:T(8,128)S(1)} %maximum_maximum_fusion.s0, f32[64,384]{1,0:T(8,128)S(1)} %collective-permute-done.10.s1, f32[64,384]{1,0:T(8,128)S(1)} %collective-permute-done.11.s2, ...), custom_call_target="tpu_custom_call" | custom-call | flops 1019215872 | bytes 2359296 | tf_op jit(solution)/shard_map/pallas_call | solution.py:72
  58.1 0.0 copy-start.1
  58.1 1.1 %collective-permute-start.17 = (bf16[144,896]{1,0:T(8,128)(2,1)S(1)}, bf16[144,896]{1,0:T(8,128)(2,1)S(1)}, u32[]{:S(2)}, u32[]{:S(2)}) collective-permute-start(bf16[144,896]{1,0:T(8,128)(2,1)S(1)} %get-tuple-element.72), channel_id=1, source_target_pairs={{0,64},{1,65},{2,66},{3,67},{4,68},{5,69},{6,70},{7,71},{8,72},{9,... | collective-permute-start | bytes 774152 | tf_op jit(solution)/shard_map/ppermute | solution.py:44
  59.2 2.6 %collective-permute-start.18 = (bf16[144,896]{1,0:T(8,128)(2,1)S(1)}, bf16[144,896]{1,0:T(8,128)(2,1)S(1)}, u32[]{:S(2)}, u32[]{:S(2)}) collective-permute-start(bf16[144,896]{1,0:T(8,128)(2,1)S(1)} %get-tuple-element.73), channel_id=1, source_target_pairs={{0,96},{1,97},{2,98},{3,99},{4,100},{5,101},{6,102},{7,103},{8,104... | collective-permute-start | bytes 774152 | tf_op jit(solution)/shard_map/ppermute | solution.py:44
  61.8 0.0 collective-permute-done.13.refs_1_
  61.8 0.0 collective-permute-done.14.refs_2_
  61.8 0.0 collective-permute-done.15.refs_3_
  61.8 0.1 collective-permute-start.16
  61.9 0.5 shard_map.73.refs_4_
  62.4 6.4 %collective-permute-done.17.refs_2_ = bf16[144,896]{1,0:T(8,128)(2,1)S(1)} collective-permute-done((bf16[144,896]{1,0:T(8,128)(2,1)S(1)}, bf16[144,896]{1,0:T(8,128)(2,1)S(1)}, u32[]{:S(2)}, u32[]{:S(2)}) %collective-permute-start.17) | collective-permute-done | bytes 258080 | tf_op jit(solution)/shard_map/ppermute | solution.py:44
  68.8 2.8 %collective-permute-done.18.refs_3_ = bf16[144,896]{1,0:T(8,128)(2,1)S(1)} collective-permute-done((bf16[144,896]{1,0:T(8,128)(2,1)S(1)}, bf16[144,896]{1,0:T(8,128)(2,1)S(1)}, u32[]{:S(2)}, u32[]{:S(2)}) %collective-permute-start.18) | collective-permute-done | bytes 258080 | tf_op jit(solution)/shard_map/ppermute | solution.py:44
  71.7 0.3 collective-permute-done.16.refs_1_
  71.9 0.4 shard_map.74
  72.4 25.5 %all_to_all.10.in_ref = bf16[8,16,2176]{2,1,0:T(8,128)(2,1)S(1)} all-to-all(bf16[8,16,2176]{2,1,0:T(8,128)(2,1)S(1)} %shard_map.74), channel_id=1, replica_groups={{0,4,8,12,16,20,24,28},{32,36,40,44,48,52,56,60},{64,68,72,76,80,84,88,..., dimensions={0} | all-to-all | bytes 1114112 | tf_op jit(solution)/shard_map/all_to_all | solution.py:52
  97.8 0.0 copy-done.1
  97.8 1.0 %shard_map.75 = (f32[3,18,288]{2,1,0:T(8,128)}, f32[1,1]{1,0:T(1,128)}, f32[8,1152]{1,0:T(8,128)}) custom-call(bf16[8,16,2176]{2,1,0:T(8,128)(2,1)S(1)} %all_to_all.10.in_ref, bf16[8,1152]{1,0:T(8,128)(2,1)S(1)} %copy-done.1), custom_call_target="tpu_custom_call" | custom-call | bytes 258048 | tf_op jit(solution)/shard_map/pallas_call | solution.py:72
  (4 shorter events, 0.0 us)
Async XLA Ops:
  0.6 5.9 %collective-permute-start = (s32[1,32]{1,0:T(1,128)}, s32[1,32]{1,0:T(1,128)S(1)}, u32[]{:S(2)}, u32[]{:S(2)}) collective-permute-start(s32[1,32]{1,0:T(1,128)} %bitcast.12), channel_id=1, source_target_pairs={{0,128},{1,129},{2,130},{3,131},{4,132},{5,133},{6,134},{7,135},{8... | collective-permute-start | bytes 392 | tf_op jit(solution)/shard_map/ppermute | solution.py:36
  3.7 0.7 copy-start
  6.5 16.6 %collective-permute-start.2 = (bf16[4,32,1152]{2,1,0:T(8,128)(2,1)S(1)}, bf16[4,32,1152]{2,1,0:T(8,128)(2,1)S(1)}, u32[]{:S(2)}, u32[]{:S(2)}) collective-permute-start(bf16[4,32,1152]{2,1,0:T(8,128)(2,1)S(1)} %bitcast.7), channel_id=1, source_target_pairs={{0,2},{1,3},{2,0},{3,1},{4,6},{5,7},{6,4},{7,5},{8,10},{9,11},{10,... | collective-permute-start | bytes 884744 | tf_op jit(solution)/shard_map/ppermute | solution.py:36
  7.4 16.2 %collective-permute-start.4 = (bf16[4,32,1152]{2,1,0:T(8,128)(2,1)S(1)}, bf16[4,32,1152]{2,1,0:T(8,128)(2,1)S(1)}, u32[]{:S(2)}, u32[]{:S(2)}) collective-permute-start(bf16[4,32,1152]{2,1,0:T(8,128)(2,1)S(1)} %bitcast.8), channel_id=1, source_target_pairs={{0,128},{1,129},{2,130},{3,131},{4,132},{5,133},{6,134},{7,135},{8... | collective-permute-start | bytes 884744 | tf_op jit(solution)/shard_map/ppermute | solution.py:36
  10.1 14.6 %collective-permute-start.6 = (bf16[4,32,1152]{2,1,0:T(8,128)(2,1)S(1)}, bf16[4,32,1152]{2,1,0:T(8,128)(2,1)S(1)}, u32[]{:S(2)}, u32[]{:S(2)}) collective-permute-start(bf16[4,32,1152]{2,1,0:T(8,128)(2,1)S(1)} %bitcast.9), channel_id=1, source_target_pairs={{0,130},{1,131},{2,128},{3,129},{4,134},{5,135},{6,132},{7,133},{8... | collective-permute-start | bytes 884744 | tf_op jit(solution)/shard_map/ppermute | solution.py:36
  11.3 27.2 %all-to-all-start = ((bf16[32,8,1152]{2,1,0:T(8,128)(2,1)}), bf16[32,8,1152]{2,1,0:T(8,128)(2,1)S(1)}, u32[]{:S(2)}, u32[]{:S(2)}) async-start(bf16[32,8,1152]{2,1,0:T(8,128)(2,1)} %shard_map.67), calls=%async_computation | async-start | bytes 1179648 | tf_op jit(solution)/shard_map/all_to_all | solution.py:52
  23.0 4.7 %collective-permute-start.1 = (bf16[4,32,1152]{2,1,0:T(8,128)(2,1)S(1)}, bf16[4,32,1152]{2,1,0:T(8,128)(2,1)S(1)}, u32[]{:S(2)}, u32[]{:S(2)}) collective-permute-start(bf16[4,32,1152]{2,1,0:T(8,128)(2,1)S(1)} %bitcast.10), channel_id=1, source_target_pairs={{0,1},{1,0},{2,3},{3,2},{4,5},{5,4},{6,7},{7,6},{8,9},{9,8},{10,11... | collective-permute-start | bytes 884744 | tf_op jit(solution)/shard_map/ppermute | solution.py:36
  23.1 4.6 %collective-permute-start.3 = (bf16[4,32,1152]{2,1,0:T(8,128)(2,1)S(1)}, bf16[4,32,1152]{2,1,0:T(8,128)(2,1)S(1)}, u32[]{:S(2)}, u32[]{:S(2)}) collective-permute-start(bf16[4,32,1152]{2,1,0:T(8,128)(2,1)S(1)} %collective-permute-done.2.refs_0_), channel_id=1, source_target_pairs={{0,1},{1,0},{2,3},{3,2},{4,5},{5,4},{6,7},{7,6},{8,9},{9,8},{10,11... | collective-permute-start | bytes 884744 | tf_op jit(solution)/shard_map/ppermute | solution.py:36
  23.6 4.1 %collective-permute-start.5 = (bf16[4,32,1152]{2,1,0:T(8,128)(2,1)S(1)}, bf16[4,32,1152]{2,1,0:T(8,128)(2,1)S(1)}, u32[]{:S(2)}, u32[]{:S(2)}) collective-permute-start(bf16[4,32,1152]{2,1,0:T(8,128)(2,1)S(1)} %collective-permute-done.4.refs_1_), channel_id=1, source_target_pairs={{0,1},{1,0},{2,3},{3,2},{4,5},{5,4},{6,7},{7,6},{8,9},{9,8},{10,11... | collective-permute-start | bytes 884744 | tf_op jit(solution)/shard_map/ppermute | solution.py:36
  24.7 3.0 %collective-permute-start.7 = (bf16[4,32,1152]{2,1,0:T(8,128)(2,1)S(1)}, bf16[4,32,1152]{2,1,0:T(8,128)(2,1)S(1)}, u32[]{:S(2)}, u32[]{:S(2)}) collective-permute-start(bf16[4,32,1152]{2,1,0:T(8,128)(2,1)S(1)} %collective-permute-done.6.refs_2_), channel_id=1, source_target_pairs={{0,1},{1,0},{2,3},{3,2},{4,5},{5,4},{6,7},{7,6},{8,9},{9,8},{10,11... | collective-permute-start | bytes 884744 | tf_op jit(solution)/shard_map/ppermute | solution.py:36
  38.5 1.6 %collective-permute-start.8 = (f32[64,576]{1,0:T(8,128)}, f32[64,576]{1,0:T(8,128)S(1)}, u32[]{:S(2)}, u32[]{:S(2)}) collective-permute-start(f32[64,576]{1,0:T(8,128)} %get-tuple-element.48.pooled_in), channel_id=1, source_target_pairs={{0,1},{1,0},{2,3},{3,2},{4,5},{5,4},{6,7},{7,6},{8,9},{9,8},{10,11... | collective-permute-start | bytes 442376 | tf_op jit(solution)/shard_map/ppermute | solution.py:36
  42.1 1.5 %collective-permute-start.9 = (f32[64,640]{1,0:T(8,128)S(1)}, f32[64,640]{1,0:T(8,128)S(1)}, u32[]{:S(2)}, u32[]{:S(2)}) collective-permute-start(f32[64,640]{1,0:T(8,128)S(1)} %get-tuple-element.52), channel_id=1, source_target_pairs={{0,1},{1,0},{2,3},{3,2},{4,5},{5,4},{6,7},{7,6},{8,9},{9,8},{10,11... | collective-permute-start | bytes 491528 | tf_op jit(solution)/shard_map/ppermute | solution.py:36
  43.9 9.1 %collective-permute-start.10 = (f32[64,384]{1,0:T(8,128)S(1)}, f32[64,384]{1,0:T(8,128)S(1)}, u32[]{:S(2)}, u32[]{:S(2)}) collective-permute-start(f32[64,384]{1,0:T(8,128)S(1)} %maximum_maximum_fusion.s0), channel_id=1, source_target_pairs={{0,128},{1,129},{2,130},{3,131},{4,132},{5,133},{6,134},{7,135},{8... | collective-permute-start | bytes 294920 | tf_op jit(solution)/shard_map/ppermute | solution.py:36
  44.2 9.2 %collective-permute-start.11 = (f32[64,384]{1,0:T(8,128)S(1)}, f32[64,384]{1,0:T(8,128)S(1)}, u32[]{:S(2)}, u32[]{:S(2)}) collective-permute-start(f32[64,384]{1,0:T(8,128)S(1)} %concatenate.8), channel_id=1, source_target_pairs={{0,2},{1,3},{2,0},{3,1},{4,6},{5,7},{6,4},{7,5},{8,10},{9,11},{10,... | collective-permute-start | bytes 294920 | tf_op jit(solution)/shard_map/ppermute | solution.py:36
  46.0 7.4 %collective-permute-start.12 = (f32[64,384]{1,0:T(8,128)S(1)}, f32[64,384]{1,0:T(8,128)S(1)}, u32[]{:S(2)}, u32[]{:S(2)}) collective-permute-start(f32[64,384]{1,0:T(8,128)S(1)} %concatenate.8), channel_id=1, source_target_pairs={{0,130},{1,131},{2,128},{3,129},{4,134},{5,135},{6,132},{7,133},{8... | collective-permute-start | bytes 294920 | tf_op jit(solution)/shard_map/ppermute | solution.py:36
  48.5 13.3 %collective-permute-start.13 = (bf16[64,1280]{1,0:T(8,128)(2,1)S(1)}, bf16[64,1280]{1,0:T(8,128)(2,1)S(1)}, u32[]{:S(2)}, u32[]{:S(2)}) collective-permute-start(bf16[64,1280]{1,0:T(8,128)(2,1)S(1)} %get-tuple-element.67), channel_id=1, source_target_pairs={{0,32},{1,33},{2,34},{3,35},{4,36},{5,37},{6,38},{7,39},{8,40},{9,... | collective-permute-start | bytes 491528 | tf_op jit(solution)/shard_map/ppermute | solution.py:44
  50.0 11.8 %collective-permute-start.14 = (bf16[64,1280]{1,0:T(8,128)(2,1)S(1)}, bf16[64,1280]{1,0:T(8,128)(2,1)S(1)}, u32[]{:S(2)}, u32[]{:S(2)}) collective-permute-start(bf16[64,1280]{1,0:T(8,128)(2,1)S(1)} %get-tuple-element.68), channel_id=1, source_target_pairs={{0,64},{1,65},{2,66},{3,67},{4,68},{5,69},{6,70},{7,71},{8,72},{9,... | collective-permute-start | bytes 491528 | tf_op jit(solution)/shard_map/ppermute | solution.py:44
  53.0 8.8 %collective-permute-start.15 = (bf16[64,1280]{1,0:T(8,128)(2,1)S(1)}, bf16[64,1280]{1,0:T(8,128)(2,1)S(1)}, u32[]{:S(2)}, u32[]{:S(2)}) collective-permute-start(bf16[64,1280]{1,0:T(8,128)(2,1)S(1)} %get-tuple-element.69), channel_id=1, source_target_pairs={{0,96},{1,97},{2,98},{3,99},{4,100},{5,101},{6,102},{7,103},{8,104... | collective-permute-start | bytes 491528 | tf_op jit(solution)/shard_map/ppermute | solution.py:44
  58.1 39.8 %copy-start.1 = (bf16[8,1152]{1,0:T(8,128)(2,1)S(1)}, bf16[8,1152]{1,0:T(8,128)(2,1)}, u32[]{:S(2)}) copy-start(bf16[8,1152]{1,0:T(8,128)(2,1)} %captions.3) | copy-start | bytes 55300
  58.1 10.8 %collective-permute-start.17 = (bf16[144,896]{1,0:T(8,128)(2,1)S(1)}, bf16[144,896]{1,0:T(8,128)(2,1)S(1)}, u32[]{:S(2)}, u32[]{:S(2)}) collective-permute-start(bf16[144,896]{1,0:T(8,128)(2,1)S(1)} %get-tuple-element.72), channel_id=1, source_target_pairs={{0,64},{1,65},{2,66},{3,67},{4,68},{5,69},{6,70},{7,71},{8,72},{9,... | collective-permute-start | bytes 774152 | tf_op jit(solution)/shard_map/ppermute | solution.py:44
  59.2 12.5 %collective-permute-start.18 = (bf16[144,896]{1,0:T(8,128)(2,1)S(1)}, bf16[144,896]{1,0:T(8,128)(2,1)S(1)}, u32[]{:S(2)}, u32[]{:S(2)}) collective-permute-start(bf16[144,896]{1,0:T(8,128)(2,1)S(1)} %get-tuple-element.73), channel_id=1, source_target_pairs={{0,96},{1,97},{2,98},{3,99},{4,100},{5,101},{6,102},{7,103},{8,104... | collective-permute-start | bytes 774152 | tf_op jit(solution)/shard_map/ppermute | solution.py:44
  61.8 10.1 %collective-permute-start.16 = (bf16[144,896]{1,0:T(8,128)(2,1)S(1)}, bf16[144,896]{1,0:T(8,128)(2,1)S(1)}, u32[]{:S(2)}, u32[]{:S(2)}) collective-permute-start(bf16[144,896]{1,0:T(8,128)(2,1)S(1)} %get-tuple-element.71), channel_id=1, source_target_pairs={{0,32},{1,33},{2,34},{3,35},{4,36},{5,37},{6,38},{7,39},{8,40},{9,... | collective-permute-start | bytes 774152 | tf_op jit(solution)/shard_map/ppermute | solution.py:44

commit v4 on v3

--- a/solution.py
+++ b/solution.py
@@ -83,11 +83,12 @@
 
 
 def conv_kernel(cols, *refs):
-    (mine, *near, held), w_ref, (x_ref, out_ref, mean_ref, slope_ref, sum_ref, part_ref, pooled_ref, x_sem, o_sem) = (
+    (mine, *near, held), (w_ref, positive, across), rest = (
         refs[:6],
-        refs[6],
-        refs[7:],
-    )
+        refs[6:9],
+        refs[9:],
+    )
+    x_ref, out_ref, mean_ref, wanted_ref, slope_ref, sum_ref, part_ref, pooled_ref, id_ref, pos_ref, x_sem, o_sem = rest
     far = [mine] + [held.at[i] for i in range(held.shape[0])]
     pieces = [far[0], near[0], far[1], near[1], far[2], near[2], far[3], near[3]]
     frame, half, _, _ = whereabouts()
@@ -104,12 +105,20 @@
                 piece, x_ref.at[pl.ds(first, steps), pl.ds(start, block), :], x_sem.at[i]
             )
         )
+    load = pltpu.make_async_copy(positive, pos_ref, o_sem.at[FRAMES // steps + 1])
+    load.start()
     for copy in copies:
         copy.start()
     x_ref[0] = jnp.zeros((group, width), BF16)
     x_ref[FRAMES + 1] = jnp.zeros((group, width), BF16)
     sum_ref[...] = jnp.zeros_like(sum_ref)
     part_ref[...] = jnp.zeros_like(part_ref)
+    load.wait()
+    first = jnp.where(half == 0, pos_ref[...], across[...])
+    second = jnp.where(half == 0, across[...], pos_ref[...])
+    id_ref[...] = jnp.concatenate([column(first), column(second)], axis=0)
+    stores = [pltpu.make_async_copy(id_ref, wanted_ref, o_sem.at[FRAMES // steps + 1])]
+    stores[0].start()
     for copy in copies:
         copy.wait()
 
@@ -131,7 +140,6 @@
         slope_ref[pl.ds(base, steps)] = slope.reshape(steps, group, wide)
         sum_ref[...] += jnp.sum(x_ref[pl.ds(base + 1, steps)].astype(F32), axis=0)
 
-    stores = []
     for m in range(FRAMES // steps):
         step(m)
         rows = pl.ds(m * steps, steps)
@@ -379,10 +387,10 @@
     out_ref[...] = jnp.broadcast_to(low[None], out_ref.shape)
 
 
-def stage_kernel(wide, positive, across, weights, *refs):
-    ins, (out_ref, far_ref, w_ref, near_ref, pos_ref, sem, w_sem) = refs[:-7], refs[-7:]
-    frame, half, _, _ = whereabouts()
-    copies = []
+def stage_kernel(wide, weights, *refs):
+    ins, (out_ref, w_ref, sem, w_sem) = refs[:-4], refs[-4:]
+    frame = whereabouts()[0]
+    copies = [pltpu.make_async_copy(piece, out_ref.at[i], sem.at[i]) for i, piece in enumerate(ins)]
     for k in range(3):
         for i in range(XL):
             start = pl.multiple_of((frame ^ (i * CORE)) * (wide - 128), 128)
@@ -391,17 +399,8 @@
                     weights.at[k, :, pl.ds(start, wide)], w_ref.at[k, :, pl.ds(i * wide, wide)], w_sem.at[k, i]
                 )
             )
-    load = pltpu.make_async_copy(positive, pos_ref, sem.at[len(ins) + 1])
-    copies = [pltpu.make_async_copy(piece, out_ref.at[i], sem.at[i]) for i, piece in enumerate(ins)] + copies
-    load.start()
     for copy in copies:
         copy.start()
-    load.wait()
-    first = jnp.where(half == 0, pos_ref[...], across[...])
-    second = jnp.where(half == 0, across[...], pos_ref[...])
-    near_ref[...] = jnp.concatenate([column(first), column(second)], axis=0)
-    copies.append(pltpu.make_async_copy(near_ref, far_ref, sem.at[len(ins)]))
-    copies[-1].start()
     for copy in copies:
         copy.wait()
 
@@ -425,52 +424,49 @@
         Y * Z * cap_dev * width * 2,
         captions,
     )
-    mine, across, spread = lax.optimization_barrier((mine, across, spread))
     first = swap(mine, 0, 0, 1)
     far = [swap(mine, 0, 1, 0), swap(mine, 1, 0, 0), swap(mine, 1, 1, 0)]
     near = [first] + [swap(part, 0, 0, 1) for part in far]
     wide = cols + (XL * CORE - 1) * (cols % 128)
-    held, wanted, weights = call(
+    held, weights = call(
         functools.partial(stage_kernel, wide),
         2,
-        [((3,) + mine.shape, BF16), ((group, 1), jnp.int32), ((3, width, XL * wide), BF16)],
-        [
-            pltpu.VMEM((group, 1), jnp.int32),
-            pltpu.VMEM(positive.shape, jnp.int32),
-            pltpu.SemaphoreType.DMA((5,)),
-            pltpu.SemaphoreType.DMA((3, XL)),
-        ],
+        [((3,) + mine.shape, BF16), ((3, width, XL * wide), BF16)],
+        [pltpu.SemaphoreType.DMA((3,)), pltpu.SemaphoreType.DMA((3, XL))],
         0,
         mine.size * 12,
-        positive,
-        across,
         conv_weight,
         *far,
-        loose={0: pltpu.HBM, 2: pltpu.HBM} | {i: pl.ANY for i in range(3, 6)},
-        far={0: pltpu.HBM, 1: pltpu.HBM},
+        loose={0: pltpu.HBM} | {i: pl.ANY for i in range(1, 4)},
+        far={0: pltpu.HBM},
     )
     pieces = [mine, *near, held]
 
     piece = exchange(spread, YZ_GROUPS).reshape(Y * Z * cap_dev, width)
     count = piece.shape[0]
-    x, slope, pooled = call(
+    x, slope, pooled, wanted = call(
         functools.partial(conv_kernel, cols),
         24,
-        [((FRAMES + 2, group, width), BF16), ((FRAMES, group, wide), F32), ((group, XL * cols), F32)],
+        [((FRAMES + 2, group, width), BF16), ((FRAMES, group, wide), F32), ((group, XL * cols), F32)]
+        + [((group, 1), jnp.int32)],
         [
             pltpu.VMEM((FRAMES, group, wide), F32),
             pltpu.VMEM((group, width), F32),
             pltpu.VMEM((group, XL * wide), F32),
             pltpu.VMEM((group, XL * cols), F32),
+            pltpu.VMEM((group, 1), jnp.int32),
+            pltpu.VMEM(positive.shape, jnp.int32),
             pltpu.SemaphoreType.DMA((8,)),
-            pltpu.SemaphoreType.DMA((FRAMES // fr_dev + 1,)),
+            pltpu.SemaphoreType.DMA((FRAMES // fr_dev + 2,)),
         ],
         int(3.5 * rows * 3 * width * 2 * cols),
         3 * width * 2 * wide * 2,
         *pieces,
         weights,
-        loose={i: pl.ANY for i in range(5)} | {5: pltpu.HBM},
-        far={1: pltpu.HBM, 2: pltpu.HBM},
+        positive,
+        across,
+        loose={i: pl.ANY for i in range(5)} | {5: pltpu.HBM, 7: pltpu.HBM},
+        far={1: pltpu.HBM, 2: pltpu.HBM, 3: pltpu.HBM},
     )
     pooled, piece = lax.optimization_barrier((pooled, piece))
     peer = swap(pooled, 0, 0, 1)

time: 101 us -> 100 us (0.990)
  starting transfers between devices: 33.4 us -> 31.7 us
  blocking collectives: 25.5 us -> 26.8 us
    all_to_all x1, waiting for transfers between devices: 1.74 us -> 0.01 us  [exchange(): lax.all_to_all(value, 'clip', 0, 0, axis_index_groups=groups, tiled=True)]
    ppermute x13, starting transfers between devices: 12.9 us -> 11.3 us  [swap(): return lax.ppermute(value, BOTH, pairs)]
    all_to_all x1, blocking collectives: 25.5 us -> 26.8 us  [exchange(): lax.all_to_all(value, 'clip', 0, 0, axis_index_groups=groups, tiled=True)]
    ppermute x13, waiting for transfers between devices: 3.76 us -> 4.9 us  [swap(): return lax.ppermute(value, BOTH, pairs)]
  transfers between devices with their start and end apart: 20 -> 20, of which waited for: 7 -> 7; matrix products, arithmetic and copies ran while one was open for 1% -> 0% of each run, Pallas kernels for 18% -> 19%
where the time goes in v4:
time: 100 us; the launch traced here: 99.9 us
  starting transfers between devices  31.7 us (32%)
  blocking collectives  26.8 us (27%)
  Pallas kernels  22.2 us (22%)
  waiting for transfers between devices  14.5 us (14%)
  between operations  2.57 us (3%)
  local copies, waits for them, and re-layouts  1.98 us (2%)
    all_to_all x1, blocking collectives, exchange(): lax.all_to_all(value, 'clip', 0, 0, axis_index_groups=groups, tiled=True)  26.8 us
    pallas_call x9, Pallas kernels, call(): pl.pallas_call(body, out_shape=[far[i](s, d) if i in far else jax.ShapeDt...  22.2 us
    all_to_all x1, starting transfers between devices, exchange(): lax.all_to_all(value, 'clip', 0, 0, axis_index_groups=groups, tiled=True)  11.7 us
    ppermute x13, starting transfers between devices, swap(): return lax.ppermute(value, BOTH, pairs)  11.3 us
    ppermute x6, waiting for transfers between devices, move(): return lax.ppermute(value, BOTH, pairs)  9.56 us
    ppermute x6, starting transfers between devices, move(): return lax.ppermute(value, BOTH, pairs)  8.71 us
    ppermute x13, waiting for transfers between devices, swap(): return lax.ppermute(value, BOTH, pairs)  4.9 us
  transfers between devices with their start and end apart: 20, of which 7 were waited for; matrix products, arithmetic and copies ran while one was open for 0% of the time, Pallas kernels for 19%

profile of v4, /device:TPU:8, one launch (start us, length us, event | category | flops | bytes accessed | tf_op | source)
XLA Modules:
  0.0 99.9 jit_solution(2199221566466594081)
XLA Ops:
  0.6 1.0 copy.9
  1.6 1.6 %collective-permute-start.1 = (bf16[4,32,1152]{2,1,0:T(8,128)(2,1)S(1)}, bf16[4,32,1152]{2,1,0:T(8,128)(2,1)S(1)}, u32[]{:S(2)}, u32[]{:S(2)}) collective-permute-start(bf16[4,32,1152]{2,1,0:T(8,128)(2,1)S(1)} %bitcast.7), channel_id=1, source_target_pairs={{0,2},{1,3},{2,0},{3,1},{4,6},{5,7},{6,4},{7,5},{8,10},{9,11},{10,... | collective-permute-start | bytes 884744 | tf_op jit(solution)/shard_map/ppermute | solution.py:36
  3.2 2.7 %collective-permute-start.3 = (bf16[4,32,1152]{2,1,0:T(8,128)(2,1)S(1)}, bf16[4,32,1152]{2,1,0:T(8,128)(2,1)S(1)}, u32[]{:S(2)}, u32[]{:S(2)}) collective-permute-start(bf16[4,32,1152]{2,1,0:T(8,128)(2,1)S(1)} %bitcast.8), channel_id=1, source_target_pairs={{0,128},{1,129},{2,130},{3,131},{4,132},{5,133},{6,134},{7,135},{8... | collective-permute-start | bytes 884744 | tf_op jit(solution)/shard_map/ppermute | solution.py:36
  5.9 0.5 collective-permute-start.5
  6.4 0.0 copy-start
  6.4 0.7 copy-done
  7.1 1.0 %shard_map.69 = bf16[32,8,1152]{2,1,0:T(8,128)(2,1)} custom-call(bf16[8,1152]{1,0:T(8,128)(2,1)S(1)} %copy-done), custom_call_target="tpu_custom_call" | custom-call | bytes 589824 | tf_op jit(solution)/shard_map/pallas_call | solution.py:72
  8.2 11.7 %all-to-all-start = ((bf16[32,8,1152]{2,1,0:T(8,128)(2,1)}), bf16[32,8,1152]{2,1,0:T(8,128)(2,1)S(1)}, u32[]{:S(2)}, u32[]{:S(2)}) async-start(bf16[32,8,1152]{2,1,0:T(8,128)(2,1)} %shard_map.69), calls=%async_computation | async-start | bytes 1179648 | tf_op jit(solution)/shard_map/all_to_all | solution.py:52
  19.9 0.1 collective-permute-start
  20.0 0.0 collective-permute-done.1.refs_0_
  20.0 0.5 collective-permute-start.2
  20.5 0.0 collective-permute-done.3.refs_1_
  20.5 0.1 collective-permute-start.4
  20.6 1.1 %collective-permute-done.5.refs_2_ = bf16[4,32,1152]{2,1,0:T(8,128)(2,1)S(1)} collective-permute-done((bf16[4,32,1152]{2,1,0:T(8,128)(2,1)S(1)}, bf16[4,32,1152]{2,1,0:T(8,128)(2,1)S(1)}, u32[]{:S(2)}, u32[]{:S(2)}) %collective-permute-start.5) | collective-permute-done | bytes 294944 | tf_op jit(solution)/shard_map/ppermute | solution.py:36
  21.7 0.0 collective-permute-start.6
  21.7 1.2 %collective-permute-start.7 = (s32[1,32]{1,0:T(1,128)}, s32[1,32]{1,0:T(1,128)S(1)}, u32[]{:S(2)}, u32[]{:S(2)}) collective-permute-start(s32[1,32]{1,0:T(1,128)} %bitcast.12), channel_id=1, source_target_pairs={{0,128},{1,129},{2,130},{3,131},{4,132},{5,133},{6,134},{7,135},{8... | collective-permute-start | bytes 392 | tf_op jit(solution)/shard_map/ppermute | solution.py:36
  22.8 2.9 %shard_map.67 = (bf16[3,4,32,1152]{3,2,1,0:T(8,128)(2,1)}, bf16[3,1152,768]{2,1,0:T(8,128)(2,1)S(1)}) custom-call(bf16[3,1152,1152]{2,1,0:T(8,128)(2,1)} %weights.1, bf16[4,32,1152]{2,1,0:T(8,128)(2,1)S(1)} %collective-permute-done.1.refs_0_, bf16[4,32,1152]{2,1,0:T(8,128)(2,1)S(1)} %collective-permute-done.3.refs_1_, ...), custom_call_target="tpu_custom_call" | custom-call | bytes 1769472 | tf_op jit(solution)/shard_map/pallas_call | solution.py:72
  25.8 1.1 %collective-permute-done.7.refs_8_ = s32[1,32]{1,0:T(1,128)S(1)} collective-permute-done((s32[1,32]{1,0:T(1,128)}, s32[1,32]{1,0:T(1,128)S(1)}, u32[]{:S(2)}, u32[]{:S(2)}) %collective-permute-start.7) | collective-permute-done | bytes 160 | tf_op jit(solution)/shard_map/ppermute | solution.py:36
  26.8 0.0 collective-permute-done.refs_1_
  26.8 0.0 collective-permute-done.2.refs_2_
  26.8 0.0 collective-permute-done.4.refs_3_
  26.9 0.0 collective-permute-done.6.refs_4_
  26.9 9.2 %shard_map.68 = (bf16[18,64,1152]{2,1,0:T(8,128)(2,1)S(1)}, f32[16,64,384]{2,1,0:T(8,128)}, f32[64,576]{1,0:T(8,128)}, s32[64,1]{1,0:T(8,128)}) custom-call(bf16[4,32,1152]{2,1,0:T(8,128)(2,1)S(1)} %bitcast.11, bf16[4,32,1152]{2,1,0:T(8,128)(2,1)S(1)} %collective-permute-done.refs_1_, bf16[4,32,1152]{2,1,0:T(8,128)(2,1)S(1)} %collective-permute-done.2.refs_2_, ...), custom_call_target="tpu_custom_call" | custom-call | flops 7134511104 | bytes 5308416 | tf_op jit(solution)/shard_map/pallas_call | solution.py:72
  36.1 0.0 all-to-all-done
  36.1 0.3 collective-permute-start.8
  36.4 1.6 %collective-permute-done.8.peer = f32[64,576]{1,0:T(8,128)S(1)} collective-permute-done((f32[64,576]{1,0:T(8,128)}, f32[64,576]{1,0:T(8,128)S(1)}, u32[]{:S(2)}, u32[]{:S(2)}) %collective-permute-start.8) | collective-permute-done | bytes 147488 | tf_op jit(solution)/shard_map/ppermute | solution.py:36
  38.0 2.0 %shard_map.70 = (f32[64,640]{1,0:T(8,128)S(1)}, f32[64,640]{1,0:T(8,128)S(1)}, f32[64,288]{1,0:T(8,128)S(1)}, f32[64,1]{1,0:T(8,128)S(1)}, bf16[64,1280]{1,0:T(8...) custom-call(f32[64,576]{1,0:T(8,128)} %get-tuple-element.42.pooled_in, ...), custom_call_target="tpu_custom_call" | custom-call | flops 113246208 | bytes 1769472 | tf_op jit(solution)/shard_map/pallas_call | solution.py:72
  40.0 0.2 collective-permute-start.9
  40.2 0.1 pad.3.clone
  40.3 1.2 %collective-permute-done.9 = f32[64,640]{1,0:T(8,128)S(1)} collective-permute-done((f32[64,640]{1,0:T(8,128)S(1)}, f32[64,640]{1,0:T(8,128)S(1)}, u32[]{:S(2)}, u32[]{:S(2)}) %collective-permute-start.9) | collective-permute-done | bytes 163872 | tf_op jit(solution)/shard_map/ppermute | solution.py:36
  41.5 0.1 slice.14
  41.6 0.1 slice.15
  41.7 0.1 maximum_maximum_fusion.s0
  41.8 1.4 %collective-permute-start.10 = (f32[64,384]{1,0:T(8,128)S(1)}, f32[64,384]{1,0:T(8,128)S(1)}, u32[]{:S(2)}, u32[]{:S(2)}) collective-permute-start(f32[64,384]{1,0:T(8,128)S(1)} %maximum_maximum_fusion.s0), channel_id=1, source_target_pairs={{0,128},{1,129},{2,130},{3,131},{4,132},{5,133},{6,134},{7,135},{8... | collective-permute-start | bytes 294920 | tf_op jit(solution)/shard_map/ppermute | solution.py:36
  43.2 1.7 %collective-permute-start.11 = (f32[64,384]{1,0:T(8,128)S(1)}, f32[64,384]{1,0:T(8,128)S(1)}, u32[]{:S(2)}, u32[]{:S(2)}) collective-permute-start(f32[64,384]{1,0:T(8,128)S(1)} %concatenate.8), channel_id=1, source_target_pairs={{0,2},{1,3},{2,0},{3,1},{4,6},{5,7},{6,4},{7,5},{8,10},{9,11},{10,... | collective-permute-start | bytes 294920 | tf_op jit(solution)/shard_map/ppermute | solution.py:36
  44.8 1.1 %collective-permute-start.12 = (f32[64,384]{1,0:T(8,128)S(1)}, f32[64,384]{1,0:T(8,128)S(1)}, u32[]{:S(2)}, u32[]{:S(2)}) collective-permute-start(f32[64,384]{1,0:T(8,128)S(1)} %concatenate.8), channel_id=1, source_target_pairs={{0,130},{1,131},{2,128},{3,129},{4,134},{5,135},{6,132},{7,133},{8... | collective-permute-start | bytes 294920 | tf_op jit(solution)/shard_map/ppermute | solution.py:36
  45.9 0.4 shard_map.71.x_ref
  46.4 1.7 %collective-permute-start.13 = (bf16[64,1280]{1,0:T(8,128)(2,1)S(1)}, bf16[64,1280]{1,0:T(8,128)(2,1)S(1)}, u32[]{:S(2)}, u32[]{:S(2)}) collective-permute-start(bf16[64,1280]{1,0:T(8,128)(2,1)S(1)} %get-tuple-element.61), channel_id=1, source_target_pairs={{0,32},{1,33},{2,34},{3,35},{4,36},{5,37},{6,38},{7,39},{8,40},{9,... | collective-permute-start | bytes 491528 | tf_op jit(solution)/shard_map/ppermute | solution.py:44
  48.0 2.3 %collective-permute-start.14 = (bf16[64,1280]{1,0:T(8,128)(2,1)S(1)}, bf16[64,1280]{1,0:T(8,128)(2,1)S(1)}, u32[]{:S(2)}, u32[]{:S(2)}) collective-permute-start(bf16[64,1280]{1,0:T(8,128)(2,1)S(1)} %get-tuple-element.62), channel_id=1, source_target_pairs={{0,64},{1,65},{2,66},{3,67},{4,68},{5,69},{6,70},{7,71},{8,72},{9,... | collective-permute-start | bytes 491528 | tf_op jit(solution)/shard_map/ppermute | solution.py:44
  50.3 0.0 collective-permute-done.10.s1
  50.3 1.1 %collective-permute-start.15 = (bf16[64,1280]{1,0:T(8,128)(2,1)S(1)}, bf16[64,1280]{1,0:T(8,128)(2,1)S(1)}, u32[]{:S(2)}, u32[]{:S(2)}) collective-permute-start(bf16[64,1280]{1,0:T(8,128)(2,1)S(1)} %get-tuple-element.63), channel_id=1, source_target_pairs={{0,96},{1,97},{2,98},{3,99},{4,100},{5,101},{6,102},{7,103},{8,104... | collective-permute-start | bytes 491528 | tf_op jit(solution)/shard_map/ppermute | solution.py:44
  51.4 0.0 collective-permute-done.11.s2
  51.4 0.0 collective-permute-done.12.s3
  51.4 4.6 %shard_map.72 = (bf16[144,896]{1,0:T(8,128)(2,1)S(1)}, bf16[144,896]{1,0:T(8,128)(2,1)S(1)}, bf16[144,896]{1,0:T(8,128)(2,1)S(1)}, bf16[144,896]{1,0:T(8,128)(2,1)S(1)}) custom-call(f32[64,384]{1,0:T(8,128)S(1)} %maximum_maximum_fusion.s0, f32[64,384]{1,0:T(8,128)S(1)} %collective-permute-done.10.s1, f32[64,384]{1,0:T(8,128)S(1)} %collective-permute-done.11.s2, ...), custom_call_target="tpu_custom_call" | custom-call | flops 1019215872 | bytes 2359296 | tf_op jit(solution)/shard_map/pallas_call | solution.py:72
  56.0 0.0 copy-start.1
  56.0 1.6 %collective-permute-start.17 = (bf16[144,896]{1,0:T(8,128)(2,1)S(1)}, bf16[144,896]{1,0:T(8,128)(2,1)S(1)}, u32[]{:S(2)}, u32[]{:S(2)}) collective-permute-start(bf16[144,896]{1,0:T(8,128)(2,1)S(1)} %get-tuple-element.66), channel_id=1, source_target_pairs={{0,64},{1,65},{2,66},{3,67},{4,68},{5,69},{6,70},{7,71},{8,72},{9,... | collective-permute-start | bytes 774152 | tf_op jit(solution)/shard_map/ppermute | solution.py:44
  57.6 1.5 %collective-permute-start.18 = (bf16[144,896]{1,0:T(8,128)(2,1)S(1)}, bf16[144,896]{1,0:T(8,128)(2,1)S(1)}, u32[]{:S(2)}, u32[]{:S(2)}) collective-permute-start(bf16[144,896]{1,0:T(8,128)(2,1)S(1)} %get-tuple-element.67), channel_id=1, source_target_pairs={{0,96},{1,97},{2,98},{3,99},{4,100},{5,101},{6,102},{7,103},{8,104... | collective-permute-start | bytes 774152 | tf_op jit(solution)/shard_map/ppermute | solution.py:44
  59.1 0.0 collective-permute-done.13.refs_1_
  59.1 0.0 collective-permute-done.14.refs_2_
  59.1 0.0 collective-permute-done.15.refs_3_
  59.1 0.6 collective-permute-start.16
  59.7 0.5 shard_map.73.refs_4_
  60.2 6.5 %collective-permute-done.17.refs_2_ = bf16[144,896]{1,0:T(8,128)(2,1)S(1)} collective-permute-done((bf16[144,896]{1,0:T(8,128)(2,1)S(1)}, bf16[144,896]{1,0:T(8,128)(2,1)S(1)}, u32[]{:S(2)}, u32[]{:S(2)}) %collective-permute-start.17) | collective-permute-done | bytes 258080 | tf_op jit(solution)/shard_map/ppermute | solution.py:44
  66.8 3.0 %collective-permute-done.18.refs_3_ = bf16[144,896]{1,0:T(8,128)(2,1)S(1)} collective-permute-done((bf16[144,896]{1,0:T(8,128)(2,1)S(1)}, bf16[144,896]{1,0:T(8,128)(2,1)S(1)}, u32[]{:S(2)}, u32[]{:S(2)}) %collective-permute-start.18) | collective-permute-done | bytes 258080 | tf_op jit(solution)/shard_map/ppermute | solution.py:44
  69.7 0.1 collective-permute-done.16.refs_1_
  69.8 0.4 shard_map.74
  70.2 26.8 %all_to_all.10.in_ref = bf16[8,16,2176]{2,1,0:T(8,128)(2,1)S(1)} all-to-all(bf16[8,16,2176]{2,1,0:T(8,128)(2,1)S(1)} %shard_map.74), channel_id=1, replica_groups={{0,4,8,12,16,20,24,28},{32,36,40,44,48,52,56,60},{64,68,72,76,80,84,88,..., dimensions={0} | all-to-all | bytes 1114112 | tf_op jit(solution)/shard_map/all_to_all | solution.py:52
  97.1 0.0 copy-done.1
  97.1 1.0 %shard_map.75 = (f32[3,18,288]{2,1,0:T(8,128)}, f32[1,1]{1,0:T(1,128)}, f32[8,1152]{1,0:T(8,128)}) custom-call(bf16[8,16,2176]{2,1,0:T(8,128)(2,1)S(1)} %all_to_all.10.in_ref, bf16[8,1152]{1,0:T(8,128)(2,1)S(1)} %copy-done.1), custom_call_target="tpu_custom_call" | custom-call | bytes 258048 | tf_op jit(solution)/shard_map/pallas_call | solution.py:72
  (4 shorter events, 0.0 us)
Async XLA Ops:
  1.6 18.4 %collective-permute-start.1 = (bf16[4,32,1152]{2,1,0:T(8,128)(2,1)S(1)}, bf16[4,32,1152]{2,1,0:T(8,128)(2,1)S(1)}, u32[]{:S(2)}, u32[]{:S(2)}) collective-permute-start(bf16[4,32,1152]{2,1,0:T(8,128)(2,1)S(1)} %bitcast.7), channel_id=1, source_target_pairs={{0,2},{1,3},{2,0},{3,1},{4,6},{5,7},{6,4},{7,5},{8,10},{9,11},{10,... | collective-permute-start | bytes 884744 | tf_op jit(solution)/shard_map/ppermute | solution.py:36
  3.2 17.3 %collective-permute-start.3 = (bf16[4,32,1152]{2,1,0:T(8,128)(2,1)S(1)}, bf16[4,32,1152]{2,1,0:T(8,128)(2,1)S(1)}, u32[]{:S(2)}, u32[]{:S(2)}) collective-permute-start(bf16[4,32,1152]{2,1,0:T(8,128)(2,1)S(1)} %bitcast.8), channel_id=1, source_target_pairs={{0,128},{1,129},{2,130},{3,131},{4,132},{5,133},{6,134},{7,135},{8... | collective-permute-start | bytes 884744 | tf_op jit(solution)/shard_map/ppermute | solution.py:36
  5.9 15.7 %collective-permute-start.5 = (bf16[4,32,1152]{2,1,0:T(8,128)(2,1)S(1)}, bf16[4,32,1152]{2,1,0:T(8,128)(2,1)S(1)}, u32[]{:S(2)}, u32[]{:S(2)}) collective-permute-start(bf16[4,32,1152]{2,1,0:T(8,128)(2,1)S(1)} %bitcast.9), channel_id=1, source_target_pairs={{0,130},{1,131},{2,128},{3,129},{4,134},{5,135},{6,132},{7,133},{8... | collective-permute-start | bytes 884744 | tf_op jit(solution)/shard_map/ppermute | solution.py:36
  6.4 0.7 copy-start
  8.2 27.9 %all-to-all-start = ((bf16[32,8,1152]{2,1,0:T(8,128)(2,1)}), bf16[32,8,1152]{2,1,0:T(8,128)(2,1)S(1)}, u32[]{:S(2)}, u32[]{:S(2)}) async-start(bf16[32,8,1152]{2,1,0:T(8,128)(2,1)} %shard_map.69), calls=%async_computation | async-start | bytes 1179648 | tf_op jit(solution)/shard_map/all_to_all | solution.py:52
  19.9 6.9 %collective-permute-start = (bf16[4,32,1152]{2,1,0:T(8,128)(2,1)S(1)}, bf16[4,32,1152]{2,1,0:T(8,128)(2,1)S(1)}, u32[]{:S(2)}, u32[]{:S(2)}) collective-permute-start(bf16[4,32,1152]{2,1,0:T(8,128)(2,1)S(1)} %bitcast.10), channel_id=1, source_target_pairs={{0,1},{1,0},{2,3},{3,2},{4,5},{5,4},{6,7},{7,6},{8,9},{9,8},{10,11... | collective-permute-start | bytes 884744 | tf_op jit(solution)/shard_map/ppermute | solution.py:36
  20.0 6.8 %collective-permute-start.2 = (bf16[4,32,1152]{2,1,0:T(8,128)(2,1)S(1)}, bf16[4,32,1152]{2,1,0:T(8,128)(2,1)S(1)}, u32[]{:S(2)}, u32[]{:S(2)}) collective-permute-start(bf16[4,32,1152]{2,1,0:T(8,128)(2,1)S(1)} %collective-permute-done.1.refs_0_), channel_id=1, source_target_pairs={{0,1},{1,0},{2,3},{3,2},{4,5},{5,4},{6,7},{7,6},{8,9},{9,8},{10,11... | collective-permute-start | bytes 884744 | tf_op jit(solution)/shard_map/ppermute | solution.py:36
  20.5 6.4 %collective-permute-start.4 = (bf16[4,32,1152]{2,1,0:T(8,128)(2,1)S(1)}, bf16[4,32,1152]{2,1,0:T(8,128)(2,1)S(1)}, u32[]{:S(2)}, u32[]{:S(2)}) collective-permute-start(bf16[4,32,1152]{2,1,0:T(8,128)(2,1)S(1)} %collective-permute-done.3.refs_1_), channel_id=1, source_target_pairs={{0,1},{1,0},{2,3},{3,2},{4,5},{5,4},{6,7},{7,6},{8,9},{9,8},{10,11... | collective-permute-start | bytes 884744 | tf_op jit(solution)/shard_map/ppermute | solution.py:36
  21.7 5.2 %collective-permute-start.6 = (bf16[4,32,1152]{2,1,0:T(8,128)(2,1)S(1)}, bf16[4,32,1152]{2,1,0:T(8,128)(2,1)S(1)}, u32[]{:S(2)}, u32[]{:S(2)}) collective-permute-start(bf16[4,32,1152]{2,1,0:T(8,128)(2,1)S(1)} %collective-permute-done.5.refs_2_), channel_id=1, source_target_pairs={{0,1},{1,0},{2,3},{3,2},{4,5},{5,4},{6,7},{7,6},{8,9},{9,8},{10,11... | collective-permute-start | bytes 884744 | tf_op jit(solution)/shard_map/ppermute | solution.py:36
  21.7 5.2 %collective-permute-start.7 = (s32[1,32]{1,0:T(1,128)}, s32[1,32]{1,0:T(1,128)S(1)}, u32[]{:S(2)}, u32[]{:S(2)}) collective-permute-start(s32[1,32]{1,0:T(1,128)} %bitcast.12), channel_id=1, source_target_pairs={{0,128},{1,129},{2,130},{3,131},{4,132},{5,133},{6,134},{7,135},{8... | collective-permute-start | bytes 392 | tf_op jit(solution)/shard_map/ppermute | solution.py:36
  36.1 1.9 %collective-permute-start.8 = (f32[64,576]{1,0:T(8,128)}, f32[64,576]{1,0:T(8,128)S(1)}, u32[]{:S(2)}, u32[]{:S(2)}) collective-permute-start(f32[64,576]{1,0:T(8,128)} %get-tuple-element.42.pooled_in), channel_id=1, source_target_pairs={{0,1},{1,0},{2,3},{3,2},{4,5},{5,4},{6,7},{7,6},{8,9},{9,8},{10,11... | collective-permute-start | bytes 442376 | tf_op jit(solution)/shard_map/ppermute | solution.py:36
  40.0 1.5 %collective-permute-start.9 = (f32[64,640]{1,0:T(8,128)S(1)}, f32[64,640]{1,0:T(8,128)S(1)}, u32[]{:S(2)}, u32[]{:S(2)}) collective-permute-start(f32[64,640]{1,0:T(8,128)S(1)} %get-tuple-element.46), channel_id=1, source_target_pairs={{0,1},{1,0},{2,3},{3,2},{4,5},{5,4},{6,7},{7,6},{8,9},{9,8},{10,11... | collective-permute-start | bytes 491528 | tf_op jit(solution)/shard_map/ppermute | solution.py:36
  41.8 8.5 %collective-permute-start.10 = (f32[64,384]{1,0:T(8,128)S(1)}, f32[64,384]{1,0:T(8,128)S(1)}, u32[]{:S(2)}, u32[]{:S(2)}) collective-permute-start(f32[64,384]{1,0:T(8,128)S(1)} %maximum_maximum_fusion.s0), channel_id=1, source_target_pairs={{0,128},{1,129},{2,130},{3,131},{4,132},{5,133},{6,134},{7,135},{8... | collective-permute-start | bytes 294920 | tf_op jit(solution)/shard_map/ppermute | solution.py:36
  43.2 8.2 %collective-permute-start.11 = (f32[64,384]{1,0:T(8,128)S(1)}, f32[64,384]{1,0:T(8,128)S(1)}, u32[]{:S(2)}, u32[]{:S(2)}) collective-permute-start(f32[64,384]{1,0:T(8,128)S(1)} %concatenate.8), channel_id=1, source_target_pairs={{0,2},{1,3},{2,0},{3,1},{4,6},{5,7},{6,4},{7,5},{8,10},{9,11},{10,... | collective-permute-start | bytes 294920 | tf_op jit(solution)/shard_map/ppermute | solution.py:36
  44.8 6.6 %collective-permute-start.12 = (f32[64,384]{1,0:T(8,128)S(1)}, f32[64,384]{1,0:T(8,128)S(1)}, u32[]{:S(2)}, u32[]{:S(2)}) collective-permute-start(f32[64,384]{1,0:T(8,128)S(1)} %concatenate.8), channel_id=1, source_target_pairs={{0,130},{1,131},{2,128},{3,129},{4,134},{5,135},{6,132},{7,133},{8... | collective-permute-start | bytes 294920 | tf_op jit(solution)/shard_map/ppermute | solution.py:36
  46.4 12.8 %collective-permute-start.13 = (bf16[64,1280]{1,0:T(8,128)(2,1)S(1)}, bf16[64,1280]{1,0:T(8,128)(2,1)S(1)}, u32[]{:S(2)}, u32[]{:S(2)}) collective-permute-start(bf16[64,1280]{1,0:T(8,128)(2,1)S(1)} %get-tuple-element.61), channel_id=1, source_target_pairs={{0,32},{1,33},{2,34},{3,35},{4,36},{5,37},{6,38},{7,39},{8,40},{9,... | collective-permute-start | bytes 491528 | tf_op jit(solution)/shard_map/ppermute | solution.py:44
  48.0 11.1 %collective-permute-start.14 = (bf16[64,1280]{1,0:T(8,128)(2,1)S(1)}, bf16[64,1280]{1,0:T(8,128)(2,1)S(1)}, u32[]{:S(2)}, u32[]{:S(2)}) collective-permute-start(bf16[64,1280]{1,0:T(8,128)(2,1)S(1)} %get-tuple-element.62), channel_id=1, source_target_pairs={{0,64},{1,65},{2,66},{3,67},{4,68},{5,69},{6,70},{7,71},{8,72},{9,... | collective-permute-start | bytes 491528 | tf_op jit(solution)/shard_map/ppermute | solution.py:44
  50.3 8.8 %collective-permute-start.15 = (bf16[64,1280]{1,0:T(8,128)(2,1)S(1)}, bf16[64,1280]{1,0:T(8,128)(2,1)S(1)}, u32[]{:S(2)}, u32[]{:S(2)}) collective-permute-start(bf16[64,1280]{1,0:T(8,128)(2,1)S(1)} %get-tuple-element.63), channel_id=1, source_target_pairs={{0,96},{1,97},{2,98},{3,99},{4,100},{5,101},{6,102},{7,103},{8,104... | collective-permute-start | bytes 491528 | tf_op jit(solution)/shard_map/ppermute | solution.py:44
  56.0 41.1 %copy-start.1 = (bf16[8,1152]{1,0:T(8,128)(2,1)S(1)}, bf16[8,1152]{1,0:T(8,128)(2,1)}, u32[]{:S(2)}) copy-start(bf16[8,1152]{1,0:T(8,128)(2,1)} %captions.3) | copy-start | bytes 55300
  56.0 10.7 %collective-permute-start.17 = (bf16[144,896]{1,0:T(8,128)(2,1)S(1)}, bf16[144,896]{1,0:T(8,128)(2,1)S(1)}, u32[]{:S(2)}, u32[]{:S(2)}) collective-permute-start(bf16[144,896]{1,0:T(8,128)(2,1)S(1)} %get-tuple-element.66), channel_id=1, source_target_pairs={{0,64},{1,65},{2,66},{3,67},{4,68},{5,69},{6,70},{7,71},{8,72},{9,... | collective-permute-start | bytes 774152 | tf_op jit(solution)/shard_map/ppermute | solution.py:44
  57.6 12.1 %collective-permute-start.18 = (bf16[144,896]{1,0:T(8,128)(2,1)S(1)}, bf16[144,896]{1,0:T(8,128)(2,1)S(1)}, u32[]{:S(2)}, u32[]{:S(2)}) collective-permute-start(bf16[144,896]{1,0:T(8,128)(2,1)S(1)} %get-tuple-element.67), channel_id=1, source_target_pairs={{0,96},{1,97},{2,98},{3,99},{4,100},{5,101},{6,102},{7,103},{8,104... | collective-permute-start | bytes 774152 | tf_op jit(solution)/shard_map/ppermute | solution.py:44
  59.1 10.6 %collective-permute-start.16 = (bf16[144,896]{1,0:T(8,128)(2,1)S(1)}, bf16[144,896]{1,0:T(8,128)(2,1)S(1)}, u32[]{:S(2)}, u32[]{:S(2)}) collective-permute-start(bf16[144,896]{1,0:T(8,128)(2,1)S(1)} %get-tuple-element.65), channel_id=1, source_target_pairs={{0,32},{1,33},{2,34},{3,35},{4,36},{5,37},{6,38},{7,39},{8,40},{9,... | collective-permute-start | bytes 774152 | tf_op jit(solution)/shard_map/ppermute | solution.py:44

commit v5 on v4

--- a/solution.py
+++ b/solution.py
@@ -61,7 +61,7 @@
     return lax.axis_index("frame"), clip // (Y * Z), clip // Z % Y, clip % Z
 
 
-def call(body, mib, out_shapes, scratch, flops, moved, *operands, loose={}, far={}):
+def call(body, mib, out_shapes, scratch, flops, moved, *operands, loose={}, far={}, same={}):
     specs = []
     operands = list(operands)
     for i, o in enumerate(operands):
@@ -77,40 +77,25 @@
         in_specs=specs,
         out_specs=[pl.BlockSpec(memory_space=far.get(i, pltpu.VMEM)) for i in range(len(out_shapes))],
         scratch_shapes=scratch,
+        input_output_aliases=same,
         cost_estimate=pl.CostEstimate(flops=flops, bytes_accessed=moved, transcendentals=0),
         compiler_params=pltpu.CompilerParams(vmem_limit_bytes=mib * 2**20),
     )(*operands)
 
 
 def conv_kernel(cols, *refs):
-    (mine, *near, held), (w_ref, positive, across), rest = (
-        refs[:6],
-        refs[6:9],
-        refs[9:],
-    )
+    near, (_, w_ref, positive, across), rest = refs[:4], refs[4:8], refs[8:]
     x_ref, out_ref, mean_ref, wanted_ref, slope_ref, sum_ref, part_ref, pooled_ref, id_ref, pos_ref, x_sem, o_sem = rest
-    far = [mine] + [held.at[i] for i in range(held.shape[0])]
-    pieces = [far[0], near[0], far[1], near[1], far[2], near[2], far[3], near[3]]
     frame, half, _, _ = whereabouts()
-    steps, block, width = mine.shape
+    steps, block, width = near[0].shape
     group = pooled_ref.shape[0]
     wide = slope_ref.shape[2]
-    copies = []
-    for i, piece in enumerate(pieces):
-        j, side = i % 4, i // 4
-        first = (frame ^ j) * steps + 1
-        start = pl.multiple_of((half ^ side) * block, block)
-        copies.append(
-            pltpu.make_async_copy(
-                piece, x_ref.at[pl.ds(first, steps), pl.ds(start, block), :], x_sem.at[i]
-            )
-        )
+    order = ((1, 0), (CORE ^ 1, 0), (1, 1), (CORE ^ 1, 1))
+    copies = placed(dict(zip(order, near)), x_ref, x_sem)
     load = pltpu.make_async_copy(positive, pos_ref, o_sem.at[FRAMES // steps + 1])
     load.start()
     for copy in copies:
         copy.start()
-    x_ref[0] = jnp.zeros((group, width), BF16)
-    x_ref[FRAMES + 1] = jnp.zeros((group, width), BF16)
     sum_ref[...] = jnp.zeros_like(sum_ref)
     part_ref[...] = jnp.zeros_like(part_ref)
     load.wait()
@@ -387,10 +372,26 @@
     out_ref[...] = jnp.broadcast_to(low[None], out_ref.shape)
 
 
+def placed(pieces, x_ref, sem):
+    frame, half, _, _ = whereabouts()
+    copies = []
+    for (j, side), piece in pieces.items():
+        steps, block, _ = piece.shape
+        first = (frame ^ j) * steps + 1
+        start = pl.multiple_of((half ^ side) * block, block)
+        copies.append(
+            pltpu.make_async_copy(
+                piece, x_ref.at[pl.ds(first, steps), pl.ds(start, block), :], sem.at[len(copies)]
+            )
+        )
+    return copies
+
+
 def stage_kernel(wide, weights, *refs):
-    ins, (out_ref, w_ref, sem, w_sem) = refs[:-4], refs[-4:]
+    (mine, *far), (x_ref, w_ref, sem, w_sem) = refs[:-4], refs[-4:]
     frame = whereabouts()[0]
-    copies = [pltpu.make_async_copy(piece, out_ref.at[i], sem.at[i]) for i, piece in enumerate(ins)]
+    group, width = x_ref.shape[1:]
+    copies = []
     for k in range(3):
         for i in range(XL):
             start = pl.multiple_of((frame ^ (i * CORE)) * (wide - 128), 128)
@@ -399,8 +400,11 @@
                     weights.at[k, :, pl.ds(start, wide)], w_ref.at[k, :, pl.ds(i * wide, wide)], w_sem.at[k, i]
                 )
             )
+    copies += placed({(0, 0): mine, (CORE, 0): far[0], (0, 1): far[1], (CORE, 1): far[2]}, x_ref, sem)
     for copy in copies:
         copy.start()
+    x_ref[0] = jnp.zeros((group, width), BF16)
+    x_ref[FRAMES + 1] = jnp.zeros((group, width), BF16)
     for copy in copies:
         copy.wait()
 
@@ -428,19 +432,18 @@
     far = [swap(mine, 0, 1, 0), swap(mine, 1, 0, 0), swap(mine, 1, 1, 0)]
     near = [first] + [swap(part, 0, 0, 1) for part in far]
     wide = cols + (XL * CORE - 1) * (cols % 128)
-    held, weights = call(
+    x, weights = call(
         functools.partial(stage_kernel, wide),
         2,
-        [((3,) + mine.shape, BF16), ((3, width, XL * wide), BF16)],
-        [pltpu.SemaphoreType.DMA((3,)), pltpu.SemaphoreType.DMA((3, XL))],
+        [((FRAMES + 2, group, width), BF16), ((3, width, XL * wide), BF16)],
+        [pltpu.SemaphoreType.DMA((4,)), pltpu.SemaphoreType.DMA((3, XL))],
         0,
         mine.size * 12,
         conv_weight,
+        mine,
         *far,
-        loose={0: pltpu.HBM} | {i: pl.ANY for i in range(1, 4)},
-        far={0: pltpu.HBM},
-    )
-    pieces = [mine, *near, held]
+        loose={0: pltpu.HBM} | {i: pl.ANY for i in range(1, 5)},
+    )
 
     piece = exchange(spread, YZ_GROUPS).reshape(Y * Z * cap_dev, width)
     count = piece.shape[0]
@@ -456,16 +459,18 @@
             pltpu.VMEM((group, XL * cols), F32),
             pltpu.VMEM((group, 1), jnp.int32),
             pltpu.VMEM(positive.shape, jnp.int32),
-            pltpu.SemaphoreType.DMA((8,)),
+            pltpu.SemaphoreType.DMA((4,)),
             pltpu.SemaphoreType.DMA((FRAMES // fr_dev + 2,)),
         ],
         int(3.5 * rows * 3 * width * 2 * cols),
         3 * width * 2 * wide * 2,
-        *pieces,
+        *near,
+        x,
         weights,
         positive,
         across,
-        loose={i: pl.ANY for i in range(5)} | {5: pltpu.HBM, 7: pltpu.HBM},
+        same={4: 0},
+        loose={i: pl.ANY for i in range(4)} | {6: pltpu.HBM},
         far={1: pltpu.HBM, 2: pltpu.HBM, 3: pltpu.HBM},
     )
     pooled, piece = lax.optimization_barrier((pooled, piece))

time: 100 us -> 99.7 us (level)
  transfers between devices with their start and end apart: 20 -> 20, of which waited for: 7 -> 8; matrix products, arithmetic and copies ran while one was open for 0% -> 0% of each run, Pallas kernels for 19% -> 18%
where the time goes in v5:
time: 99.7 us; the launch traced here: 99.3 us
  starting transfers between devices  31.8 us (32%)
  blocking collectives  26.8 us (27%)
  Pallas kernels  21.5 us (22%)
  waiting for transfers between devices  14.5 us (15%)
  between operations  2.57 us (3%)
  local copies, waits for them, and re-layouts  1.98 us (2%)
    all_to_all x1, blocking collectives, exchange(): lax.all_to_all(value, 'clip', 0, 0, axis_index_groups=groups, tiled=True)  26.8 us
    pallas_call x9, Pallas kernels, call(): pl.pallas_call(body, out_shape=[far[i](s, d) if i in far else jax.ShapeDt...  21.5 us
    all_to_all x1, starting transfers between devices, exchange(): lax.all_to_all(value, 'clip', 0, 0, axis_index_groups=groups, tiled=True)  11.7 us
    ppermute x13, starting transfers between devices, swap(): return lax.ppermute(value, BOTH, pairs)  11.1 us
    ppermute x6, waiting for transfers between devices, move(): return lax.ppermute(value, BOTH, pairs)  9.23 us
    ppermute x6, starting transfers between devices, move(): return lax.ppermute(value, BOTH, pairs)  9.06 us
    ppermute x13, waiting for transfers between devices, swap(): return lax.ppermute(value, BOTH, pairs)  5.16 us
  transfers between devices with their start and end apart: 20, of which 8 were waited for; matrix products, arithmetic and copies ran while one was open for 0% of the time, Pallas kernels for 18%

profile of v5, /device:TPU:8, one launch (start us, length us, event | category | flops | bytes accessed | tf_op | source)
XLA Modules:
  0.0 99.3 jit_solution(15576780890543311929)
XLA Ops:
  0.6 1.0 %copy.10 = bf16[32,4,1152]{2,0,1:T(8,128)(2,1)S(1)} copy(bf16[32,4,1152]{2,1,0:T(4,128)(2,1)} %param.4) | data formatting | bytes 589824 | tf_op args[0]
  1.6 1.6 %collective-permute-start.1 = (bf16[4,32,1152]{2,1,0:T(8,128)(2,1)S(1)}, bf16[4,32,1152]{2,1,0:T(8,128)(2,1)}, u32[]{:S(2)}, u32[]{:S(2)}) collective-permute-start(bf16[4,32,1152]{2,1,0:T(8,128)(2,1)S(1)} %bitcast.7), channel_id=1, source_target_pairs={{0,2},{1,3},{2,0},{3,1},{4,6},{5,7},{6,4},{7,5},{8,10},{9,11},{10,... | collective-permute-start | bytes 884744 | tf_op jit(solution)/shard_map/ppermute | solution.py:36
  3.2 2.7 %collective-permute-start.3 = (bf16[4,32,1152]{2,1,0:T(8,128)(2,1)S(1)}, bf16[4,32,1152]{2,1,0:T(8,128)(2,1)}, u32[]{:S(2)}, u32[]{:S(2)}) collective-permute-start(bf16[4,32,1152]{2,1,0:T(8,128)(2,1)S(1)} %bitcast.8), channel_id=1, source_target_pairs={{0,128},{1,129},{2,130},{3,131},{4,132},{5,133},{6,134},{7,135},{8... | collective-permute-start | bytes 884744 | tf_op jit(solution)/shard_map/ppermute | solution.py:36
  5.9 0.5 collective-permute-start.5
  6.4 0.0 copy-start
  6.4 0.7 copy-done
  7.1 1.1 %shard_map.69 = bf16[32,8,1152]{2,1,0:T(8,128)(2,1)} custom-call(bf16[8,1152]{1,0:T(8,128)(2,1)S(1)} %copy-done), custom_call_target="tpu_custom_call" | custom-call | bytes 589824 | tf_op jit(solution)/shard_map/pallas_call | solution.py:72
  8.2 11.7 %all-to-all-start = ((bf16[32,8,1152]{2,1,0:T(8,128)(2,1)}), bf16[32,8,1152]{2,1,0:T(8,128)(2,1)S(1)}, u32[]{:S(2)}, u32[]{:S(2)}) async-start(bf16[32,8,1152]{2,1,0:T(8,128)(2,1)} %shard_map.69), calls=%async_computation | async-start | bytes 1179648 | tf_op jit(solution)/shard_map/all_to_all | solution.py:52
  19.9 0.1 collective-permute-start
  20.0 0.0 collective-permute-done.1.refs_1_
  20.0 0.5 collective-permute-start.2
  20.5 0.0 collective-permute-done.3.refs_2_
  20.5 0.1 collective-permute-start.4
  20.6 1.1 %collective-permute-done.5.refs_3_ = bf16[4,32,1152]{2,1,0:T(8,128)(2,1)} collective-permute-done((bf16[4,32,1152]{2,1,0:T(8,128)(2,1)S(1)}, bf16[4,32,1152]{2,1,0:T(8,128)(2,1)}, u32[]{:S(2)}, u32[]{:S(2)}) %collective-permute-start.5) | collective-permute-done | bytes 294944 | tf_op jit(solution)/shard_map/ppermute | solution.py:36
  21.8 0.0 collective-permute-start.6
  21.8 1.1 %collective-permute-start.7 = (s32[1,32]{1,0:T(1,128)}, s32[1,32]{1,0:T(1,128)S(1)}, u32[]{:S(2)}, u32[]{:S(2)}) collective-permute-start(s32[1,32]{1,0:T(1,128)} %bitcast.12), channel_id=1, source_target_pairs={{0,128},{1,129},{2,130},{3,131},{4,132},{5,133},{6,134},{7,135},{8... | collective-permute-start | bytes 392 | tf_op jit(solution)/shard_map/ppermute | solution.py:36
  22.8 2.9 %shard_map.67 = (bf16[18,64,1152]{2,1,0:T(8,128)(2,1)S(1)}, bf16[3,1152,768]{2,1,0:T(8,128)(2,1)S(1)}) custom-call(bf16[3,1152,1152]{2,1,0:T(8,128)(2,1)} %weights.1, bf16[4,32,1152]{2,1,0:T(8,128)(2,1)S(1)} %bitcast.11, bf16[4,32,1152]{2,1,0:T(8,128)(2,1)} %collective-permute-done.1.refs_1_, bf16[4,32,1152]{2,1,0:T(8,128)(2,1)} %collective-permute-done.3.refs_2_, ...), custom_call_target="tpu_custom_call" | custom-call | bytes 1769472 | tf_op jit(solution)/shard_map/pallas_call | solution.py:72
  25.7 1.2 %collective-permute-done.7.refs_7_ = s32[1,32]{1,0:T(1,128)S(1)} collective-permute-done((s32[1,32]{1,0:T(1,128)}, s32[1,32]{1,0:T(1,128)S(1)}, u32[]{:S(2)}, u32[]{:S(2)}) %collective-permute-start.7) | collective-permute-done | bytes 160 | tf_op jit(solution)/shard_map/ppermute | solution.py:36
  26.9 0.0 collective-permute-done.refs_0_
  26.9 0.0 collective-permute-done.2.refs_1_
  26.9 0.0 collective-permute-done.4.refs_2_
  27.0 0.0 collective-permute-done.6.refs_3_
  27.0 8.6 %shard_map.68 = (bf16[18,64,1152]{2,1,0:T(8,128)(2,1)S(1)}, f32[16,64,384]{2,1,0:T(8,128)}, f32[64,576]{1,0:T(8,128)}, s32[64,1]{1,0:T(8,128)}) custom-call(bf16[4,32,1152]{2,1,0:T(8,128)(2,1)S(1)} %collective-permute-done.refs_0_, bf16[4,32,1152]{2,1,0:T(8,128)(2,1)S(1)} %collective-permute-done.2.refs_1_, ...), custom_call_target="tpu_custom_call", output_to_operand_aliasing={{0}: (4, {})} | custom-call | flops 7134511104 | bytes 5308416 | tf_op jit(solution)/shard_map/pallas_call | solution.py:72
  35.5 0.1 all-to-all-done
  35.7 0.2 collective-permute-start.8
  35.8 1.6 %collective-permute-done.8.peer = f32[64,576]{1,0:T(8,128)S(1)} collective-permute-done((f32[64,576]{1,0:T(8,128)}, f32[64,576]{1,0:T(8,128)S(1)}, u32[]{:S(2)}, u32[]{:S(2)}) %collective-permute-start.8) | collective-permute-done | bytes 147488 | tf_op jit(solution)/shard_map/ppermute | solution.py:36
  37.4 2.0 %shard_map.70 = (f32[64,640]{1,0:T(8,128)S(1)}, f32[64,640]{1,0:T(8,128)S(1)}, f32[64,288]{1,0:T(8,128)S(1)}, f32[64,1]{1,0:T(8,128)S(1)}, bf16[64,1280]{1,0:T(8...) custom-call(f32[64,576]{1,0:T(8,128)} %get-tuple-element.42.pooled_in, ...), custom_call_target="tpu_custom_call" | custom-call | flops 113246208 | bytes 1769472 | tf_op jit(solution)/shard_map/pallas_call | solution.py:72
  39.5 0.2 collective-permute-start.9
  39.7 0.1 pad.3.clone
  39.8 1.2 %collective-permute-done.9 = f32[64,640]{1,0:T(8,128)S(1)} collective-permute-done((f32[64,640]{1,0:T(8,128)S(1)}, f32[64,640]{1,0:T(8,128)S(1)}, u32[]{:S(2)}, u32[]{:S(2)}) %collective-permute-start.9) | collective-permute-done | bytes 163872 | tf_op jit(solution)/shard_map/ppermute | solution.py:36
  41.0 0.1 slice.14
  41.1 0.1 slice.15
  41.2 0.1 maximum_maximum_fusion.s0
  41.3 1.7 %collective-permute-start.10 = (f32[64,384]{1,0:T(8,128)S(1)}, f32[64,384]{1,0:T(8,128)S(1)}, u32[]{:S(2)}, u32[]{:S(2)}) collective-permute-start(f32[64,384]{1,0:T(8,128)S(1)} %maximum_maximum_fusion.s0), channel_id=1, source_target_pairs={{0,128},{1,129},{2,130},{3,131},{4,132},{5,133},{6,134},{7,135},{8... | collective-permute-start | bytes 294920 | tf_op jit(solution)/shard_map/ppermute | solution.py:36
  42.9 1.8 %collective-permute-start.11 = (f32[64,384]{1,0:T(8,128)S(1)}, f32[64,384]{1,0:T(8,128)S(1)}, u32[]{:S(2)}, u32[]{:S(2)}) collective-permute-start(f32[64,384]{1,0:T(8,128)S(1)} %concatenate.8), channel_id=1, source_target_pairs={{0,2},{1,3},{2,0},{3,1},{4,6},{5,7},{6,4},{7,5},{8,10},{9,11},{10,... | collective-permute-start | bytes 294920 | tf_op jit(solution)/shard_map/ppermute | solution.py:36
  44.7 0.6 collective-permute-start.12
  45.4 0.4 shard_map.71.x_ref
  45.8 1.6 %collective-permute-start.13 = (bf16[64,1280]{1,0:T(8,128)(2,1)S(1)}, bf16[64,1280]{1,0:T(8,128)(2,1)S(1)}, u32[]{:S(2)}, u32[]{:S(2)}) collective-permute-start(bf16[64,1280]{1,0:T(8,128)(2,1)S(1)} %get-tuple-element.61), channel_id=1, source_target_pairs={{0,32},{1,33},{2,34},{3,35},{4,36},{5,37},{6,38},{7,39},{8,40},{9,... | collective-permute-start | bytes 491528 | tf_op jit(solution)/shard_map/ppermute | solution.py:44
  47.5 2.8 %collective-permute-start.14 = (bf16[64,1280]{1,0:T(8,128)(2,1)S(1)}, bf16[64,1280]{1,0:T(8,128)(2,1)S(1)}, u32[]{:S(2)}, u32[]{:S(2)}) collective-permute-start(bf16[64,1280]{1,0:T(8,128)(2,1)S(1)} %get-tuple-element.62), channel_id=1, source_target_pairs={{0,64},{1,65},{2,66},{3,67},{4,68},{5,69},{6,70},{7,71},{8,72},{9,... | collective-permute-start | bytes 491528 | tf_op jit(solution)/shard_map/ppermute | solution.py:44
  50.3 0.0 collective-permute-done.10.s1
  50.3 0.5 collective-permute-start.15
  50.8 0.0 collective-permute-done.11.s2
  50.8 0.0 collective-permute-done.12.s3
  50.8 4.6 %shard_map.72 = (bf16[144,896]{1,0:T(8,128)(2,1)S(1)}, bf16[144,896]{1,0:T(8,128)(2,1)S(1)}, bf16[144,896]{1,0:T(8,128)(2,1)S(1)}, bf16[144,896]{1,0:T(8,128)(2,1)S(1)}) custom-call(f32[64,384]{1,0:T(8,128)S(1)} %maximum_maximum_fusion.s0, f32[64,384]{1,0:T(8,128)S(1)} %collective-permute-done.10.s1, f32[64,384]{1,0:T(8,128)S(1)} %collective-permute-done.11.s2, ...), custom_call_target="tpu_custom_call" | custom-call | flops 1019215872 | bytes 2359296 | tf_op jit(solution)/shard_map/pallas_call | solution.py:72
  55.4 0.0 copy-start.1
  55.5 2.0 %collective-permute-start.17 = (bf16[144,896]{1,0:T(8,128)(2,1)S(1)}, bf16[144,896]{1,0:T(8,128)(2,1)S(1)}, u32[]{:S(2)}, u32[]{:S(2)}) collective-permute-start(bf16[144,896]{1,0:T(8,128)(2,1)S(1)} %get-tuple-element.66), channel_id=1, source_target_pairs={{0,64},{1,65},{2,66},{3,67},{4,68},{5,69},{6,70},{7,71},{8,72},{9,... | collective-permute-start | bytes 774152 | tf_op jit(solution)/shard_map/ppermute | solution.py:44
  57.4 1.7 %collective-permute-start.18 = (bf16[144,896]{1,0:T(8,128)(2,1)S(1)}, bf16[144,896]{1,0:T(8,128)(2,1)S(1)}, u32[]{:S(2)}, u32[]{:S(2)}) collective-permute-start(bf16[144,896]{1,0:T(8,128)(2,1)S(1)} %get-tuple-element.67), channel_id=1, source_target_pairs={{0,96},{1,97},{2,98},{3,99},{4,100},{5,101},{6,102},{7,103},{8,104... | collective-permute-start | bytes 774152 | tf_op jit(solution)/shard_map/ppermute | solution.py:44
  59.1 0.0 collective-permute-done.13.refs_1_
  59.1 0.0 collective-permute-done.14.refs_2_
  59.1 0.0 collective-permute-done.15.refs_3_
  59.1 0.4 collective-permute-start.16
  59.5 0.5 shard_map.73.refs_4_
  60.0 6.2 %collective-permute-done.17.refs_2_ = bf16[144,896]{1,0:T(8,128)(2,1)S(1)} collective-permute-done((bf16[144,896]{1,0:T(8,128)(2,1)S(1)}, bf16[144,896]{1,0:T(8,128)(2,1)S(1)}, u32[]{:S(2)}, u32[]{:S(2)}) %collective-permute-start.17) | collective-permute-done | bytes 258080 | tf_op jit(solution)/shard_map/ppermute | solution.py:44
  66.2 3.0 %collective-permute-done.18.refs_3_ = bf16[144,896]{1,0:T(8,128)(2,1)S(1)} collective-permute-done((bf16[144,896]{1,0:T(8,128)(2,1)S(1)}, bf16[144,896]{1,0:T(8,128)(2,1)S(1)}, u32[]{:S(2)}, u32[]{:S(2)}) %collective-permute-start.18) | collective-permute-done | bytes 258080 | tf_op jit(solution)/shard_map/ppermute | solution.py:44
  69.2 0.1 collective-permute-done.16.refs_1_
  69.2 0.4 shard_map.74
  69.7 26.8 %all_to_all.10.in_ref = bf16[8,16,2176]{2,1,0:T(8,128)(2,1)S(1)} all-to-all(bf16[8,16,2176]{2,1,0:T(8,128)(2,1)S(1)} %shard_map.74), channel_id=1, replica_groups={{0,4,8,12,16,20,24,28},{32,36,40,44,48,52,56,60},{64,68,72,76,80,84,88,..., dimensions={0} | all-to-all | bytes 1114112 | tf_op jit(solution)/shard_map/all_to_all | solution.py:52
  96.5 0.0 copy-done.1
  96.5 1.0 %shard_map.75 = (f32[3,18,288]{2,1,0:T(8,128)}, f32[1,1]{1,0:T(1,128)}, f32[8,1152]{1,0:T(8,128)}) custom-call(bf16[8,16,2176]{2,1,0:T(8,128)(2,1)S(1)} %all_to_all.10.in_ref, bf16[8,1152]{1,0:T(8,128)(2,1)S(1)} %copy-done.1), custom_call_target="tpu_custom_call" | custom-call | bytes 258048 | tf_op jit(solution)/shard_map/pallas_call | solution.py:72
  (4 shorter events, 0.0 us)
Async XLA Ops:
  1.6 18.4 %collective-permute-start.1 = (bf16[4,32,1152]{2,1,0:T(8,128)(2,1)S(1)}, bf16[4,32,1152]{2,1,0:T(8,128)(2,1)}, u32[]{:S(2)}, u32[]{:S(2)}) collective-permute-start(bf16[4,32,1152]{2,1,0:T(8,128)(2,1)S(1)} %bitcast.7), channel_id=1, source_target_pairs={{0,2},{1,3},{2,0},{3,1},{4,6},{5,7},{6,4},{7,5},{8,10},{9,11},{10,... | collective-permute-start | bytes 884744 | tf_op jit(solution)/shard_map/ppermute | solution.py:36
  3.2 17.3 %collective-permute-start.3 = (bf16[4,32,1152]{2,1,0:T(8,128)(2,1)S(1)}, bf16[4,32,1152]{2,1,0:T(8,128)(2,1)}, u32[]{:S(2)}, u32[]{:S(2)}) collective-permute-start(bf16[4,32,1152]{2,1,0:T(8,128)(2,1)S(1)} %bitcast.8), channel_id=1, source_target_pairs={{0,128},{1,129},{2,130},{3,131},{4,132},{5,133},{6,134},{7,135},{8... | collective-permute-start | bytes 884744 | tf_op jit(solution)/shard_map/ppermute | solution.py:36
  5.9 15.8 %collective-permute-start.5 = (bf16[4,32,1152]{2,1,0:T(8,128)(2,1)S(1)}, bf16[4,32,1152]{2,1,0:T(8,128)(2,1)}, u32[]{:S(2)}, u32[]{:S(2)}) collective-permute-start(bf16[4,32,1152]{2,1,0:T(8,128)(2,1)S(1)} %bitcast.9), channel_id=1, source_target_pairs={{0,130},{1,131},{2,128},{3,129},{4,134},{5,135},{6,132},{7,133},{8... | collective-permute-start | bytes 884744 | tf_op jit(solution)/shard_map/ppermute | solution.py:36
  6.4 0.7 copy-start
  8.2 27.5 %all-to-all-start = ((bf16[32,8,1152]{2,1,0:T(8,128)(2,1)}), bf16[32,8,1152]{2,1,0:T(8,128)(2,1)S(1)}, u32[]{:S(2)}, u32[]{:S(2)}) async-start(bf16[32,8,1152]{2,1,0:T(8,128)(2,1)} %shard_map.69), calls=%async_computation | async-start | bytes 1179648 | tf_op jit(solution)/shard_map/all_to_all | solution.py:52
  19.9 7.0 %collective-permute-start = (bf16[4,32,1152]{2,1,0:T(8,128)(2,1)S(1)}, bf16[4,32,1152]{2,1,0:T(8,128)(2,1)S(1)}, u32[]{:S(2)}, u32[]{:S(2)}) collective-permute-start(bf16[4,32,1152]{2,1,0:T(8,128)(2,1)S(1)} %bitcast.10), channel_id=1, source_target_pairs={{0,1},{1,0},{2,3},{3,2},{4,5},{5,4},{6,7},{7,6},{8,9},{9,8},{10,11... | collective-permute-start | bytes 884744 | tf_op jit(solution)/shard_map/ppermute | solution.py:36
  20.0 6.9 %collective-permute-start.2 = (bf16[4,32,1152]{2,1,0:T(8,128)(2,1)}, bf16[4,32,1152]{2,1,0:T(8,128)(2,1)S(1)}, u32[]{:S(2)}, u32[]{:S(2)}) collective-permute-start(bf16[4,32,1152]{2,1,0:T(8,128)(2,1)} %collective-permute-done.1.refs_1_), channel_id=1, source_target_pairs={{0,1},{1,0},{2,3},{3,2},{4,5},{5,4},{6,7},{7,6},{8,9},{9,8},{10,11... | collective-permute-start | bytes 884744 | tf_op jit(solution)/shard_map/ppermute | solution.py:36
  20.5 6.4 %collective-permute-start.4 = (bf16[4,32,1152]{2,1,0:T(8,128)(2,1)}, bf16[4,32,1152]{2,1,0:T(8,128)(2,1)S(1)}, u32[]{:S(2)}, u32[]{:S(2)}) collective-permute-start(bf16[4,32,1152]{2,1,0:T(8,128)(2,1)} %collective-permute-done.3.refs_2_), channel_id=1, source_target_pairs={{0,1},{1,0},{2,3},{3,2},{4,5},{5,4},{6,7},{7,6},{8,9},{9,8},{10,11... | collective-permute-start | bytes 884744 | tf_op jit(solution)/shard_map/ppermute | solution.py:36
  21.8 5.2 %collective-permute-start.6 = (bf16[4,32,1152]{2,1,0:T(8,128)(2,1)}, bf16[4,32,1152]{2,1,0:T(8,128)(2,1)S(1)}, u32[]{:S(2)}, u32[]{:S(2)}) collective-permute-start(bf16[4,32,1152]{2,1,0:T(8,128)(2,1)} %collective-permute-done.5.refs_3_), channel_id=1, source_target_pairs={{0,1},{1,0},{2,3},{3,2},{4,5},{5,4},{6,7},{7,6},{8,9},{9,8},{10,11... | collective-permute-start | bytes 884744 | tf_op jit(solution)/shard_map/ppermute | solution.py:36
  21.8 5.2 %collective-permute-start.7 = (s32[1,32]{1,0:T(1,128)}, s32[1,32]{1,0:T(1,128)S(1)}, u32[]{:S(2)}, u32[]{:S(2)}) collective-permute-start(s32[1,32]{1,0:T(1,128)} %bitcast.12), channel_id=1, source_target_pairs={{0,128},{1,129},{2,130},{3,131},{4,132},{5,133},{6,134},{7,135},{8... | collective-permute-start | bytes 392 | tf_op jit(solution)/shard_map/ppermute | solution.py:36
  35.7 1.8 %collective-permute-start.8 = (f32[64,576]{1,0:T(8,128)}, f32[64,576]{1,0:T(8,128)S(1)}, u32[]{:S(2)}, u32[]{:S(2)}) collective-permute-start(f32[64,576]{1,0:T(8,128)} %get-tuple-element.42.pooled_in), channel_id=1, source_target_pairs={{0,1},{1,0},{2,3},{3,2},{4,5},{5,4},{6,7},{7,6},{8,9},{9,8},{10,11... | collective-permute-start | bytes 442376 | tf_op jit(solution)/shard_map/ppermute | solution.py:36
  39.5 1.5 %collective-permute-start.9 = (f32[64,640]{1,0:T(8,128)S(1)}, f32[64,640]{1,0:T(8,128)S(1)}, u32[]{:S(2)}, u32[]{:S(2)}) collective-permute-start(f32[64,640]{1,0:T(8,128)S(1)} %get-tuple-element.46), channel_id=1, source_target_pairs={{0,1},{1,0},{2,3},{3,2},{4,5},{5,4},{6,7},{7,6},{8,9},{9,8},{10,11... | collective-permute-start | bytes 491528 | tf_op jit(solution)/shard_map/ppermute | solution.py:36
  41.3 9.1 %collective-permute-start.10 = (f32[64,384]{1,0:T(8,128)S(1)}, f32[64,384]{1,0:T(8,128)S(1)}, u32[]{:S(2)}, u32[]{:S(2)}) collective-permute-start(f32[64,384]{1,0:T(8,128)S(1)} %maximum_maximum_fusion.s0), channel_id=1, source_target_pairs={{0,128},{1,129},{2,130},{3,131},{4,132},{5,133},{6,134},{7,135},{8... | collective-permute-start | bytes 294920 | tf_op jit(solution)/shard_map/ppermute | solution.py:36
  42.9 7.9 %collective-permute-start.11 = (f32[64,384]{1,0:T(8,128)S(1)}, f32[64,384]{1,0:T(8,128)S(1)}, u32[]{:S(2)}, u32[]{:S(2)}) collective-permute-start(f32[64,384]{1,0:T(8,128)S(1)} %concatenate.8), channel_id=1, source_target_pairs={{0,2},{1,3},{2,0},{3,1},{4,6},{5,7},{6,4},{7,5},{8,10},{9,11},{10,... | collective-permute-start | bytes 294920 | tf_op jit(solution)/shard_map/ppermute | solution.py:36
  44.7 6.1 %collective-permute-start.12 = (f32[64,384]{1,0:T(8,128)S(1)}, f32[64,384]{1,0:T(8,128)S(1)}, u32[]{:S(2)}, u32[]{:S(2)}) collective-permute-start(f32[64,384]{1,0:T(8,128)S(1)} %concatenate.8), channel_id=1, source_target_pairs={{0,130},{1,131},{2,128},{3,129},{4,134},{5,135},{6,132},{7,133},{8... | collective-permute-start | bytes 294920 | tf_op jit(solution)/shard_map/ppermute | solution.py:36
  45.8 13.3 %collective-permute-start.13 = (bf16[64,1280]{1,0:T(8,128)(2,1)S(1)}, bf16[64,1280]{1,0:T(8,128)(2,1)S(1)}, u32[]{:S(2)}, u32[]{:S(2)}) collective-permute-start(bf16[64,1280]{1,0:T(8,128)(2,1)S(1)} %get-tuple-element.61), channel_id=1, source_target_pairs={{0,32},{1,33},{2,34},{3,35},{4,36},{5,37},{6,38},{7,39},{8,40},{9,... | collective-permute-start | bytes 491528 | tf_op jit(solution)/shard_map/ppermute | solution.py:44
  47.5 11.6 %collective-permute-start.14 = (bf16[64,1280]{1,0:T(8,128)(2,1)S(1)}, bf16[64,1280]{1,0:T(8,128)(2,1)S(1)}, u32[]{:S(2)}, u32[]{:S(2)}) collective-permute-start(bf16[64,1280]{1,0:T(8,128)(2,1)S(1)} %get-tuple-element.62), channel_id=1, source_target_pairs={{0,64},{1,65},{2,66},{3,67},{4,68},{5,69},{6,70},{7,71},{8,72},{9,... | collective-permute-start | bytes 491528 | tf_op jit(solution)/shard_map/ppermute | solution.py:44
  50.3 8.8 %collective-permute-start.15 = (bf16[64,1280]{1,0:T(8,128)(2,1)S(1)}, bf16[64,1280]{1,0:T(8,128)(2,1)S(1)}, u32[]{:S(2)}, u32[]{:S(2)}) collective-permute-start(bf16[64,1280]{1,0:T(8,128)(2,1)S(1)} %get-tuple-element.63), channel_id=1, source_target_pairs={{0,96},{1,97},{2,98},{3,99},{4,100},{5,101},{6,102},{7,103},{8,104... | collective-permute-start | bytes 491528 | tf_op jit(solution)/shard_map/ppermute | solution.py:44
  55.4 41.1 %copy-start.1 = (bf16[8,1152]{1,0:T(8,128)(2,1)S(1)}, bf16[8,1152]{1,0:T(8,128)(2,1)}, u32[]{:S(2)}) copy-start(bf16[8,1152]{1,0:T(8,128)(2,1)} %captions.3) | copy-start | bytes 55300
  55.5 10.7 %collective-permute-start.17 = (bf16[144,896]{1,0:T(8,128)(2,1)S(1)}, bf16[144,896]{1,0:T(8,128)(2,1)S(1)}, u32[]{:S(2)}, u32[]{:S(2)}) collective-permute-start(bf16[144,896]{1,0:T(8,128)(2,1)S(1)} %get-tuple-element.66), channel_id=1, source_target_pairs={{0,64},{1,65},{2,66},{3,67},{4,68},{5,69},{6,70},{7,71},{8,72},{9,... | collective-permute-start | bytes 774152 | tf_op jit(solution)/shard_map/ppermute | solution.py:44
  57.4 11.7 %collective-permute-start.18 = (bf16[144,896]{1,0:T(8,128)(2,1)S(1)}, bf16[144,896]{1,0:T(8,128)(2,1)S(1)}, u32[]{:S(2)}, u32[]{:S(2)}) collective-permute-start(bf16[144,896]{1,0:T(8,128)(2,1)S(1)} %get-tuple-element.67), channel_id=1, source_target_pairs={{0,96},{1,97},{2,98},{3,99},{4,100},{5,101},{6,102},{7,103},{8,104... | collective-permute-start | bytes 774152 | tf_op jit(solution)/shard_map/ppermute | solution.py:44
  59.1 10.1 %collective-permute-start.16 = (bf16[144,896]{1,0:T(8,128)(2,1)S(1)}, bf16[144,896]{1,0:T(8,128)(2,1)S(1)}, u32[]{:S(2)}, u32[]{:S(2)}) collective-permute-start(bf16[144,896]{1,0:T(8,128)(2,1)S(1)} %get-tuple-element.65), channel_id=1, source_target_pairs={{0,32},{1,33},{2,34},{3,35},{4,36},{5,37},{6,38},{7,39},{8,40},{9,... | collective-permute-start | bytes 774152 | tf_op jit(solution)/shard_map/ppermute | solution.py:44
